TPU v7x, 256 devices: a whole 4x4x8 slice. The times are simulated.
256 devices in a mesh: seq: 32 (over y, z), mp: 8 (over x, core).
Axes of the slice: x: 4, y: 4, z: 8, core: 2. Of those that a mesh axis runs over, the one named last changes fastest.
Arguments:
- queries: bfloat16 [16384, 4096], P('seq', 'mp'), may hold values from -30 to 30
- keys: bfloat16 [16384, 1024], P('seq', 'mp'), may hold values from -6 to 6
- values: bfloat16 [16384, 1024], P('seq', 'mp'), may hold values from -6 to 6
- routing: int32 [32, 32, 3], P(None, 'mp'), may hold values from 0 to 31, as said below
- w_out: bfloat16 [4096, 4096], P('mp', 'seq'), may hold values from -0.09375 to 0.09375
Outputs:
- mixed: bfloat16 [16384, 4096], P('seq', 'mp')
Inputs may be any that keep to these rules, and one draw needn't show every extreme that they name: `routing`: entries of one query block i and head are distinct where below i; they are min(i, 3) distinct blocks before i, and any other entry equals i.
All inputs are finite; a program needn't handle non-finite values.
Results may differ from a plain program's by a relative error of at most 0.02.
Values may be sent and summed in bfloat16 or wider, within the bound.
No kernel may reach another device: no remote copies, remote signals or barrier semaphores. Data moves between devices by JAX's collectives and lax.ppermute only.
A program may use at most 128 MiB of HBM per device.

v0:
```python
import functools
import math

import jax
import jax.numpy as jnp
from jax import lax
from jax.experimental import pallas as pl
from jax.experimental.pallas import tpu as pltpu
from jax.sharding import Mesh, PartitionSpec as P

HD = 128
BLK = 512
HEADS = 4
SLOTS = 3
NY, NZ, NX, NC = 4, 8, 4, 2
AXES = ("y", "z", "x", "c")
HALF = BLK // 2
SCALE = math.log2(math.e) / math.sqrt(HD)
def shift(v, axis, d, n):
    return lax.ppermute(v, axis, [(i, (i + d) % n) for i in range(n)])


zp = functools.partial(shift, axis="z", d=1, n=NZ)
zm = functools.partial(shift, axis="z", d=-1, n=NZ)
yp = functools.partial(shift, axis="y", d=1, n=NY)
ym = functools.partial(shift, axis="y", d=-1, n=NY)
xp = functools.partial(shift, axis="x", d=1, n=NX)
xm = functools.partial(shift, axis="x", d=-1, n=NX)
swap = functools.partial(shift, axis="c", d=1, n=NC)


def gate(vals, waits):
    return lax.optimization_barrier((vals, waits))


def join(*parts):
    return jnp.concatenate(parts)


def gather(zc, yc, w, early):
    n = zc.shape[0]
    y1p, y1m, z1p, z1m = yp(yc), ym(yc), zp(zc), zm(zc)
    (y1p, y1m, z1p, z1m), w = gate((y1p, y1m, z1p, z1m), w)
    w = lax.all_gather(w, "z", axis=0, tiled=False)
    y2p, y2m, z2p, z2m = yp(y1p[: n // 2]), ym(y1m[n // 2 :]), zp(z1p), zm(z1m)
    (y2p, y2m, z2p, z2m), early = gate((y2p, y2m, z2p, z2m), early)
    s0 = jnp.stack([yc, y1p, y1m, join(y2p, y2m)])
    g1 = jnp.stack([zc, z1m, z1p, z2m])
    a1p, a1m, g1p, g1m, z3p = zp(s0), zm(s0), yp(g1), ym(g1), zp(z2p)
    (a1p, a1m, g1p, g1m, z3p, z2m), _ = gate((a1p, a1m, g1p, g1m, z3p, z2m), ())
    a2p, a2m, z4p, z3m, g1x = zp(a1p), zm(a1m), zp(z3p), zm(z2m), yp(g1p)
    (a2p, a2m, z4p, z3m, g1x), w = gate((a2p, a2m, z4p, z3m, g1x), w)
    w = lax.all_gather(w, "y", axis=0, tiled=False)
    g2 = jnp.stack([z2p, z3m, z3p, z4p])
    a3p, a3m, g2p, g2m = zp(a2p), zm(a2m), yp(g2), ym(g2)
    (a3p, a3m, g2p, g2m), _ = gate((a3p, a3m, g2p, g2m), ())
    a4p, a4m, g2h, g2l = zp(a3p[:2]), zm(a3m[2:]), yp(g2p[:2]), ym(g2m[2:])
    za = [g1, g1p, g1m, g1x, g2, g2p, g2m, g2h, g2l]
    ya = [s0, a1m, a2m, a3m, a4p, a3p, a2p, a1p, a4m]
    return za, ya, w, early


def block_places(route, y, z):
    by, dz = route // NZ, (route - z) % NZ
    dy = (by - y) % NY
    first = (dz == 0) | (dz == 1) | (dz == 7) | (dz == 2)
    zslot = jnp.where((dz == 1) | (dz == 3), 1, jnp.where((dz == 7) | (dz == 5), 2, jnp.where((dz == 2) | (dz == 4), 3, 0)))
    yslot = jnp.where(dy == 0, 0, jnp.where(dy == 3, 1, jnp.where(dy == 1, 2, 3)))
    zarray = jnp.where(first, 0, 4) + yslot
    tail = (zarray == 7) & (zslot >= 2)
    late = (dz == 4) & (yslot >= 2)
    zarray, zslot = jnp.where(tail, 8, zarray), jnp.where(tail, zslot - 2, zslot)
    yarray, yslot = jnp.where(late, NZ, dz), jnp.where(late, yslot - 2, yslot)
    ok = (route < y * NZ + z).astype(jnp.int32)
    return jnp.stack([zarray, zslot, yarray, yslot, ok]).reshape(-1)


TILE = 128


def attend_kernel(place_ref, q_ref, k_ref, v_ref, *rest):
    za, ya, out_ref, kbuf, vbuf, sems = rest[:9], rest[9:18], rest[18], rest[19], rest[20], rest[21]
    n = HEADS * SLOTS

    def fetch(u, i, block):
        rows = pl.ds(i * HALF, HALF)
        pltpu.make_async_copy(block.at[pl.ds(0, HALF)], kbuf.at[u, rows], sems.at[u, i, 0]).start()
        pltpu.make_async_copy(block.at[pl.ds(HALF, HALF)], vbuf.at[u, rows, pl.ds(0, HD)], sems.at[u, i, 1]).start()

    def choose(u, i, arrays):
        array, slot = place_ref[2 * i * n + u], place_ref[(2 * i + 1) * n + u]
        for low, high in ((0, 4), (4, 9)):

            @pl.when((array >= low) & (array < high))
            def _():
                for a in range(low, high):

                    @pl.when(array == a)
                    def _():
                        fetch(u, i, arrays[a].at[slot])

    for u in range(n):
        choose(u, 0, za)
        choose(u, 1, ya)
    for u in range(n + 1):
        vbuf[u, :, HD:] = jnp.ones((BLK, HD), jnp.bfloat16)
    vbuf[n, :, :HD] = v_ref[...]
    scores_of = lambda q, k: lax.dot_general(q, k, (((1,), (1,)), ((), ())), preferred_element_type=jnp.float32)
    for h in range(HEADS):
        cols = slice(h * HD, (h + 1) * HD)
        for s in range(SLOTS):
            u = h * SLOTS + s
            for i in range(2):
                rows = pl.ds(i * HALF, HALF)
                some = za[0].at[0, pl.ds(0, HALF)]
                pltpu.make_async_copy(some, kbuf.at[u, rows], sems.at[u, i, 0]).wait()
                pltpu.make_async_copy(some, vbuf.at[u, rows, pl.ds(0, HD)], sems.at[u, i, 1]).wait()
        for t in range(BLK // TILE):
            rows = slice(t * TILE, (t + 1) * TILE)
            q = q_ref[rows, cols]
            seen = (t + 1) * TILE
            own = scores_of(q, k_ref[:seen])
            later = lax.broadcasted_iota(jnp.int32, (TILE, seen), 1) - t * TILE
            own = jnp.where(lax.broadcasted_iota(jnp.int32, (TILE, seen), 0) >= later, own, -1e30)
            m = jnp.max(own, axis=1, keepdims=True) * SCALE
            scores = []
            for s in range(SLOTS):
                u = h * SLOTS + s
                sc = scores_of(q, kbuf[u])
                top = jnp.max(sc, axis=1, keepdims=True) * SCALE
                m = jnp.maximum(m, jnp.where(place_ref[4 * n + u] == 1, top, -1e30))
                scores.append(sc)
            e = jnp.exp2(own * SCALE - m).astype(jnp.bfloat16)
            both = jnp.dot(e, vbuf[n, :seen], preferred_element_type=jnp.float32)
            for s in range(SLOTS):
                u = h * SLOTS + s
                e = jnp.exp2(scores[s] * SCALE - jnp.where(place_ref[4 * n + u] == 1, m, 1e30)).astype(jnp.bfloat16)
                both = both + jnp.dot(e, vbuf[u], preferred_element_type=jnp.float32)
            out_ref[rows, cols] = (both[:, :HD] / both[:, HD:]).astype(out_ref.dtype)


def near_kernel(at_ref, a0_ref, a1_ref, a2_ref, w_ref, out_ref, buf, sems):
    copies = [pltpu.make_async_copy(w_ref.at[at_ref[i]], buf.at[i], sems.at[i]) for i in range(3)]
    for copy in copies:
        copy.start()
    for copy in copies:
        copy.wait()
    for n in range(NZ // 2):
        total = None
        for i, a_ref in enumerate((a0_ref, a1_ref, a2_ref)):
            rows = jnp.concatenate([buf[i, 2 * n], buf[i, 2 * n + 1]], axis=1)
            part = jnp.dot(a_ref[...], rows, preferred_element_type=jnp.float32)
            total = part if total is None else total + part
        out_ref[:, n * 2 * HD : (n + 1) * 2 * HD] = total


def far_kernel(at_ref, total_ref, a0_ref, a1_ref, w_ref, out_ref, buf, sem):
    width, count = NZ * HD // NC, NZ // NC
    copy = pltpu.make_async_copy(w_ref.at[at_ref[0], pl.ds(at_ref[1] * count, count)], buf, sem)
    copy.start()
    copy.wait()
    for i, a_ref in enumerate((a0_ref, a1_ref)):
        rows = slice(i * HALF, (i + 1) * HALF)
        for n in range(count // 2):
            part = jnp.dot(
                a_ref[...], jnp.concatenate([buf[2 * n], buf[2 * n + 1]], axis=1), preferred_element_type=jnp.float32
            )
            cols = pl.ds(pl.multiple_of(at_ref[1] * width, width) + n * 2 * HD, 2 * HD)
            out_ref[rows, n * 2 * HD : (n + 1) * 2 * HD] = (total_ref[rows, cols] + part).astype(out_ref.dtype)


def call(kernel, out_shape, scalars, near, far, scratch, flops, exps=0, vmem=32):
    spec = lambda space, arrays: [pl.BlockSpec(memory_space=space)] * len(arrays)
    return pl.pallas_call(
        kernel,
        out_shape=out_shape,
        in_specs=spec(pltpu.SMEM, scalars) + spec(pltpu.VMEM, near) + spec(pl.ANY, far),
        out_specs=jax.tree.map(lambda _: pl.BlockSpec(memory_space=pltpu.VMEM), out_shape),
        scratch_shapes=scratch,
        compiler_params=pltpu.CompilerParams(vmem_limit_bytes=vmem << 20),
        cost_estimate=pl.CostEstimate(flops=flops, transcendentals=exps, bytes_accessed=8 << 20),
    )(*scalars, *near, *far)


def attention(places, q, k, v, za, ya):
    n = HEADS * SLOTS
    scratch = [
        pltpu.VMEM((n, BLK, HD), jnp.bfloat16),
        pltpu.VMEM((n + 1, BLK, 2 * HD), jnp.bfloat16),
        pltpu.SemaphoreType.DMA((n, 2, 2)),
    ]
    out = jax.ShapeDtypeStruct((BLK, HEADS * HD), jnp.bfloat16)
    flops, exps = 6 * (n + HEADS) * BLK * BLK * HD, (n + HEADS) * BLK * BLK
    return call(attend_kernel, out, (places,), (q, k, v), (*za, *ya), scratch, flops, exps, 56)


def project_near(at, a0, a1, a2, w):
    out = jax.ShapeDtypeStruct((BLK, NZ * HD), jnp.float32)
    scratch = [pltpu.VMEM((3, NZ, BLK, HD), jnp.bfloat16), pltpu.SemaphoreType.DMA((3,))]
    return call(near_kernel, out, (at,), (a0, a1, a2), (w,), scratch, 6 * BLK * BLK * NZ * HD)


def project_far(at, total, a0, a1, w, dtype):
    out = jax.ShapeDtypeStruct((BLK, NZ * HD // NC), dtype)
    scratch = [pltpu.VMEM((NZ // NC, BLK, HD), jnp.bfloat16), pltpu.SemaphoreType.DMA]
    return call(far_kernel, out, (at,), (total, a0, a1), (w,), scratch, 2 * BLK * BLK * NZ * HD // NC)


def body(queries, keys, values, routing, w_out):
    y, z, x, c = (lax.axis_index(a) for a in AXES)
    at = lambda y, z, x, c: ((y * NZ + z) * NX + x) * NC + c
    turn = [
        (at(y, z, x, c), at(x, z, y, c)) for y in range(NY) for z in range(NZ) for x in range(NX) for c in range(NC)
    ]
    w = lax.ppermute(w_out, AXES, turn)
    route = lax.dynamic_index_in_dim(routing, y * NZ + z, 0, keepdims=False)
    places = block_places(route.reshape(-1), y, z)
    zc, yc = join(keys[:HALF], values[:HALF]), join(keys[HALF:], values[HALF:])
    za, ya, w, places = gather(zc, yc, w, places)
    attn = attention(places, queries, keys, values, za, ya)
    x1p, x1m = xp(attn), xm(attn)
    x2p, x2m = xp(x1p[:HALF]), xm(x1m[HALF:])
    total = project_near(jnp.stack([x, (x - 1) % NX, (x + 1) % NX]), attn, x1p, x1m, w)
    far = (x + 2) % NX
    other = project_far(jnp.stack([far, 1 - c]), total, x2p, x2m, w, jnp.bfloat16)
    theirs = swap(other)
    mine = project_far(jnp.stack([far, c]), total, x2p, x2m, w, jnp.float32)
    return (mine + theirs.astype(jnp.float32)).astype(jnp.bfloat16)


def solution(mesh):
    grid = Mesh(mesh.devices.reshape(NY, NZ, NX, NC), AXES)
    seq, mp = ("y", "z"), ("x", "c")
    in_specs = (P(seq, mp), P(seq, mp), P(seq, mp), P(None, mp, None), P(mp, seq))
    return jax.shard_map(body, mesh=grid, in_specs=in_specs, out_specs=P(seq, mp), check_vma=False)
```

profile of v0, /device:TPU:1, one launch (start us, length us, event | category | flops | bytes accessed | tf_op | source)
XLA Modules:
  0.0 158.5 jit_solution(16868948519620104123)
XLA Ops:
  7.5 2.5 %collective-permute-start.2 = (bf16[512,128]{1,0:T(8,128)(2,1)S(1)}, bf16[512,128]{1,0:T(8,128)(2,1)S(1)}, u32[]{:S(2)}, u32[]{:S(2)}) collective-permute-start(bf16[512,128]{1,0:T(8,128)(2,1)S(1)} %get-tuple-element.66), channel_id=1, source_target_pairs={{0,8},{8,16},{16,24},{24,32},{32,40},{40,48},{48,56},{56,0},{1,9},... | collective-permute-start | bytes 393224 | tf_op jit(solution)/shard_map/ppermute | solution.py:20
  10.1 4.0 %collective-permute-start.3 = (bf16[512,128]{1,0:T(8,128)(2,1)S(1)}, bf16[512,128]{1,0:T(8,128)(2,1)S(1)}, u32[]{:S(2)}, u32[]{:S(2)}) collective-permute-start(bf16[512,128]{1,0:T(8,128)(2,1)S(1)} %get-tuple-element.66), channel_id=1, source_target_pairs={{0,56},{8,0},{16,8},{24,16},{32,24},{40,32},{48,40},{56,48},{1,57}... | collective-permute-start | bytes 393224 | tf_op jit(solution)/shard_map/ppermute | solution.py:20
  14.1 1.4 collective-permute-start
  15.5 1.5 collective-permute-start.1
  17.0 1.6 collective-permute-start.4
  20.4 4.3 %collective-permute-start.5 = (bf16[256,128]{1,0:T(8,128)(2,1)S(1)}, bf16[256,128]{1,0:T(8,128)(2,1)S(1)}, u32[]{:S(2)}, u32[]{:S(2)}) collective-permute-start(bf16[256,128]{1,0:T(8,128)(2,1)S(1)} %slice.40), channel_id=1, source_target_pairs={{0,64},{64,128},{128,192},{192,0},{1,65},{65,129},{129,193},{193,1... | collective-permute-start | bytes 196616 | tf_op jit(solution)/shard_map/ppermute | solution.py:20
  24.7 7.7 %collective-permute-start.6 = (bf16[256,128]{1,0:T(8,128)(2,1)S(1)}, bf16[256,128]{1,0:T(8,128)(2,1)S(1)}, u32[]{:S(2)}, u32[]{:S(2)}) collective-permute-start(bf16[256,128]{1,0:T(8,128)(2,1)S(1)} %slice.41), channel_id=1, source_target_pairs={{0,192},{64,0},{128,64},{192,128},{1,193},{65,1},{129,65},{193,129... | collective-permute-start | bytes 196616 | tf_op jit(solution)/shard_map/ppermute | solution.py:20
  32.4 2.7 %collective-permute-start.8 = (bf16[512,128]{1,0:T(8,128)(2,1)S(1)}, bf16[512,128]{1,0:T(8,128)(2,1)S(1)}, u32[]{:S(2)}, u32[]{:S(2)}) collective-permute-start(bf16[512,128]{1,0:T(8,128)(2,1)S(1)} %collective-permute-done.3), channel_id=1, source_target_pairs={{0,56},{8,0},{16,8},{24,16},{32,24},{40,32},{48,40},{56,48},{1,57}... | collective-permute-start | bytes 393224 | tf_op jit(solution)/shard_map/ppermute | solution.py:20
  35.8 1.6 %collective-permute-done.7 = bf16[512,128]{1,0:T(8,128)(2,1)S(1)} collective-permute-done((bf16[512,128]{1,0:T(8,128)(2,1)S(1)}, bf16[512,128]{1,0:T(8,128)(2,1)S(1)}, u32[]{:S(2)}, u32[]{:S(2)}) %collective-permute-start.7) | collective-permute-done | bytes 131104 | tf_op jit(solution)/shard_map/ppermute | solution.py:20
  37.6 2.7 %collective-permute-start.10 = (bf16[4,512,128]{2,1,0:T(8,128)(2,1)S(1)}, bf16[4,512,128]{2,1,0:T(8,128)(2,1)S(1)}, u32[]{:S(2)}, u32[]{:S(2)}) collective-permute-start(bf16[4,512,128]{2,1,0:T(8,128)(2,1)S(1)} %pad_maximum_fusion.1.rest_9_), channel_id=1, source_target_pairs={{0,56},{8,0},{16,8},{24,16},{32,24},{40,32},{48,40},{56,48},{1,57}... | collective-permute-start | bytes 1572872 | tf_op jit(solution)/shard_map/ppermute | solution.py:20
  40.5 2.7 %collective-permute-start.12 = (bf16[4,512,128]{2,1,0:T(8,128)(2,1)S(1)}, bf16[4,512,128]{2,1,0:T(8,128)(2,1)S(1)}, u32[]{:S(2)}, u32[]{:S(2)}) collective-permute-start(bf16[4,512,128]{2,1,0:T(8,128)(2,1)S(1)} %pad_maximum_fusion.rest_0_), channel_id=1, source_target_pairs={{0,192},{64,0},{128,64},{192,128},{1,193},{65,1},{129,65},{193,129... | collective-permute-start | bytes 1572872 | tf_op jit(solution)/shard_map/ppermute | solution.py:20
  43.2 20.3 %collective-permute-done.13 = bf16[512,128]{1,0:T(8,128)(2,1)S(1)} collective-permute-done((bf16[512,128]{1,0:T(8,128)(2,1)S(1)}, bf16[512,128]{1,0:T(8,128)(2,1)S(1)}, u32[]{:S(2)}, u32[]{:S(2)}) %collective-permute-start.13) | collective-permute-done | bytes 131104 | tf_op jit(solution)/shard_map/ppermute | solution.py:20
  63.7 2.7 %collective-permute-start.15 = (bf16[4,512,128]{2,1,0:T(8,128)(2,1)S(1)}, bf16[4,512,128]{2,1,0:T(8,128)(2,1)S(1)}, u32[]{:S(2)}, u32[]{:S(2)}) collective-permute-start(bf16[4,512,128]{2,1,0:T(8,128)(2,1)S(1)} %collective-permute-done.10.rest_10_), channel_id=1, source_target_pairs={{0,56},{8,0},{16,8},{24,16},{32,24},{40,32},{48,40},{56,48},{1,57}... | collective-permute-start | bytes 1572872 | tf_op jit(solution)/shard_map/ppermute | solution.py:20
  66.3 2.7 %collective-permute-start.17 = (bf16[512,128]{1,0:T(8,128)(2,1)S(1)}, bf16[512,128]{1,0:T(8,128)(2,1)S(1)}, u32[]{:S(2)}, u32[]{:S(2)}) collective-permute-start(bf16[512,128]{1,0:T(8,128)(2,1)S(1)} %collective-permute-done.8), channel_id=1, source_target_pairs={{0,56},{8,0},{16,8},{24,16},{32,24},{40,32},{48,40},{56,48},{1,57}... | collective-permute-start | bytes 393224 | tf_op jit(solution)/shard_map/ppermute | solution.py:20
  69.0 8.6 %collective-permute-done.16 = bf16[512,128]{1,0:T(8,128)(2,1)S(1)} collective-permute-done((bf16[512,128]{1,0:T(8,128)(2,1)S(1)}, bf16[512,128]{1,0:T(8,128)(2,1)S(1)}, u32[]{:S(2)}, u32[]{:S(2)}) %collective-permute-start.16) | collective-permute-done | bytes 131104 | tf_op jit(solution)/shard_map/ppermute | solution.py:20
  79.5 2.7 %collective-permute-start.22 = (bf16[4,512,128]{2,1,0:T(8,128)(2,1)S(1)}, bf16[4,512,128]{2,1,0:T(8,128)(2,1)S(1)}, u32[]{:S(2)}, u32[]{:S(2)}) collective-permute-start(bf16[4,512,128]{2,1,0:T(8,128)(2,1)S(1)} %pad_maximum_fusion.2.rest_4_), channel_id=1, source_target_pairs={{0,192},{64,0},{128,64},{192,128},{1,193},{65,1},{129,65},{193,129... | collective-permute-start | bytes 1572872 | tf_op jit(solution)/shard_map/ppermute | solution.py:20
  82.1 2.7 %collective-permute-start.20 = (bf16[4,512,128]{2,1,0:T(8,128)(2,1)}, bf16[4,512,128]{2,1,0:T(8,128)(2,1)S(1)}, u32[]{:S(2)}, u32[]{:S(2)}) collective-permute-start(bf16[4,512,128]{2,1,0:T(8,128)(2,1)} %copy-done.17), channel_id=1, source_target_pairs={{0,56},{8,0},{16,8},{24,16},{32,24},{40,32},{48,40},{56,48},{1,57}... | collective-permute-start | bytes 1572872 | tf_op jit(solution)/shard_map/ppermute | solution.py:20
  84.8 4.7 %collective-permute-done.21.rest_5_ = bf16[4,512,128]{2,1,0:T(8,128)(2,1)S(1)} collective-permute-done((bf16[4,512,128]{2,1,0:T(8,128)(2,1)S(1)}, bf16[4,512,128]{2,1,0:T(8,128)(2,1)S(1)}, u32[]{:S(2)}, u32[]{:S(2)}) %collective-permute-start.21) | collective-permute-done | bytes 524320 | tf_op jit(solution)/shard_map/ppermute | solution.py:20
  89.6 2.3 %collective-permute-done.19.rest_14_ = bf16[4,512,128]{2,1,0:T(8,128)(2,1)S(1)} collective-permute-done((bf16[4,512,128]{2,1,0:T(8,128)(2,1)}, bf16[4,512,128]{2,1,0:T(8,128)(2,1)S(1)}, u32[]{:S(2)}, u32[]{:S(2)}) %collective-permute-start.19) | collective-permute-done | bytes 524320 | tf_op jit(solution)/shard_map/ppermute | solution.py:20
  92.0 2.7 %collective-permute-start.24 = (bf16[2,512,128]{2,1,0:T(8,128)(2,1)S(1)}, bf16[2,512,128]{2,1,0:T(8,128)(2,1)S(1)}, u32[]{:S(2)}, u32[]{:S(2)}) collective-permute-start(bf16[2,512,128]{2,1,0:T(8,128)(2,1)S(1)} %slice.43), channel_id=1, source_target_pairs={{0,192},{64,0},{128,64},{192,128},{1,193},{65,1},{129,65},{193,129... | collective-permute-start | bytes 786440 | tf_op jit(solution)/shard_map/ppermute | solution.py:20
  94.9 3.0 %collective-permute-start.26 = (bf16[2,512,128]{2,1,0:T(8,128)(2,1)S(1)}, bf16[2,512,128]{2,1,0:T(8,128)(2,1)S(1)}, u32[]{:S(2)}, u32[]{:S(2)}) collective-permute-start(bf16[2,512,128]{2,1,0:T(8,128)(2,1)S(1)} %slice.45), channel_id=1, source_target_pairs={{0,56},{8,0},{16,8},{24,16},{32,24},{40,32},{48,40},{56,48},{1,57}... | collective-permute-start | bytes 786440 | tf_op jit(solution)/shard_map/ppermute | solution.py:20
  98.6 4.3 %collective-permute-done.24.rest_8_ = bf16[2,512,128]{2,1,0:T(8,128)(2,1)S(1)} collective-permute-done((bf16[2,512,128]{2,1,0:T(8,128)(2,1)S(1)}, bf16[2,512,128]{2,1,0:T(8,128)(2,1)S(1)}, u32[]{:S(2)}, u32[]{:S(2)}) %collective-permute-start.24) | collective-permute-done | bytes 262176 | tf_op jit(solution)/shard_map/ppermute | solution.py:20
  104.4 11.8 %shard_map.55.a0_ref = bf16[512,512]{1,0:T(8,128)(2,1)} custom-call(s32[60]{0:T(128)} %reshape.322.place_ref, bf16[512,512]{1,0:T(8,128)(2,1)} %q_ref.1, bf16[512,128]{1,0:T(8,128)(2,1)} %k_ref.1, bf16[512,128]{1,0:T(8,128)(2,1)} %v_ref.1, bf16[4,512,128]{2,1,0:T(8,128)(2,1)} %copy-done.5, bf16[4,512,128]{2,1,0:T(8,128)(2,1)} %copy-done.14, ...), custom_call_target="tpu_custom_call" | custom-call | flops 3221225472 | bytes 8388608 | tf_op jit(solution)/shard_map/pallas_call | solution.py:174
  116.3 4.8 %collective-permute-start.28 = (bf16[512,512]{1,0:T(8,128)(2,1)}, bf16[512,512]{1,0:T(8,128)(2,1)S(1)}, u32[]{:S(2)}, u32[]{:S(2)}) collective-permute-start(bf16[512,512]{1,0:T(8,128)(2,1)} %shard_map.55.a0_ref), channel_id=1, source_target_pairs={{0,6},{2,0},{4,2},{6,4},{1,7},{3,1},{5,3},{7,5},{8,14},{10,8},{12,... | collective-permute-start | bytes 1572872 | tf_op jit(solution)/shard_map/ppermute | solution.py:20
  121.2 7.0 %collective-permute-done.27.a1_ref = bf16[512,512]{1,0:T(8,128)(2,1)S(1)} collective-permute-done((bf16[512,512]{1,0:T(8,128)(2,1)}, bf16[512,512]{1,0:T(8,128)(2,1)S(1)}, u32[]{:S(2)}, u32[]{:S(2)}) %collective-permute-start.27) | collective-permute-done | bytes 524320 | tf_op jit(solution)/shard_map/ppermute | solution.py:20
  128.3 3.0 %collective-permute-start.30 = (bf16[256,512]{1,0:T(8,128)(2,1)S(1)}, bf16[256,512]{1,0:T(8,128)(2,1)S(1)}, u32[]{:S(2)}, u32[]{:S(2)}) collective-permute-start(bf16[256,512]{1,0:T(8,128)(2,1)S(1)} %slice.49), channel_id=1, source_target_pairs={{0,6},{2,0},{4,2},{6,4},{1,7},{3,1},{5,3},{7,5},{8,14},{10,8},{12,... | collective-permute-start | bytes 786440 | tf_op jit(solution)/shard_map/ppermute | solution.py:20
  131.4 4.2 %all-gather.7.cloned.1.call-done = bf16[32,512,128]{2,1,0:T(8,128)(2,1)} async-done(((bf16[8,512,128]{2,1,0:T(8,128)(2,1)}), bf16[32,512,128]{2,1,0:T(8,128)(2,1)}) %all-gather.7.cloned.1.call-update) | async-done | bytes 4194320 | tf_op jit(solution)/shard_map/all_gather | solution.py:53
  135.6 2.2 %copy-done.1 = bf16[32,512,128]{2,1,0:T(8,128)(2,1)S(1)} copy-done((bf16[32,512,128]{2,1,0:T(8,128)(2,1)S(1)}, bf16[32,512,128]{2,1,0:T(8,128)(2,1)}, u32[]{:S(2)}) %copy-start.1) | copy-done | bytes 4194328
  138.8 2.6 %shard_map.56.total_ref = f32[512,1024]{1,0:T(8,128)S(1)} custom-call(s32[3]{0:T(128)S(1)} %pad_add_fusion.1.at_ref, bf16[512,512]{1,0:T(8,128)(2,1)S(1)} %copy-done.3, bf16[512,512]{1,0:T(8,128)(2,1)S(1)} %collective-permute-done.27.a1_ref, bf16[512,512]{1,0:T(8,128)(2,1)S(1)} %collective-permute-done.28.a2_ref, bf16[4,8,512,128]{3,2,1,0:T(8,128)(2,1)S(1)} %bitcast.23), custom_call_target="tpu_custom_call" | custom-call | flops 1610612736 | bytes 8388608 | tf_op jit(solution)/shard_map/pallas_call | solution.py:174
  141.4 1.0 shard_map.58
  142.5 6.7 %collective-permute-start.31 = (bf16[512,512]{1,0:T(8,128)(2,1)S(1)}, bf16[512,512]{1,0:T(8,128)(2,1)S(1)}, u32[]{:S(2)}, u32[]{:S(2)}) collective-permute-start(bf16[512,512]{1,0:T(8,128)(2,1)S(1)} %shard_map.58), channel_id=1, source_target_pairs={{0,1},{1,0},{2,3},{3,2},{4,5},{5,4},{6,7},{7,6},{8,9},{9,8},{10,11... | collective-permute-start | bytes 1572872 | tf_op jit(solution)/shard_map/ppermute | solution.py:20
  149.3 1.0 shard_map.57
  (114 shorter events, 10.8 us)
Async XLA Ops:
  6.5 72.7 %all-gather.5.cloned.1.call-start = ((), (), s32[]{:S(2)}) async-start(), calls=%async_computation | async-start | bytes 1179648 | tf_op jit(solution)/shard_map/all_gather | solution.py:44
  7.5 11.4 %collective-permute-start.2 = (bf16[512,128]{1,0:T(8,128)(2,1)S(1)}, bf16[512,128]{1,0:T(8,128)(2,1)S(1)}, u32[]{:S(2)}, u32[]{:S(2)}) collective-permute-start(bf16[512,128]{1,0:T(8,128)(2,1)S(1)} %get-tuple-element.66), channel_id=1, source_target_pairs={{0,8},{8,16},{16,24},{24,32},{32,40},{40,48},{48,56},{56,0},{1,9},... | collective-permute-start | bytes 393224 | tf_op jit(solution)/shard_map/ppermute | solution.py:20
  10.1 8.8 %collective-permute-start.3 = (bf16[512,128]{1,0:T(8,128)(2,1)S(1)}, bf16[512,128]{1,0:T(8,128)(2,1)S(1)}, u32[]{:S(2)}, u32[]{:S(2)}) collective-permute-start(bf16[512,128]{1,0:T(8,128)(2,1)S(1)} %get-tuple-element.66), channel_id=1, source_target_pairs={{0,56},{8,0},{16,8},{24,16},{32,24},{40,32},{48,40},{56,48},{1,57}... | collective-permute-start | bytes 393224 | tf_op jit(solution)/shard_map/ppermute | solution.py:20
  14.1 5.2 %collective-permute-start = (bf16[512,128]{1,0:T(8,128)(2,1)S(1)}, bf16[512,128]{1,0:T(8,128)(2,1)S(1)}, u32[]{:S(2)}, u32[]{:S(2)}) collective-permute-start(bf16[512,128]{1,0:T(8,128)(2,1)S(1)} %get-tuple-element.64), channel_id=1, source_target_pairs={{0,64},{64,128},{128,192},{192,0},{1,65},{65,129},{129,193},{193,1... | collective-permute-start | bytes 393224 | tf_op jit(solution)/shard_map/ppermute | solution.py:20
  20.3 115.3 %all-gather.7.cloned.1.call-start = ((), (), s32[]{:S(2)}) async-start(), calls=%async_computation.1 | async-start | bytes 5242880 | tf_op jit(solution)/shard_map/all_gather | solution.py:53
  20.4 15.5 %collective-permute-start.5 = (bf16[256,128]{1,0:T(8,128)(2,1)S(1)}, bf16[256,128]{1,0:T(8,128)(2,1)S(1)}, u32[]{:S(2)}, u32[]{:S(2)}) collective-permute-start(bf16[256,128]{1,0:T(8,128)(2,1)S(1)} %slice.40), channel_id=1, source_target_pairs={{0,64},{64,128},{128,192},{192,0},{1,65},{65,129},{129,193},{193,1... | collective-permute-start | bytes 196616 | tf_op jit(solution)/shard_map/ppermute | solution.py:20
  24.7 11.1 %collective-permute-start.6 = (bf16[256,128]{1,0:T(8,128)(2,1)S(1)}, bf16[256,128]{1,0:T(8,128)(2,1)S(1)}, u32[]{:S(2)}, u32[]{:S(2)}) collective-permute-start(bf16[256,128]{1,0:T(8,128)(2,1)S(1)} %slice.41), channel_id=1, source_target_pairs={{0,192},{64,0},{128,64},{192,128},{1,193},{65,1},{129,65},{193,129... | collective-permute-start | bytes 196616 | tf_op jit(solution)/shard_map/ppermute | solution.py:20
  32.4 5.0 %collective-permute-start.7 = (bf16[512,128]{1,0:T(8,128)(2,1)S(1)}, bf16[512,128]{1,0:T(8,128)(2,1)S(1)}, u32[]{:S(2)}, u32[]{:S(2)}) collective-permute-start(bf16[512,128]{1,0:T(8,128)(2,1)S(1)} %collective-permute-done.2), channel_id=1, source_target_pairs={{0,8},{8,16},{16,24},{24,32},{32,40},{40,48},{48,56},{56,0},{1,9},... | collective-permute-start | bytes 393224 | tf_op jit(solution)/shard_map/ppermute | solution.py:20
  32.4 5.0 %collective-permute-start.8 = (bf16[512,128]{1,0:T(8,128)(2,1)S(1)}, bf16[512,128]{1,0:T(8,128)(2,1)S(1)}, u32[]{:S(2)}, u32[]{:S(2)}) collective-permute-start(bf16[512,128]{1,0:T(8,128)(2,1)S(1)} %collective-permute-done.3), channel_id=1, source_target_pairs={{0,56},{8,0},{16,8},{24,16},{32,24},{40,32},{48,40},{56,48},{1,57}... | collective-permute-start | bytes 393224 | tf_op jit(solution)/shard_map/ppermute | solution.py:20
  37.6 25.9 %collective-permute-start.10 = (bf16[4,512,128]{2,1,0:T(8,128)(2,1)S(1)}, bf16[4,512,128]{2,1,0:T(8,128)(2,1)S(1)}, u32[]{:S(2)}, u32[]{:S(2)}) collective-permute-start(bf16[4,512,128]{2,1,0:T(8,128)(2,1)S(1)} %pad_maximum_fusion.1.rest_9_), channel_id=1, source_target_pairs={{0,56},{8,0},{16,8},{24,16},{32,24},{40,32},{48,40},{56,48},{1,57}... | collective-permute-start | bytes 1572872 | tf_op jit(solution)/shard_map/ppermute | solution.py:20
  40.3 23.2 %collective-permute-start.9 = (bf16[4,512,128]{2,1,0:T(8,128)(2,1)S(1)}, bf16[4,512,128]{2,1,0:T(8,128)(2,1)S(1)}, u32[]{:S(2)}, u32[]{:S(2)}) collective-permute-start(bf16[4,512,128]{2,1,0:T(8,128)(2,1)S(1)} %pad_maximum_fusion.1.rest_9_), channel_id=1, source_target_pairs={{0,8},{8,16},{16,24},{24,32},{32,40},{40,48},{48,56},{56,0},{1,9},... | collective-permute-start | bytes 1572872 | tf_op jit(solution)/shard_map/ppermute | solution.py:20
  40.4 23.1 %collective-permute-start.11 = (bf16[4,512,128]{2,1,0:T(8,128)(2,1)S(1)}, bf16[4,512,128]{2,1,0:T(8,128)(2,1)S(1)}, u32[]{:S(2)}, u32[]{:S(2)}) collective-permute-start(bf16[4,512,128]{2,1,0:T(8,128)(2,1)S(1)} %pad_maximum_fusion.rest_0_), channel_id=1, source_target_pairs={{0,64},{64,128},{128,192},{192,0},{1,65},{65,129},{129,193},{193,1... | collective-permute-start | bytes 1572872 | tf_op jit(solution)/shard_map/ppermute | solution.py:20
  40.5 23.1 %collective-permute-start.12 = (bf16[4,512,128]{2,1,0:T(8,128)(2,1)S(1)}, bf16[4,512,128]{2,1,0:T(8,128)(2,1)S(1)}, u32[]{:S(2)}, u32[]{:S(2)}) collective-permute-start(bf16[4,512,128]{2,1,0:T(8,128)(2,1)S(1)} %pad_maximum_fusion.rest_0_), channel_id=1, source_target_pairs={{0,192},{64,0},{128,64},{192,128},{1,193},{65,1},{129,65},{193,129... | collective-permute-start | bytes 1572872 | tf_op jit(solution)/shard_map/ppermute | solution.py:20
  43.2 20.3 %collective-permute-start.13 = (bf16[512,128]{1,0:T(8,128)(2,1)S(1)}, bf16[512,128]{1,0:T(8,128)(2,1)S(1)}, u32[]{:S(2)}, u32[]{:S(2)}) collective-permute-start(bf16[512,128]{1,0:T(8,128)(2,1)S(1)} %collective-permute-done.7), channel_id=1, source_target_pairs={{0,8},{8,16},{16,24},{24,32},{32,40},{40,48},{48,56},{56,0},{1,9},... | collective-permute-start | bytes 393224 | tf_op jit(solution)/shard_map/ppermute | solution.py:20
  63.6 14.1 %collective-permute-start.14 = (bf16[4,512,128]{2,1,0:T(8,128)(2,1)S(1)}, bf16[4,512,128]{2,1,0:T(8,128)(2,1)S(1)}, u32[]{:S(2)}, u32[]{:S(2)}) collective-permute-start(bf16[4,512,128]{2,1,0:T(8,128)(2,1)S(1)} %collective-permute-done.9.rest_16_), channel_id=1, source_target_pairs={{0,8},{8,16},{16,24},{24,32},{32,40},{40,48},{48,56},{56,0},{1,9},... | collective-permute-start | bytes 1572872 | tf_op jit(solution)/shard_map/ppermute | solution.py:20
  63.7 14.0 %collective-permute-start.15 = (bf16[4,512,128]{2,1,0:T(8,128)(2,1)S(1)}, bf16[4,512,128]{2,1,0:T(8,128)(2,1)S(1)}, u32[]{:S(2)}, u32[]{:S(2)}) collective-permute-start(bf16[4,512,128]{2,1,0:T(8,128)(2,1)S(1)} %collective-permute-done.10.rest_10_), channel_id=1, source_target_pairs={{0,56},{8,0},{16,8},{24,16},{32,24},{40,32},{48,40},{56,48},{1,57}... | collective-permute-start | bytes 1572872 | tf_op jit(solution)/shard_map/ppermute | solution.py:20
  66.3 12.9 %collective-permute-start.18 = (bf16[4,512,128]{2,1,0:T(8,128)(2,1)S(1)}, bf16[4,512,128]{2,1,0:T(8,128)(2,1)}, u32[]{:S(2)}, u32[]{:S(2)}) collective-permute-start(bf16[4,512,128]{2,1,0:T(8,128)(2,1)S(1)} %collective-permute-done.11.rest_1_), channel_id=1, source_target_pairs={{0,64},{64,128},{128,192},{192,0},{1,65},{65,129},{129,193},{193,1... | collective-permute-start | bytes 1572872 | tf_op jit(solution)/shard_map/ppermute | solution.py:20
  66.3 11.3 %collective-permute-start.16 = (bf16[512,128]{1,0:T(8,128)(2,1)S(1)}, bf16[512,128]{1,0:T(8,128)(2,1)S(1)}, u32[]{:S(2)}, u32[]{:S(2)}) collective-permute-start(bf16[512,128]{1,0:T(8,128)(2,1)S(1)} %collective-permute-done.13), channel_id=1, source_target_pairs={{0,8},{8,16},{16,24},{24,32},{32,40},{40,48},{48,56},{56,0},{1,9},... | collective-permute-start | bytes 393224 | tf_op jit(solution)/shard_map/ppermute | solution.py:20
  66.3 11.3 %collective-permute-start.17 = (bf16[512,128]{1,0:T(8,128)(2,1)S(1)}, bf16[512,128]{1,0:T(8,128)(2,1)S(1)}, u32[]{:S(2)}, u32[]{:S(2)}) collective-permute-start(bf16[512,128]{1,0:T(8,128)(2,1)S(1)} %collective-permute-done.8), channel_id=1, source_target_pairs={{0,56},{8,0},{16,8},{24,16},{32,24},{40,32},{48,40},{56,48},{1,57}... | collective-permute-start | bytes 393224 | tf_op jit(solution)/shard_map/ppermute | solution.py:20
  79.4 10.2 %collective-permute-start.21 = (bf16[4,512,128]{2,1,0:T(8,128)(2,1)S(1)}, bf16[4,512,128]{2,1,0:T(8,128)(2,1)S(1)}, u32[]{:S(2)}, u32[]{:S(2)}) collective-permute-start(bf16[4,512,128]{2,1,0:T(8,128)(2,1)S(1)} %pad_maximum_fusion.2.rest_4_), channel_id=1, source_target_pairs={{0,64},{64,128},{128,192},{192,0},{1,65},{65,129},{129,193},{193,1... | collective-permute-start | bytes 1572872 | tf_op jit(solution)/shard_map/ppermute | solution.py:20
  79.5 10.1 %collective-permute-start.22 = (bf16[4,512,128]{2,1,0:T(8,128)(2,1)S(1)}, bf16[4,512,128]{2,1,0:T(8,128)(2,1)S(1)}, u32[]{:S(2)}, u32[]{:S(2)}) collective-permute-start(bf16[4,512,128]{2,1,0:T(8,128)(2,1)S(1)} %pad_maximum_fusion.2.rest_4_), channel_id=1, source_target_pairs={{0,192},{64,0},{128,64},{192,128},{1,193},{65,1},{129,65},{193,129... | collective-permute-start | bytes 1572872 | tf_op jit(solution)/shard_map/ppermute | solution.py:20
  82.1 9.7 %collective-permute-start.19 = (bf16[4,512,128]{2,1,0:T(8,128)(2,1)}, bf16[4,512,128]{2,1,0:T(8,128)(2,1)S(1)}, u32[]{:S(2)}, u32[]{:S(2)}) collective-permute-start(bf16[4,512,128]{2,1,0:T(8,128)(2,1)} %copy-done.16), channel_id=1, source_target_pairs={{0,8},{8,16},{16,24},{24,32},{32,40},{40,48},{48,56},{56,0},{1,9},... | collective-permute-start | bytes 1572872 | tf_op jit(solution)/shard_map/ppermute | solution.py:20
  82.1 9.7 %collective-permute-start.20 = (bf16[4,512,128]{2,1,0:T(8,128)(2,1)}, bf16[4,512,128]{2,1,0:T(8,128)(2,1)S(1)}, u32[]{:S(2)}, u32[]{:S(2)}) collective-permute-start(bf16[4,512,128]{2,1,0:T(8,128)(2,1)} %copy-done.17), channel_id=1, source_target_pairs={{0,56},{8,0},{16,8},{24,16},{32,24},{40,32},{48,40},{56,48},{1,57}... | collective-permute-start | bytes 1572872 | tf_op jit(solution)/shard_map/ppermute | solution.py:20
  91.9 6.7 %collective-permute-start.23 = (bf16[2,512,128]{2,1,0:T(8,128)(2,1)S(1)}, bf16[2,512,128]{2,1,0:T(8,128)(2,1)S(1)}, u32[]{:S(2)}, u32[]{:S(2)}) collective-permute-start(bf16[2,512,128]{2,1,0:T(8,128)(2,1)S(1)} %slice.42), channel_id=1, source_target_pairs={{0,64},{64,128},{128,192},{192,0},{1,65},{65,129},{129,193},{193,1... | collective-permute-start | bytes 786440 | tf_op jit(solution)/shard_map/ppermute | solution.py:20
  92.0 10.9 %collective-permute-start.24 = (bf16[2,512,128]{2,1,0:T(8,128)(2,1)S(1)}, bf16[2,512,128]{2,1,0:T(8,128)(2,1)S(1)}, u32[]{:S(2)}, u32[]{:S(2)}) collective-permute-start(bf16[2,512,128]{2,1,0:T(8,128)(2,1)S(1)} %slice.43), channel_id=1, source_target_pairs={{0,192},{64,0},{128,64},{192,128},{1,193},{65,1},{129,65},{193,129... | collective-permute-start | bytes 786440 | tf_op jit(solution)/shard_map/ppermute | solution.py:20
  94.8 8.1 %collective-permute-start.25 = (bf16[2,512,128]{2,1,0:T(8,128)(2,1)S(1)}, bf16[2,512,128]{2,1,0:T(8,128)(2,1)S(1)}, u32[]{:S(2)}, u32[]{:S(2)}) collective-permute-start(bf16[2,512,128]{2,1,0:T(8,128)(2,1)S(1)} %slice.44), channel_id=1, source_target_pairs={{0,8},{8,16},{16,24},{24,32},{32,40},{40,48},{48,56},{56,0},{1,9},... | collective-permute-start | bytes 786440 | tf_op jit(solution)/shard_map/ppermute | solution.py:20
  94.9 8.0 %collective-permute-start.26 = (bf16[2,512,128]{2,1,0:T(8,128)(2,1)S(1)}, bf16[2,512,128]{2,1,0:T(8,128)(2,1)S(1)}, u32[]{:S(2)}, u32[]{:S(2)}) collective-permute-start(bf16[2,512,128]{2,1,0:T(8,128)(2,1)S(1)} %slice.45), channel_id=1, source_target_pairs={{0,56},{8,0},{16,8},{24,16},{32,24},{40,32},{48,40},{56,48},{1,57}... | collective-permute-start | bytes 786440 | tf_op jit(solution)/shard_map/ppermute | solution.py:20
  116.2 11.9 %collective-permute-start.27 = (bf16[512,512]{1,0:T(8,128)(2,1)}, bf16[512,512]{1,0:T(8,128)(2,1)S(1)}, u32[]{:S(2)}, u32[]{:S(2)}) collective-permute-start(bf16[512,512]{1,0:T(8,128)(2,1)} %shard_map.55.a0_ref), channel_id=1, source_target_pairs={{0,2},{2,4},{4,6},{6,0},{1,3},{3,5},{5,7},{7,1},{8,10},{10,12},{12... | collective-permute-start | bytes 1572872 | tf_op jit(solution)/shard_map/ppermute | solution.py:20
  116.3 12.0 %collective-permute-start.28 = (bf16[512,512]{1,0:T(8,128)(2,1)}, bf16[512,512]{1,0:T(8,128)(2,1)S(1)}, u32[]{:S(2)}, u32[]{:S(2)}) collective-permute-start(bf16[512,512]{1,0:T(8,128)(2,1)} %shard_map.55.a0_ref), channel_id=1, source_target_pairs={{0,6},{2,0},{4,2},{6,4},{1,7},{3,1},{5,3},{7,5},{8,14},{10,8},{12,... | collective-permute-start | bytes 1572872 | tf_op jit(solution)/shard_map/ppermute | solution.py:20
  128.2 13.2 %collective-permute-start.29 = (bf16[256,512]{1,0:T(8,128)(2,1)S(1)}, bf16[256,512]{1,0:T(8,128)(2,1)S(1)}, u32[]{:S(2)}, u32[]{:S(2)}) collective-permute-start(bf16[256,512]{1,0:T(8,128)(2,1)S(1)} %slice.48), channel_id=1, source_target_pairs={{0,2},{2,4},{4,6},{6,0},{1,3},{3,5},{5,7},{7,1},{8,10},{10,12},{12... | collective-permute-start | bytes 786440 | tf_op jit(solution)/shard_map/ppermute | solution.py:20
  128.3 13.1 %collective-permute-start.30 = (bf16[256,512]{1,0:T(8,128)(2,1)S(1)}, bf16[256,512]{1,0:T(8,128)(2,1)S(1)}, u32[]{:S(2)}, u32[]{:S(2)}) collective-permute-start(bf16[256,512]{1,0:T(8,128)(2,1)S(1)} %slice.49), channel_id=1, source_target_pairs={{0,6},{2,0},{4,2},{6,4},{1,7},{3,1},{5,3},{7,5},{8,14},{10,8},{12,... | collective-permute-start | bytes 786440 | tf_op jit(solution)/shard_map/ppermute | solution.py:20
  142.5 8.3 %collective-permute-start.31 = (bf16[512,512]{1,0:T(8,128)(2,1)S(1)}, bf16[512,512]{1,0:T(8,128)(2,1)S(1)}, u32[]{:S(2)}, u32[]{:S(2)}) collective-permute-start(bf16[512,512]{1,0:T(8,128)(2,1)S(1)} %shard_map.58), channel_id=1, source_target_pairs={{0,1},{1,0},{2,3},{3,2},{4,5},{5,4},{6,7},{7,6},{8,9},{9,8},{10,11... | collective-permute-start | bytes 1572872 | tf_op jit(solution)/shard_map/ppermute | solution.py:20
  (24 other events, 366.5 us)
Sparse Core Ops, SparseCore 0:
  20.4 45.6 all-gather.4
  79.4 56.1 all-gather.6
where the time goes:
time: 159 us
  starting transfers between devices  62.7 us (39%)
  waiting for transfers between devices  55.1 us (35%)
  Pallas kernels  16.5 us (10%)
  between operations  13.9 us (9%)
  local copies, waits for them, and re-layouts  8.95 us (6%)
    ppermute x31, starting transfers between devices, shift(): return lax.ppermute(v, axis, [(i, (i + d) % n) for i in range(n)])  61.1 us
    ppermute x31, waiting for transfers between devices, shift(): return lax.ppermute(v, axis, [(i, (i + d) % n) for i in range(n)])  50.9 us
    pallas_call x4, Pallas kernels, call(): pl.pallas_call(kernel, out_shape=out_shape, in_specs=spec(pltpu.SMEM, sca...  16.5 us
    unnamed x44, local copies, waits for them, and re-layouts  6.9 us
    all_gather x1, waiting for transfers between devices, gather(): w = lax.all_gather(w, 'y', axis=0, tiled=False)  4.18 us
  transfers between devices with their start and end apart: 34, of which 12 were waited for; matrix products, arithmetic and copies ran while one was open for 1% of the time, Pallas kernels for 10%

commit v1 on v0

v1 whole, which is shorter than its diff:
```python
import functools
import math

import jax
import jax.numpy as jnp
from jax import lax
from jax.experimental import pallas as pl
from jax.experimental.pallas import tpu as pltpu
from jax.sharding import Mesh, PartitionSpec as P

HD = 128
BLK = 512
HEADS = 4
SLOTS = 3
NY, NZ, NX, NC = 4, 8, 4, 2
AXES = ("y", "z", "x", "c")
HALF = BLK // 2
SCALE = math.log2(math.e) / math.sqrt(HD)
def shift(v, axis, d, n):
    return lax.ppermute(v, axis, [(i, (i + d) % n) for i in range(n)])


zp = functools.partial(shift, axis="z", d=1, n=NZ)
zm = functools.partial(shift, axis="z", d=-1, n=NZ)
yp = functools.partial(shift, axis="y", d=1, n=NY)
ym = functools.partial(shift, axis="y", d=-1, n=NY)
y2 = functools.partial(shift, axis="y", d=2, n=NY)
xp = functools.partial(shift, axis="x", d=1, n=NX)
xm = functools.partial(shift, axis="x", d=-1, n=NX)
swap = functools.partial(shift, axis="c", d=1, n=NC)


def gate(vals, waits):
    return lax.optimization_barrier((vals, waits))


def join(*parts):
    return jnp.concatenate(parts)


def gather(zc, yc, w, turn, early):
    n = yc.shape[0] // 2
    y1p, y1m, z1p, z1m = yp(yc), ym(yc), zp(zc), zm(zc)
    w = lax.ppermute(w, AXES, turn)
    (y1p, y1m, z1p, z1m, w), _ = gate((y1p, y1m, z1p, z1m, w), ())
    both_p, both_m, w2, z2p, z2m = yp(join(y1p[:n], w)), ym(join(y1m[n:], w)), y2(w), zp(z1p), zm(z1m)
    (both_p, both_m, w2, z2p, z2m), early = gate((both_p, both_m, w2, z2p, z2m), early)
    y2p, y2m, w = both_p[:n], both_m[:n], jnp.stack([w, both_p[n:], both_m[n:], w2])
    s0 = jnp.concatenate([jnp.stack([yc, y1p, y1m, join(y2p, y2m)]), w], axis=1)
    g1 = jnp.stack([zc, z1m, z1p, z2m])
    s1p, s1m, g1p, g1m, z3p = zp(s0), zm(s0), yp(g1), ym(g1), zp(z2p)
    (s1p, s1m, g1p, g1m, z3p, z2m), _ = gate((s1p, s1m, g1p, g1m, z3p, z2m), ())
    s2p, s2m, z4p, z3m, g1x = zp(s1p), zm(s1m), zp(z3p), zm(z2m), yp(g1p)
    (s2p, s2m, z4p, z3m, g1x), _ = gate((s2p, s2m, z4p, z3m, g1x), ())
    g2 = jnp.stack([z2p, z3m, z3p, z4p])
    s3p, s3m, g2p, g2m = zp(s2p), zm(s2m), yp(g2), ym(g2)
    (s3p, s3m, g2p, g2m), _ = gate((s3p, s3m, g2p, g2m), ())
    s4p, s4m, g2h, g2l = zp(s3p[:2]), zm(s3m[2:]), yp(g2p[:2]), ym(g2m[2:])
    za = [g1, g1p, g1m, g1x, g2, g2p, g2m, g2h, g2l]
    ya = [s0, s1m, s2m, s3m, s4p, s3p, s2p, s1p, s4m]
    return za, ya, early


def block_places(route, y, z):
    by, dz = route // NZ, (route - z) % NZ
    dy = (by - y) % NY
    first = (dz == 0) | (dz == 1) | (dz == 7) | (dz == 2)
    zslot = jnp.where((dz == 1) | (dz == 3), 1, jnp.where((dz == 7) | (dz == 5), 2, jnp.where((dz == 2) | (dz == 4), 3, 0)))
    yslot = jnp.where(dy == 0, 0, jnp.where(dy == 3, 1, jnp.where(dy == 1, 2, 3)))
    zarray = jnp.where(first, 0, 4) + yslot
    tail = (zarray == 7) & (zslot >= 2)
    late = (dz == 4) & (yslot >= 2)
    zarray, zslot = jnp.where(tail, 8, zarray), jnp.where(tail, zslot - 2, zslot)
    yarray, yslot = jnp.where(late, NZ, dz), jnp.where(late, yslot - 2, yslot)
    ok = (route < y * NZ + z).astype(jnp.int32)
    return jnp.stack([zarray, zslot, yarray, yslot, ok]).reshape(-1)


TILE = 128


def attend_kernel(place_ref, q_ref, k_ref, v_ref, *rest):
    za, ya, out_ref, kbuf, vbuf, sems = rest[:9], rest[9:18], rest[18], rest[19], rest[20], rest[21]
    n = HEADS * SLOTS

    def copies(u, i, block):
        half = lambda first, at: pltpu.make_async_copy(
            block.at[pl.ds(first, HALF)], vbuf.at[u, pl.ds(at, HALF), pl.ds(0, HD)], sems.at[u, i, 1]
        )
        if i == 1:
            return [half(0, HALF)]
        return [pltpu.make_async_copy(block.at[pl.ds(0, BLK)], kbuf.at[u], sems.at[u, i, 0]), half(BLK, 0)]

    for u in range(n):
        for i, arrays in enumerate((za, ya)):
            array, slot = place_ref[2 * i * n + u], place_ref[(2 * i + 1) * n + u]
            for low, high in ((0, 4), (4, 9)):

                @pl.when((array >= low) & (array < high))
                def _():
                    for a in range(low, high):

                        @pl.when(array == a)
                        def _():
                            for copy in copies(u, i, arrays[a].at[slot]):
                                copy.start()

    for u in range(n + 1):
        vbuf[u, :, HD:] = jnp.ones((BLK, HD), jnp.bfloat16)
    vbuf[n, :, :HD] = v_ref[...]
    scores_of = lambda q, k: lax.dot_general(q, k, (((1,), (1,)), ((), ())), preferred_element_type=jnp.float32)
    for h in range(HEADS):
        cols = slice(h * HD, (h + 1) * HD)
        for s in range(SLOTS):
            u = h * SLOTS + s
            for i, arrays in enumerate((za, ya)):
                for copy in copies(u, i, arrays[0].at[0]):
                    copy.wait()
        for t in range(BLK // TILE):
            rows = slice(t * TILE, (t + 1) * TILE)
            q = q_ref[rows, cols]
            seen = (t + 1) * TILE
            own = scores_of(q, k_ref[:seen])
            later = lax.broadcasted_iota(jnp.int32, (TILE, seen), 1) - t * TILE
            own = jnp.where(lax.broadcasted_iota(jnp.int32, (TILE, seen), 0) >= later, own, -1e30)
            m = jnp.max(own, axis=1, keepdims=True) * SCALE
            scores = []
            for s in range(SLOTS):
                u = h * SLOTS + s
                sc = scores_of(q, kbuf[u])
                top = jnp.max(sc, axis=1, keepdims=True) * SCALE
                m = jnp.maximum(m, jnp.where(place_ref[4 * n + u] == 1, top, -1e30))
                scores.append(sc)
            e = jnp.exp2(own * SCALE - m).astype(jnp.bfloat16)
            both = jnp.dot(e, vbuf[n, :seen], preferred_element_type=jnp.float32)
            for s in range(SLOTS):
                u = h * SLOTS + s
                e = jnp.exp2(scores[s] * SCALE - jnp.where(place_ref[4 * n + u] == 1, m, 1e30)).astype(jnp.bfloat16)
                both = both + jnp.dot(e, vbuf[u], preferred_element_type=jnp.float32)
            out_ref[rows, cols] = (both[:, :HD] / both[:, HD:]).astype(out_ref.dtype)


def own_kernel(at_ref, a_ref, *rest):
    arrays, total_ref, near_ref, far_ref, buf, sems = rest[:9], rest[9], rest[10], rest[11], rest[12], rest[13]
    dests = (buf, near_ref.at[0], near_ref.at[1], far_ref)
    for i, dest in enumerate(dests):
        slot = at_ref[1 + i]
        for dz in range(NZ):
            col = (at_ref[0] + dz) & (NZ - 1)

            def copy(array, at):
                pltpu.make_async_copy(array.at[at, pl.ds(HALF, BLK)], dest.at[col], sems.at[i]).start()

            if dz == 4:
                pl.when(slot < 2)(lambda: copy(arrays[4], slot))
                pl.when(slot >= 2)(lambda: copy(arrays[8], slot - 2))
            else:
                copy(arrays[dz], slot)
    pltpu.make_async_copy(buf, buf, sems.at[0]).wait()
    for n in range(NZ // 2):
        cols = jnp.concatenate([buf[2 * n], buf[2 * n + 1]], axis=1)
        total_ref[:, n * 2 * HD : (n + 1) * 2 * HD] = jnp.dot(a_ref[...], cols, preferred_element_type=jnp.float32)
    for i, dest in enumerate(dests[1:]):
        pltpu.make_async_copy(dest, dest, sems.at[1 + i]).wait()


def near_kernel(total_ref, a0_ref, a1_ref, w_ref, out_ref):
    for n in range(NZ // 2):
        cols = slice(n * 2 * HD, (n + 1) * 2 * HD)
        total = total_ref[:, cols]
        for i, a_ref in enumerate((a0_ref, a1_ref)):
            rows = jnp.concatenate([w_ref[i, 2 * n], w_ref[i, 2 * n + 1]], axis=1)
            total = total + jnp.dot(a_ref[...], rows, preferred_element_type=jnp.float32)
        out_ref[:, cols] = total


def far_kernel(core_ref, total_ref, a0_ref, a1_ref, w_ref, out_ref):
    width, count = NZ * HD // NC, NZ // NC
    core = core_ref[0]
    for i, a_ref in enumerate((a0_ref, a1_ref)):
        rows = slice(i * HALF, (i + 1) * HALF)
        for n in range(count // 2):
            right = jnp.concatenate([w_ref[core * count + 2 * n], w_ref[core * count + 2 * n + 1]], axis=1)
            part = jnp.dot(a_ref[...], right, preferred_element_type=jnp.float32)
            cols = pl.ds(pl.multiple_of(core * width, width) + n * 2 * HD, 2 * HD)
            out_ref[rows, n * 2 * HD : (n + 1) * 2 * HD] = (total_ref[rows, cols] + part).astype(out_ref.dtype)


def call(kernel, out_shape, scalars, near, far, scratch, flops, exps=0, vmem=32):
    spec = lambda space, arrays: [pl.BlockSpec(memory_space=space)] * len(arrays)
    return pl.pallas_call(
        kernel,
        out_shape=out_shape,
        in_specs=spec(pltpu.SMEM, scalars) + spec(pltpu.VMEM, near) + spec(pl.ANY, far),
        out_specs=jax.tree.map(lambda _: pl.BlockSpec(memory_space=pltpu.VMEM), out_shape),
        scratch_shapes=scratch,
        compiler_params=pltpu.CompilerParams(vmem_limit_bytes=vmem << 20),
        cost_estimate=pl.CostEstimate(flops=flops, transcendentals=exps, bytes_accessed=8 << 20),
    )(*scalars, *near, *far)


def attention(places, q, k, v, za, ya):
    n = HEADS * SLOTS
    scratch = [
        pltpu.VMEM((n, BLK, HD), jnp.bfloat16),
        pltpu.VMEM((n + 1, BLK, 2 * HD), jnp.bfloat16),
        pltpu.SemaphoreType.DMA((n, 2, 2)),
    ]
    out = jax.ShapeDtypeStruct((BLK, HEADS * HD), jnp.bfloat16)
    flops, exps = 6 * (n + HEADS) * BLK * BLK * HD, (n + HEADS) * BLK * BLK
    return call(attend_kernel, out, (places,), (q, k, v), (*za, *ya), scratch, flops, exps, 56)


def project_own(at, a, w):
    total = jax.ShapeDtypeStruct((BLK, NZ * HD), jnp.float32)
    rows = lambda *n: jax.ShapeDtypeStruct((*n, NZ, BLK, HD), jnp.bfloat16)
    scratch = [pltpu.VMEM((NZ, BLK, HD), jnp.bfloat16), pltpu.SemaphoreType.DMA((4,))]
    return call(own_kernel, (total, rows(2), rows()), (at,), (a,), w, scratch, 2 * BLK * BLK * NZ * HD, vmem=56)


def project_near(total, a0, a1, w):
    out = jax.ShapeDtypeStruct((BLK, NZ * HD), jnp.float32)
    return call(near_kernel, out, (), (total, a0, a1, w), (), (), 4 * BLK * BLK * NZ * HD)


def project_far(core, total, a0, a1, w, dtype):
    out = jax.ShapeDtypeStruct((BLK, NZ * HD // NC), dtype)
    return call(far_kernel, out, (core[None],), (total, a0, a1, w), (), (), 2 * BLK * BLK * NZ * HD // NC)


def body(queries, keys, values, routing, w_out):
    y, z, x, c = (lax.axis_index(a) for a in AXES)
    at = lambda y, z, x, c: ((y * NZ + z) * NX + x) * NC + c
    turn = [
        (at(y, z, x, c), at(x, z, y, c)) for y in range(NY) for z in range(NZ) for x in range(NX) for c in range(NC)
    ]
    route = lax.dynamic_index_in_dim(routing, y * NZ + z, 0, keepdims=False)
    places = block_places(route.reshape(-1), y, z)
    zc, yc = join(keys, values[:HALF]), values[HALF:]
    rows_of = lambda x: jnp.asarray([0, 2, 3, 1], jnp.int32)[(x - y) % NX]
    at = jnp.stack([z] + [rows_of(x + d) for d in (0, -1, 1, 2)])
    za, ya, (places, at) = gather(zc, yc, w_out, turn, (places, at))
    attn = attention(places, queries, keys, values, za, ya)
    x1p, x1m = xp(attn), xm(attn)
    (x1p, x1m), (total, near, far) = gate((x1p, x1m), project_own(at, attn, ya))
    x2p, x2m = xp(x1p[:HALF]), xm(x1m[HALF:])
    total = project_near(total, x1p, x1m, near)
    theirs = swap(project_far(1 - c, total, x2p, x2m, far, jnp.bfloat16))
    mine = project_far(c, total, x2p, x2m, far, jnp.float32)
    return (mine + theirs.astype(jnp.float32)).astype(jnp.bfloat16)


def solution(mesh):
    grid = Mesh(mesh.devices.reshape(NY, NZ, NX, NC), AXES)
    seq, mp = ("y", "z"), ("x", "c")
    in_specs = (P(seq, mp), P(seq, mp), P(seq, mp), P(None, mp, None), P(mp, seq))
    return jax.shard_map(body, mesh=grid, in_specs=in_specs, out_specs=P(seq, mp), check_vma=False)
```

time: 159 us -> 153 us (0.962)
  between operations: 13.9 us -> 0.61 us
  starting transfers between devices: 62.7 us -> 68.2 us
  Pallas kernels: 16.5 us -> 19.5 us
  waiting for transfers between devices: 55.1 us -> 52.1 us
    ppermute x31 -> x32, starting transfers between devices: 61.1 us -> 66.7 us  [shift(): return lax.ppermute(v, axis, [(i, (i + d) % n) for i in range(n)])]
    all_gather x2 -> x0, waiting for transfers between devices: 4.18 us -> none  [the longest x1 4.18 us: gather(): w = lax.all_gather(w, 'y', axis=0, tiled=False)]
    another operation x0 -> x3, local copies, waits for them, and re-layouts: none -> 4 us  [the longest x1 3.06 us: body(): at = jnp.stack([z] + [rows_of(x + d) for d in (0, -1, 1, 2)])]
    pallas_call x4 -> x5, Pallas kernels: 16.5 us -> 19.5 us  [call(): pl.pallas_call(kernel, out_shape=out_shape, in_specs=spec(pltpu.SMEM, sca...]
    unnamed x44 -> x46, local copies, waits for them, and re-layouts: 6.9 us -> 4.71 us
    ppermute x31 -> x32, waiting for transfers between devices: 50.9 us -> 52 us  [shift(): return lax.ppermute(v, axis, [(i, (i + d) % n) for i in range(n)])]
  transfers between devices with their start and end apart: 34 -> 33, of which waited for: 12 -> 9; matrix products, arithmetic and copies ran while one was open for 1% -> 3% of each run, Pallas kernels for 10% -> 5%
where the time goes in v1:
time: 153 us
  starting transfers between devices  68.2 us (45%)
  waiting for transfers between devices  52.1 us (34%)
  Pallas kernels  19.5 us (13%)
  local copies, waits for them, and re-layouts  10.5 us (7%)
  other arithmetic  2.27 us (1%)
    ppermute x32, starting transfers between devices, shift(): return lax.ppermute(v, axis, [(i, (i + d) % n) for i in range(n)])  66.7 us
    ppermute x32, waiting for transfers between devices, shift(): return lax.ppermute(v, axis, [(i, (i + d) % n) for i in range(n)])  52 us
    pallas_call x5, Pallas kernels, call(): pl.pallas_call(kernel, out_shape=out_shape, in_specs=spec(pltpu.SMEM, sca...  19.5 us
    unnamed x46, local copies, waits for them, and re-layouts  4.71 us
    another operation x1, local copies, waits for them, and re-layouts, body(): at = jnp.stack([z] + [rows_of(x + d) for d in (0, -1, 1, 2)])  3.06 us
  transfers between devices with their start and end apart: 33, of which 9 were waited for; matrix products, arithmetic and copies ran while one was open for 3% of the time, Pallas kernels for 5%

profile of v1, /device:TPU:1, one launch (start us, length us, event | category | flops | bytes accessed | tf_op | source)
XLA Modules:
  0.0 153.1 jit_solution(6292951208134037111)
XLA Ops:
  1.9 2.5 %collective-permute-start.2 = (bf16[768,128]{1,0:T(8,128)(2,1)S(1)}, bf16[768,128]{1,0:T(8,128)(2,1)S(1)}, u32[]{:S(2)}, u32[]{:S(2)}) collective-permute-start(bf16[768,128]{1,0:T(8,128)(2,1)S(1)} %get-tuple-element.82), channel_id=1, source_target_pairs={{0,8},{8,16},{16,24},{24,32},{32,40},{40,48},{48,56},{56,0},{1,9},... | collective-permute-start | bytes 589832 | tf_op jit(solution)/shard_map/ppermute | solution.py:20
  4.4 4.0 %collective-permute-start.3 = (bf16[768,128]{1,0:T(8,128)(2,1)S(1)}, bf16[768,128]{1,0:T(8,128)(2,1)S(1)}, u32[]{:S(2)}, u32[]{:S(2)}) collective-permute-start(bf16[768,128]{1,0:T(8,128)(2,1)S(1)} %get-tuple-element.82), channel_id=1, source_target_pairs={{0,56},{8,0},{16,8},{24,16},{32,24},{40,32},{48,40},{56,48},{1,57}... | collective-permute-start | bytes 589832 | tf_op jit(solution)/shard_map/ppermute | solution.py:20
  9.8 1.4 collective-permute-start.1
  11.2 1.6 %collective-permute-start.4 = (bf16[512,128]{1,0:T(8,128)(2,1)}, bf16[512,128]{1,0:T(8,128)(2,1)S(1)}, u32[]{:S(2)}, u32[]{:S(2)}) collective-permute-start(bf16[512,128]{1,0:T(8,128)(2,1)} %param.13), channel_id=1, source_target_pairs={{0,0},{1,1},{2,64},{3,65},{4,128},{5,129},{6,192},{7,193},{8,8},{9... | collective-permute-start | bytes 393224 | tf_op jit(solution)/shard_map/ppermute | solution.py:44
  13.2 9.8 %collective-permute-start.7 = (bf16[512,128]{1,0:T(8,128)(2,1)S(1)}, bf16[512,128]{1,0:T(8,128)(2,1)S(1)}, u32[]{:S(2)}, u32[]{:S(2)}) collective-permute-start(bf16[512,128]{1,0:T(8,128)(2,1)S(1)} %collective-permute-done.4), channel_id=1, source_target_pairs={{0,128},{64,192},{128,0},{192,64},{1,129},{65,193},{129,1},{193,65... | collective-permute-start | bytes 393224 | tf_op jit(solution)/shard_map/ppermute | solution.py:20
  23.1 3.5 %collective-permute-start.5 = (bf16[640,128]{1,0:T(8,128)(2,1)S(1)}, bf16[640,128]{1,0:T(8,128)(2,1)S(1)}, u32[]{:S(2)}, u32[]{:S(2)}) collective-permute-start(bf16[640,128]{1,0:T(8,128)(2,1)S(1)} %get-tuple-element.87), channel_id=1, source_target_pairs={{0,64},{64,128},{128,192},{192,0},{1,65},{65,129},{129,193},{193,1... | collective-permute-start | bytes 491528 | tf_op jit(solution)/shard_map/ppermute | solution.py:20
  26.6 2.7 %collective-permute-start.9 = (bf16[768,128]{1,0:T(8,128)(2,1)S(1)}, bf16[768,128]{1,0:T(8,128)(2,1)S(1)}, u32[]{:S(2)}, u32[]{:S(2)}) collective-permute-start(bf16[768,128]{1,0:T(8,128)(2,1)S(1)} %collective-permute-done.3), channel_id=1, source_target_pairs={{0,56},{8,0},{16,8},{24,16},{32,24},{40,32},{48,40},{56,48},{1,57}... | collective-permute-start | bytes 589832 | tf_op jit(solution)/shard_map/ppermute | solution.py:20
  30.6 3.1 %stack.76.at_ref = s32[5]{0:T(128)} concatenate(s32[1]{0:T(128)} %bitcast.1, s32[1]{0:T(128)} %get-tuple-element.91, s32[1]{0:T(128)} %get-tuple-element.90, s32[1]{0:T(128)} %get-tuple-element.92, s32[1]{0:T(128)} %get-tuple-element.89), dimensions={0} | concatenate | bytes 40 | tf_op jit(solution)/shard_map/stack | solution.py:241
  33.9 2.7 %collective-permute-start.11 = (bf16[4,768,128]{2,1,0:T(8,128)(2,1)S(1)}, bf16[4,768,128]{2,1,0:T(8,128)(2,1)S(1)}, u32[]{:S(2)}, u32[]{:S(2)}) collective-permute-start(bf16[4,768,128]{2,1,0:T(8,128)(2,1)S(1)} %maximum_maximum_fusion.rest_9_.rest_0_), channel_id=1, source_target_pairs={{0,56},{8,0},{16,8},{24,16},{32,24},{40,32},{48,40},{56,48},{1,57}... | collective-permute-start | bytes 2359304 | tf_op jit(solution)/shard_map/ppermute | solution.py:20
  36.7 1.5 %collective-permute-start.12 = (bf16[4,768,128]{2,1,0:T(8,128)(2,1)S(1)}, bf16[4,768,128]{2,1,0:T(8,128)(2,1)S(1)}, u32[]{:S(2)}, u32[]{:S(2)}) collective-permute-start(bf16[4,768,128]{2,1,0:T(8,128)(2,1)S(1)} %pad_maximum_fusion.rest_0_), channel_id=1, source_target_pairs={{0,64},{64,128},{128,192},{192,0},{1,65},{65,129},{129,193},{193,1... | collective-permute-start | bytes 2359304 | tf_op jit(solution)/shard_map/ppermute | solution.py:20
  39.4 15.8 %collective-permute-done.14 = bf16[768,128]{1,0:T(8,128)(2,1)S(1)} collective-permute-done((bf16[768,128]{1,0:T(8,128)(2,1)S(1)}, bf16[768,128]{1,0:T(8,128)(2,1)S(1)}, u32[]{:S(2)}, u32[]{:S(2)}) %collective-permute-start.14) | collective-permute-done | bytes 196640 | tf_op jit(solution)/shard_map/ppermute | solution.py:20
  55.4 2.7 %collective-permute-start.16 = (bf16[4,768,128]{2,1,0:T(8,128)(2,1)S(1)}, bf16[4,768,128]{2,1,0:T(8,128)(2,1)S(1)}, u32[]{:S(2)}, u32[]{:S(2)}) collective-permute-start(bf16[4,768,128]{2,1,0:T(8,128)(2,1)S(1)} %collective-permute-done.11.rest_10_.rest_1_), channel_id=1, source_target_pairs={{0,56},{8,0},{16,8},{24,16},{32,24},{40,32},{48,40},{56,48},{1,57}... | collective-permute-start | bytes 2359304 | tf_op jit(solution)/shard_map/ppermute | solution.py:20
  58.1 2.1 %collective-permute-start.19 = (bf16[4,768,128]{2,1,0:T(8,128)(2,1)S(1)}, bf16[4,768,128]{2,1,0:T(8,128)(2,1)S(1)}, u32[]{:S(2)}, u32[]{:S(2)}) collective-permute-start(bf16[4,768,128]{2,1,0:T(8,128)(2,1)S(1)} %collective-permute-done.12.rest_1_), channel_id=1, source_target_pairs={{0,64},{64,128},{128,192},{192,0},{1,65},{65,129},{129,193},{193,1... | collective-permute-start | bytes 2359304 | tf_op jit(solution)/shard_map/ppermute | solution.py:20
  60.2 2.7 %collective-permute-start.18 = (bf16[768,128]{1,0:T(8,128)(2,1)S(1)}, bf16[768,128]{1,0:T(8,128)(2,1)S(1)}, u32[]{:S(2)}, u32[]{:S(2)}) collective-permute-start(bf16[768,128]{1,0:T(8,128)(2,1)S(1)} %collective-permute-done.9), channel_id=1, source_target_pairs={{0,56},{8,0},{16,8},{24,16},{32,24},{40,32},{48,40},{56,48},{1,57}... | collective-permute-start | bytes 589832 | tf_op jit(solution)/shard_map/ppermute | solution.py:20
  62.9 13.0 %collective-permute-done.17 = bf16[768,128]{1,0:T(8,128)(2,1)S(1)} collective-permute-done((bf16[768,128]{1,0:T(8,128)(2,1)S(1)}, bf16[768,128]{1,0:T(8,128)(2,1)S(1)}, u32[]{:S(2)}, u32[]{:S(2)}) %collective-permute-start.17) | collective-permute-done | bytes 196640 | tf_op jit(solution)/shard_map/ppermute | solution.py:20
  76.1 2.8 %collective-permute-start.22 = (bf16[4,768,128]{2,1,0:T(8,128)(2,1)S(1)}, bf16[4,768,128]{2,1,0:T(8,128)(2,1)S(1)}, u32[]{:S(2)}, u32[]{:S(2)}) collective-permute-start(bf16[4,768,128]{2,1,0:T(8,128)(2,1)S(1)} %pad_maximum_fusion.1.rest_4_), channel_id=1, source_target_pairs={{0,64},{64,128},{128,192},{192,0},{1,65},{65,129},{129,193},{193,1... | collective-permute-start | bytes 2359304 | tf_op jit(solution)/shard_map/ppermute | solution.py:20
  78.9 2.7 %collective-permute-start.23 = (bf16[4,768,128]{2,1,0:T(8,128)(2,1)S(1)}, bf16[4,768,128]{2,1,0:T(8,128)(2,1)S(1)}, u32[]{:S(2)}, u32[]{:S(2)}) collective-permute-start(bf16[4,768,128]{2,1,0:T(8,128)(2,1)S(1)} %pad_maximum_fusion.1.rest_4_), channel_id=1, source_target_pairs={{0,192},{64,0},{128,64},{192,128},{1,193},{65,1},{129,65},{193,129... | collective-permute-start | bytes 2359304 | tf_op jit(solution)/shard_map/ppermute | solution.py:20
  81.6 2.7 %collective-permute-start.21 = (bf16[4,768,128]{2,1,0:T(8,128)(2,1)S(1)}, bf16[4,768,128]{2,1,0:T(8,128)(2,1)S(1)}, u32[]{:S(2)}, u32[]{:S(2)}) collective-permute-start(bf16[4,768,128]{2,1,0:T(8,128)(2,1)S(1)} %collective-permute-done.16.rest_11_.rest_2_), channel_id=1, source_target_pairs={{0,56},{8,0},{16,8},{24,16},{32,24},{40,32},{48,40},{56,48},{1,57}... | collective-permute-start | bytes 2359304 | tf_op jit(solution)/shard_map/ppermute | solution.py:20
  84.3 11.9 %collective-permute-done.22.rest_5_ = bf16[4,768,128]{2,1,0:T(8,128)(2,1)S(1)} collective-permute-done((bf16[4,768,128]{2,1,0:T(8,128)(2,1)S(1)}, bf16[4,768,128]{2,1,0:T(8,128)(2,1)S(1)}, u32[]{:S(2)}, u32[]{:S(2)}) %collective-permute-start.22) | collective-permute-done | bytes 786464 | tf_op jit(solution)/shard_map/ppermute | solution.py:20
  96.2 2.2 %collective-permute-done.20.rest_14_.rest_5_ = bf16[4,768,128]{2,1,0:T(8,128)(2,1)S(1)} collective-permute-done((bf16[4,768,128]{2,1,0:T(8,128)(2,1)S(1)}, bf16[4,768,128]{2,1,0:T(8,128)(2,1)S(1)}, u32[]{:S(2)}, u32[]{:S(2)}) %collective-permute-start.20) | collective-permute-done | bytes 786464 | tf_op jit(solution)/shard_map/ppermute | solution.py:20
  98.6 2.7 %collective-permute-start.25 = (bf16[2,768,128]{2,1,0:T(8,128)(2,1)S(1)}, bf16[2,768,128]{2,1,0:T(8,128)(2,1)S(1)}, u32[]{:S(2)}, u32[]{:S(2)}) collective-permute-start(bf16[2,768,128]{2,1,0:T(8,128)(2,1)S(1)} %slice.51), channel_id=1, source_target_pairs={{0,192},{64,0},{128,64},{192,128},{1,193},{65,1},{129,65},{193,129... | collective-permute-start | bytes 1179656 | tf_op jit(solution)/shard_map/ppermute | solution.py:20
  101.5 3.0 %collective-permute-start.27 = (bf16[2,768,128]{2,1,0:T(8,128)(2,1)S(1)}, bf16[2,768,128]{2,1,0:T(8,128)(2,1)S(1)}, u32[]{:S(2)}, u32[]{:S(2)}) collective-permute-start(bf16[2,768,128]{2,1,0:T(8,128)(2,1)S(1)} %slice.53), channel_id=1, source_target_pairs={{0,56},{8,0},{16,8},{24,16},{32,24},{40,32},{48,40},{56,48},{1,57}... | collective-permute-start | bytes 1179656 | tf_op jit(solution)/shard_map/ppermute | solution.py:20
  104.5 1.9 %collective-permute-done.24.rest_7_ = bf16[2,768,128]{2,1,0:T(8,128)(2,1)S(1)} collective-permute-done((bf16[2,768,128]{2,1,0:T(8,128)(2,1)S(1)}, bf16[2,768,128]{2,1,0:T(8,128)(2,1)S(1)}, u32[]{:S(2)}, u32[]{:S(2)}) %collective-permute-start.24) | collective-permute-done | bytes 393248 | tf_op jit(solution)/shard_map/ppermute | solution.py:20
  106.4 3.2 %collective-permute-done.26.rest_13_.rest_4_ = bf16[2,768,128]{2,1,0:T(8,128)(2,1)S(1)} collective-permute-done((bf16[2,768,128]{2,1,0:T(8,128)(2,1)S(1)}, bf16[2,768,128]{2,1,0:T(8,128)(2,1)S(1)}, u32[]{:S(2)}, u32[]{:S(2)}) %collective-permute-start.26) | collective-permute-done | bytes 393248 | tf_op jit(solution)/shard_map/ppermute | solution.py:20
  111.1 11.7 %shard_map.91.a_ref = bf16[512,512]{1,0:T(8,128)(2,1)} custom-call(s32[60]{0:T(128)} %reshape.322.place_ref, bf16[512,512]{1,0:T(8,128)(2,1)} %q_ref.1, bf16[512,128]{1,0:T(8,128)(2,1)} %k_ref.1, bf16[512,128]{1,0:T(8,128)(2,1)} %v_ref.1, bf16[4,768,128]{2,1,0:T(8,128)(2,1)} %copy-done.7, bf16[4,768,128]{2,1,0:T(8,128)(2,1)} %copy-done.17, ...), custom_call_target="tpu_custom_call" | custom-call | flops 3221225472 | bytes 8388608 | tf_op jit(solution)/shard_map/pallas_call | solution.py:191
  122.9 2.7 %collective-permute-start.29 = (bf16[512,512]{1,0:T(8,128)(2,1)}, bf16[512,512]{1,0:T(8,128)(2,1)S(1)}, u32[]{:S(2)}, u32[]{:S(2)}) collective-permute-start(bf16[512,512]{1,0:T(8,128)(2,1)} %shard_map.91.a_ref), channel_id=1, source_target_pairs={{0,6},{2,0},{4,2},{6,4},{1,7},{3,1},{5,3},{7,5},{8,14},{10,8},{12,... | collective-permute-start | bytes 1572872 | tf_op jit(solution)/shard_map/ppermute | solution.py:20
  125.6 5.7 %shard_map.92 = (f32[512,1024]{1,0:T(8,128)}, bf16[2,8,512,128]{3,2,1,0:T(8,128)(2,1)}, bf16[8,512,128]{2,1,0:T(8,128)(2,1)}) custom-call(s32[5]{0:T(128)} %stack.76.at_ref, bf16[512,512]{1,0:T(8,128)(2,1)} %shard_map.91.a_ref, bf16[4,768,128]{2,1,0:T(8,128)(2,1)} %copy-done.4, bf16[4,768,128]{2,1,0:T(8,128)(2,1)} %copy-done.10, ...), custom_call_target="tpu_custom_call" | custom-call | flops 536870912 | bytes 8388608 | tf_op jit(solution)/shard_map/pallas_call | solution.py:191
  133.0 2.2 %collective-permute-start.31 = (bf16[256,512]{1,0:T(8,128)(2,1)S(1)}, bf16[256,512]{1,0:T(8,128)(2,1)S(1)}, u32[]{:S(2)}, u32[]{:S(2)}) collective-permute-start(bf16[256,512]{1,0:T(8,128)(2,1)S(1)} %slice.55), channel_id=1, source_target_pairs={{0,6},{2,0},{4,2},{6,4},{1,7},{3,1},{5,3},{7,5},{8,14},{10,8},{12,... | collective-permute-start | bytes 786440 | tf_op jit(solution)/shard_map/ppermute | solution.py:20
  135.3 1.6 %copy-done.2 = f32[512,1024]{1,0:T(8,128)S(1)} copy-done((f32[512,1024]{1,0:T(8,128)S(1)}, f32[512,1024]{1,0:T(8,128)}, u32[]{:S(2)}) %copy-start.2) | copy-done | bytes 2097176
  136.9 1.6 %copy-done.3 = bf16[2,8,512,128]{3,2,1,0:T(8,128)(2,1)S(1)} copy-done((bf16[2,8,512,128]{3,2,1,0:T(8,128)(2,1)S(1)}, bf16[2,8,512,128]{3,2,1,0:T(8,128)(2,1)}, u32[]{:S(2)}) %copy-start.3) | copy-done | bytes 2097176
  139.7 1.7 %collective-permute-done.30.a0_ref = bf16[256,512]{1,0:T(8,128)(2,1)S(1)} collective-permute-done((bf16[256,512]{1,0:T(8,128)(2,1)S(1)}, bf16[256,512]{1,0:T(8,128)(2,1)S(1)}, u32[]{:S(2)}, u32[]{:S(2)}) %collective-permute-start.30) | collective-permute-done | bytes 262176 | tf_op jit(solution)/shard_map/ppermute | solution.py:20
  141.9 8.7 %collective-permute-start.32 = (bf16[512,512]{1,0:T(8,128)(2,1)S(1)}, bf16[512,512]{1,0:T(8,128)(2,1)S(1)}, u32[]{:S(2)}, u32[]{:S(2)}) collective-permute-start(bf16[512,512]{1,0:T(8,128)(2,1)S(1)} %shard_map.95), channel_id=1, source_target_pairs={{0,1},{1,0},{2,3},{3,2},{4,5},{5,4},{6,7},{7,6},{8,9},{9,8},{10,11... | collective-permute-start | bytes 1572872 | tf_op jit(solution)/shard_map/ppermute | solution.py:20
  (115 shorter events, 14.4 us)
Async XLA Ops:
  1.9 11.3 %collective-permute-start.2 = (bf16[768,128]{1,0:T(8,128)(2,1)S(1)}, bf16[768,128]{1,0:T(8,128)(2,1)S(1)}, u32[]{:S(2)}, u32[]{:S(2)}) collective-permute-start(bf16[768,128]{1,0:T(8,128)(2,1)S(1)} %get-tuple-element.82), channel_id=1, source_target_pairs={{0,8},{8,16},{16,24},{24,32},{32,40},{40,48},{48,56},{56,0},{1,9},... | collective-permute-start | bytes 589832 | tf_op jit(solution)/shard_map/ppermute | solution.py:20
  4.4 8.8 %collective-permute-start.3 = (bf16[768,128]{1,0:T(8,128)(2,1)S(1)}, bf16[768,128]{1,0:T(8,128)(2,1)S(1)}, u32[]{:S(2)}, u32[]{:S(2)}) collective-permute-start(bf16[768,128]{1,0:T(8,128)(2,1)S(1)} %get-tuple-element.82), channel_id=1, source_target_pairs={{0,56},{8,0},{16,8},{24,16},{32,24},{40,32},{48,40},{56,48},{1,57}... | collective-permute-start | bytes 589832 | tf_op jit(solution)/shard_map/ppermute | solution.py:20
  8.5 4.7 %collective-permute-start = (bf16[256,128]{1,0:T(8,128)(2,1)S(1)}, bf16[256,128]{1,0:T(8,128)(2,1)S(1)}, u32[]{:S(2)}, u32[]{:S(2)}) collective-permute-start(bf16[256,128]{1,0:T(8,128)(2,1)S(1)} %get-tuple-element.84), channel_id=1, source_target_pairs={{0,64},{64,128},{128,192},{192,0},{1,65},{65,129},{129,193},{193,1... | collective-permute-start | bytes 196616 | tf_op jit(solution)/shard_map/ppermute | solution.py:20
  9.8 3.4 %collective-permute-start.1 = (bf16[256,128]{1,0:T(8,128)(2,1)S(1)}, bf16[256,128]{1,0:T(8,128)(2,1)S(1)}, u32[]{:S(2)}, u32[]{:S(2)}) collective-permute-start(bf16[256,128]{1,0:T(8,128)(2,1)S(1)} %get-tuple-element.84), channel_id=1, source_target_pairs={{0,192},{64,0},{128,64},{192,128},{1,193},{65,1},{129,65},{193,129... | collective-permute-start | bytes 196616 | tf_op jit(solution)/shard_map/ppermute | solution.py:20
  13.2 20.4 %collective-permute-start.7 = (bf16[512,128]{1,0:T(8,128)(2,1)S(1)}, bf16[512,128]{1,0:T(8,128)(2,1)S(1)}, u32[]{:S(2)}, u32[]{:S(2)}) collective-permute-start(bf16[512,128]{1,0:T(8,128)(2,1)S(1)} %collective-permute-done.4), channel_id=1, source_target_pairs={{0,128},{64,192},{128,0},{192,64},{1,129},{65,193},{129,1},{193,65... | collective-permute-start | bytes 393224 | tf_op jit(solution)/shard_map/ppermute | solution.py:20
  23.1 10.6 %collective-permute-start.5 = (bf16[640,128]{1,0:T(8,128)(2,1)S(1)}, bf16[640,128]{1,0:T(8,128)(2,1)S(1)}, u32[]{:S(2)}, u32[]{:S(2)}) collective-permute-start(bf16[640,128]{1,0:T(8,128)(2,1)S(1)} %get-tuple-element.87), channel_id=1, source_target_pairs={{0,64},{64,128},{128,192},{192,0},{1,65},{65,129},{129,193},{193,1... | collective-permute-start | bytes 491528 | tf_op jit(solution)/shard_map/ppermute | solution.py:20
  26.5 7.1 %collective-permute-start.6 = (bf16[640,128]{1,0:T(8,128)(2,1)S(1)}, bf16[640,128]{1,0:T(8,128)(2,1)S(1)}, u32[]{:S(2)}, u32[]{:S(2)}) collective-permute-start(bf16[640,128]{1,0:T(8,128)(2,1)S(1)} %get-tuple-element.86), channel_id=1, source_target_pairs={{0,192},{64,0},{128,64},{192,128},{1,193},{65,1},{129,65},{193,129... | collective-permute-start | bytes 491528 | tf_op jit(solution)/shard_map/ppermute | solution.py:20
  26.6 7.1 %collective-permute-start.8 = (bf16[768,128]{1,0:T(8,128)(2,1)S(1)}, bf16[768,128]{1,0:T(8,128)(2,1)S(1)}, u32[]{:S(2)}, u32[]{:S(2)}) collective-permute-start(bf16[768,128]{1,0:T(8,128)(2,1)S(1)} %collective-permute-done.2), channel_id=1, source_target_pairs={{0,8},{8,16},{16,24},{24,32},{32,40},{40,48},{48,56},{56,0},{1,9},... | collective-permute-start | bytes 589832 | tf_op jit(solution)/shard_map/ppermute | solution.py:20
  26.6 7.1 %collective-permute-start.9 = (bf16[768,128]{1,0:T(8,128)(2,1)S(1)}, bf16[768,128]{1,0:T(8,128)(2,1)S(1)}, u32[]{:S(2)}, u32[]{:S(2)}) collective-permute-start(bf16[768,128]{1,0:T(8,128)(2,1)S(1)} %collective-permute-done.3), channel_id=1, source_target_pairs={{0,56},{8,0},{16,8},{24,16},{32,24},{40,32},{48,40},{56,48},{1,57}... | collective-permute-start | bytes 589832 | tf_op jit(solution)/shard_map/ppermute | solution.py:20
  33.8 21.5 %collective-permute-start.10 = (bf16[4,768,128]{2,1,0:T(8,128)(2,1)S(1)}, bf16[4,768,128]{2,1,0:T(8,128)(2,1)S(1)}, u32[]{:S(2)}, u32[]{:S(2)}) collective-permute-start(bf16[4,768,128]{2,1,0:T(8,128)(2,1)S(1)} %maximum_maximum_fusion.rest_9_.rest_0_), channel_id=1, source_target_pairs={{0,8},{8,16},{16,24},{24,32},{32,40},{40,48},{48,56},{56,0},{1,9},... | collective-permute-start | bytes 2359304 | tf_op jit(solution)/shard_map/ppermute | solution.py:20
  33.9 21.4 %collective-permute-start.11 = (bf16[4,768,128]{2,1,0:T(8,128)(2,1)S(1)}, bf16[4,768,128]{2,1,0:T(8,128)(2,1)S(1)}, u32[]{:S(2)}, u32[]{:S(2)}) collective-permute-start(bf16[4,768,128]{2,1,0:T(8,128)(2,1)S(1)} %maximum_maximum_fusion.rest_9_.rest_0_), channel_id=1, source_target_pairs={{0,56},{8,0},{16,8},{24,16},{32,24},{40,32},{48,40},{56,48},{1,57}... | collective-permute-start | bytes 2359304 | tf_op jit(solution)/shard_map/ppermute | solution.py:20
  36.7 18.6 %collective-permute-start.12 = (bf16[4,768,128]{2,1,0:T(8,128)(2,1)S(1)}, bf16[4,768,128]{2,1,0:T(8,128)(2,1)S(1)}, u32[]{:S(2)}, u32[]{:S(2)}) collective-permute-start(bf16[4,768,128]{2,1,0:T(8,128)(2,1)S(1)} %pad_maximum_fusion.rest_0_), channel_id=1, source_target_pairs={{0,64},{64,128},{128,192},{192,0},{1,65},{65,129},{129,193},{193,1... | collective-permute-start | bytes 2359304 | tf_op jit(solution)/shard_map/ppermute | solution.py:20
  38.2 17.1 %collective-permute-start.13 = (bf16[4,768,128]{2,1,0:T(8,128)(2,1)S(1)}, bf16[4,768,128]{2,1,0:T(8,128)(2,1)S(1)}, u32[]{:S(2)}, u32[]{:S(2)}) collective-permute-start(bf16[4,768,128]{2,1,0:T(8,128)(2,1)S(1)} %pad_maximum_fusion.rest_0_), channel_id=1, source_target_pairs={{0,192},{64,0},{128,64},{192,128},{1,193},{65,1},{129,65},{193,129... | collective-permute-start | bytes 2359304 | tf_op jit(solution)/shard_map/ppermute | solution.py:20
  39.4 15.8 %collective-permute-start.14 = (bf16[768,128]{1,0:T(8,128)(2,1)S(1)}, bf16[768,128]{1,0:T(8,128)(2,1)S(1)}, u32[]{:S(2)}, u32[]{:S(2)}) collective-permute-start(bf16[768,128]{1,0:T(8,128)(2,1)S(1)} %collective-permute-done.8), channel_id=1, source_target_pairs={{0,8},{8,16},{16,24},{24,32},{32,40},{40,48},{48,56},{56,0},{1,9},... | collective-permute-start | bytes 589832 | tf_op jit(solution)/shard_map/ppermute | solution.py:20
  55.3 20.6 %collective-permute-start.15 = (bf16[4,768,128]{2,1,0:T(8,128)(2,1)S(1)}, bf16[4,768,128]{2,1,0:T(8,128)(2,1)S(1)}, u32[]{:S(2)}, u32[]{:S(2)}) collective-permute-start(bf16[4,768,128]{2,1,0:T(8,128)(2,1)S(1)} %collective-permute-done.10.rest_16_.rest_7_), channel_id=1, source_target_pairs={{0,8},{8,16},{16,24},{24,32},{32,40},{40,48},{48,56},{56,0},{1,9},... | collective-permute-start | bytes 2359304 | tf_op jit(solution)/shard_map/ppermute | solution.py:20
  55.4 20.5 %collective-permute-start.16 = (bf16[4,768,128]{2,1,0:T(8,128)(2,1)S(1)}, bf16[4,768,128]{2,1,0:T(8,128)(2,1)S(1)}, u32[]{:S(2)}, u32[]{:S(2)}) collective-permute-start(bf16[4,768,128]{2,1,0:T(8,128)(2,1)S(1)} %collective-permute-done.11.rest_10_.rest_1_), channel_id=1, source_target_pairs={{0,56},{8,0},{16,8},{24,16},{32,24},{40,32},{48,40},{56,48},{1,57}... | collective-permute-start | bytes 2359304 | tf_op jit(solution)/shard_map/ppermute | solution.py:20
  58.1 17.8 %collective-permute-start.19 = (bf16[4,768,128]{2,1,0:T(8,128)(2,1)S(1)}, bf16[4,768,128]{2,1,0:T(8,128)(2,1)S(1)}, u32[]{:S(2)}, u32[]{:S(2)}) collective-permute-start(bf16[4,768,128]{2,1,0:T(8,128)(2,1)S(1)} %collective-permute-done.12.rest_1_), channel_id=1, source_target_pairs={{0,64},{64,128},{128,192},{192,0},{1,65},{65,129},{129,193},{193,1... | collective-permute-start | bytes 2359304 | tf_op jit(solution)/shard_map/ppermute | solution.py:20
  60.2 15.7 %collective-permute-start.17 = (bf16[768,128]{1,0:T(8,128)(2,1)S(1)}, bf16[768,128]{1,0:T(8,128)(2,1)S(1)}, u32[]{:S(2)}, u32[]{:S(2)}) collective-permute-start(bf16[768,128]{1,0:T(8,128)(2,1)S(1)} %collective-permute-done.14), channel_id=1, source_target_pairs={{0,8},{8,16},{16,24},{24,32},{32,40},{40,48},{48,56},{56,0},{1,9},... | collective-permute-start | bytes 589832 | tf_op jit(solution)/shard_map/ppermute | solution.py:20
  60.2 15.7 %collective-permute-start.18 = (bf16[768,128]{1,0:T(8,128)(2,1)S(1)}, bf16[768,128]{1,0:T(8,128)(2,1)S(1)}, u32[]{:S(2)}, u32[]{:S(2)}) collective-permute-start(bf16[768,128]{1,0:T(8,128)(2,1)S(1)} %collective-permute-done.9), channel_id=1, source_target_pairs={{0,56},{8,0},{16,8},{24,16},{32,24},{40,32},{48,40},{56,48},{1,57}... | collective-permute-start | bytes 589832 | tf_op jit(solution)/shard_map/ppermute | solution.py:20
  76.1 20.1 %collective-permute-start.22 = (bf16[4,768,128]{2,1,0:T(8,128)(2,1)S(1)}, bf16[4,768,128]{2,1,0:T(8,128)(2,1)S(1)}, u32[]{:S(2)}, u32[]{:S(2)}) collective-permute-start(bf16[4,768,128]{2,1,0:T(8,128)(2,1)S(1)} %pad_maximum_fusion.1.rest_4_), channel_id=1, source_target_pairs={{0,64},{64,128},{128,192},{192,0},{1,65},{65,129},{129,193},{193,1... | collective-permute-start | bytes 2359304 | tf_op jit(solution)/shard_map/ppermute | solution.py:20
  78.9 17.3 %collective-permute-start.23 = (bf16[4,768,128]{2,1,0:T(8,128)(2,1)S(1)}, bf16[4,768,128]{2,1,0:T(8,128)(2,1)S(1)}, u32[]{:S(2)}, u32[]{:S(2)}) collective-permute-start(bf16[4,768,128]{2,1,0:T(8,128)(2,1)S(1)} %pad_maximum_fusion.1.rest_4_), channel_id=1, source_target_pairs={{0,192},{64,0},{128,64},{192,128},{1,193},{65,1},{129,65},{193,129... | collective-permute-start | bytes 2359304 | tf_op jit(solution)/shard_map/ppermute | solution.py:20
  81.6 16.8 %collective-permute-start.20 = (bf16[4,768,128]{2,1,0:T(8,128)(2,1)S(1)}, bf16[4,768,128]{2,1,0:T(8,128)(2,1)S(1)}, u32[]{:S(2)}, u32[]{:S(2)}) collective-permute-start(bf16[4,768,128]{2,1,0:T(8,128)(2,1)S(1)} %collective-permute-done.15.rest_15_.rest_6_), channel_id=1, source_target_pairs={{0,8},{8,16},{16,24},{24,32},{32,40},{40,48},{48,56},{56,0},{1,9},... | collective-permute-start | bytes 2359304 | tf_op jit(solution)/shard_map/ppermute | solution.py:20
  81.6 16.8 %collective-permute-start.21 = (bf16[4,768,128]{2,1,0:T(8,128)(2,1)S(1)}, bf16[4,768,128]{2,1,0:T(8,128)(2,1)S(1)}, u32[]{:S(2)}, u32[]{:S(2)}) collective-permute-start(bf16[4,768,128]{2,1,0:T(8,128)(2,1)S(1)} %collective-permute-done.16.rest_11_.rest_2_), channel_id=1, source_target_pairs={{0,56},{8,0},{16,8},{24,16},{32,24},{40,32},{48,40},{56,48},{1,57}... | collective-permute-start | bytes 2359304 | tf_op jit(solution)/shard_map/ppermute | solution.py:20
  98.4 7.9 %collective-permute-start.24 = (bf16[2,768,128]{2,1,0:T(8,128)(2,1)S(1)}, bf16[2,768,128]{2,1,0:T(8,128)(2,1)S(1)}, u32[]{:S(2)}, u32[]{:S(2)}) collective-permute-start(bf16[2,768,128]{2,1,0:T(8,128)(2,1)S(1)} %slice.50), channel_id=1, source_target_pairs={{0,64},{64,128},{128,192},{192,0},{1,65},{65,129},{129,193},{193,1... | collective-permute-start | bytes 1179656 | tf_op jit(solution)/shard_map/ppermute | solution.py:20
  98.6 7.8 %collective-permute-start.25 = (bf16[2,768,128]{2,1,0:T(8,128)(2,1)S(1)}, bf16[2,768,128]{2,1,0:T(8,128)(2,1)S(1)}, u32[]{:S(2)}, u32[]{:S(2)}) collective-permute-start(bf16[2,768,128]{2,1,0:T(8,128)(2,1)S(1)} %slice.51), channel_id=1, source_target_pairs={{0,192},{64,0},{128,64},{192,128},{1,193},{65,1},{129,65},{193,129... | collective-permute-start | bytes 1179656 | tf_op jit(solution)/shard_map/ppermute | solution.py:20
  101.4 8.2 %collective-permute-start.26 = (bf16[2,768,128]{2,1,0:T(8,128)(2,1)S(1)}, bf16[2,768,128]{2,1,0:T(8,128)(2,1)S(1)}, u32[]{:S(2)}, u32[]{:S(2)}) collective-permute-start(bf16[2,768,128]{2,1,0:T(8,128)(2,1)S(1)} %slice.52), channel_id=1, source_target_pairs={{0,8},{8,16},{16,24},{24,32},{32,40},{40,48},{48,56},{56,0},{1,9},... | collective-permute-start | bytes 1179656 | tf_op jit(solution)/shard_map/ppermute | solution.py:20
  101.5 8.1 %collective-permute-start.27 = (bf16[2,768,128]{2,1,0:T(8,128)(2,1)S(1)}, bf16[2,768,128]{2,1,0:T(8,128)(2,1)S(1)}, u32[]{:S(2)}, u32[]{:S(2)}) collective-permute-start(bf16[2,768,128]{2,1,0:T(8,128)(2,1)S(1)} %slice.53), channel_id=1, source_target_pairs={{0,56},{8,0},{16,8},{24,16},{32,24},{40,32},{48,40},{56,48},{1,57}... | collective-permute-start | bytes 1179656 | tf_op jit(solution)/shard_map/ppermute | solution.py:20
  122.8 9.5 %collective-permute-start.28 = (bf16[512,512]{1,0:T(8,128)(2,1)}, bf16[512,512]{1,0:T(8,128)(2,1)S(1)}, u32[]{:S(2)}, u32[]{:S(2)}) collective-permute-start(bf16[512,512]{1,0:T(8,128)(2,1)} %shard_map.91.a_ref), channel_id=1, source_target_pairs={{0,2},{2,4},{4,6},{6,0},{1,3},{3,5},{5,7},{7,1},{8,10},{10,12},{12... | collective-permute-start | bytes 1572872 | tf_op jit(solution)/shard_map/ppermute | solution.py:20
  122.9 9.4 %collective-permute-start.29 = (bf16[512,512]{1,0:T(8,128)(2,1)}, bf16[512,512]{1,0:T(8,128)(2,1)S(1)}, u32[]{:S(2)}, u32[]{:S(2)}) collective-permute-start(bf16[512,512]{1,0:T(8,128)(2,1)} %shard_map.91.a_ref), channel_id=1, source_target_pairs={{0,6},{2,0},{4,2},{6,4},{1,7},{3,1},{5,3},{7,5},{8,14},{10,8},{12,... | collective-permute-start | bytes 1572872 | tf_op jit(solution)/shard_map/ppermute | solution.py:20
  132.4 9.0 %collective-permute-start.30 = (bf16[256,512]{1,0:T(8,128)(2,1)S(1)}, bf16[256,512]{1,0:T(8,128)(2,1)S(1)}, u32[]{:S(2)}, u32[]{:S(2)}) collective-permute-start(bf16[256,512]{1,0:T(8,128)(2,1)S(1)} %slice.54), channel_id=1, source_target_pairs={{0,2},{2,4},{4,6},{6,0},{1,3},{3,5},{5,7},{7,1},{8,10},{10,12},{12... | collective-permute-start | bytes 786440 | tf_op jit(solution)/shard_map/ppermute | solution.py:20
  133.0 8.4 %collective-permute-start.31 = (bf16[256,512]{1,0:T(8,128)(2,1)S(1)}, bf16[256,512]{1,0:T(8,128)(2,1)S(1)}, u32[]{:S(2)}, u32[]{:S(2)}) collective-permute-start(bf16[256,512]{1,0:T(8,128)(2,1)S(1)} %slice.55), channel_id=1, source_target_pairs={{0,6},{2,0},{4,2},{6,4},{1,7},{3,1},{5,3},{7,5},{8,14},{10,8},{12,... | collective-permute-start | bytes 786440 | tf_op jit(solution)/shard_map/ppermute | solution.py:20
  141.9 10.3 %collective-permute-start.32 = (bf16[512,512]{1,0:T(8,128)(2,1)S(1)}, bf16[512,512]{1,0:T(8,128)(2,1)S(1)}, u32[]{:S(2)}, u32[]{:S(2)}) collective-permute-start(bf16[512,512]{1,0:T(8,128)(2,1)S(1)} %shard_map.95), channel_id=1, source_target_pairs={{0,1},{1,0},{2,3},{3,2},{4,5},{5,4},{6,7},{7,6},{8,9},{9,8},{10,11... | collective-permute-start | bytes 1572872 | tf_op jit(solution)/shard_map/ppermute | solution.py:20
  (24 other events, 517.8 us)

commit v2 on v1

--- a/solution.py
+++ b/solution.py
@@ -14,7 +14,13 @@
 SLOTS = 3
 NY, NZ, NX, NC = 4, 8, 4, 2
 AXES = ("y", "z", "x", "c")
+ARRAYS = ("kv", "z1m", "z1p", "z2m", "z2p", "s1m", "s1p", "s2p", "g0p", "g0m")
+ARRAYS += ("gap", "gam", "gbp", "gbm", "gcp", "gcm", "gdp")
 HALF = BLK // 2
+ZROWS = 896
+ZVALUES = ZROWS - BLK
+LAST = BLK - ZVALUES
+SLOT = LAST + BLK
 SCALE = math.log2(math.e) / math.sqrt(HD)
 def shift(v, axis, d, n):
     return lax.ppermute(v, axis, [(i, (i + d) % n) for i in range(n)])
@@ -38,72 +44,87 @@
     return jnp.concatenate(parts)
 
 
-def gather(zc, yc, w, turn, early):
-    n = yc.shape[0] // 2
-    y1p, y1m, z1p, z1m = yp(yc), ym(yc), zp(zc), zm(zc)
+def places():
+    z3 = NY * SLOT
+    out = {}
+    own = {0: ("kv", 0), 1: ("z1m", 0), 7: ("z1p", 0), 2: ("z2m", 0), 6: ("z2p", 0), 3: ("s1m", z3), 5: ("s1p", z3), 4: ("s2p", z3)}
+    side = {0: ("g0", 0), 1: ("ga", 0), 7: ("ga", 1), 2: ("ga", 2), 6: ("ga", 3), 3: ("gb", 0), 5: ("gb", 1), 4: ("gc", 0)}
+    far = {0: ("gbm", 2), 1: ("gbp", 2), 7: ("gbp", 3), 2: ("gcp", 1), 6: ("gcm", 1), 3: ("gcp", 2), 5: ("gcm", 2), 4: ("gdp", 0)}
+    for dz in range(NZ):
+        out[0, dz] = own[dz]
+        out[2, dz] = far[dz][0], far[dz][1] * ZROWS
+        for dy, way in ((3, "p"), (1, "m")):
+            out[dy, dz] = side[dz][0] + way, side[dz][1] * ZROWS
+    return out
+
+
+def gather(kv, w, turn, early):
+    half = ZROWS + LAST // 2
+    z1p, z1m, g0p, g0m = zp(kv), zm(kv), yp(kv), ym(kv)
     w = lax.ppermute(w, AXES, turn)
-    (y1p, y1m, z1p, z1m, w), _ = gate((y1p, y1m, z1p, z1m, w), ())
-    both_p, both_m, w2, z2p, z2m = yp(join(y1p[:n], w)), ym(join(y1m[n:], w)), y2(w), zp(z1p), zm(z1m)
-    (both_p, both_m, w2, z2p, z2m), early = gate((both_p, both_m, w2, z2p, z2m), early)
-    y2p, y2m, w = both_p[:n], both_m[:n], jnp.stack([w, both_p[n:], both_m[n:], w2])
-    s0 = jnp.concatenate([jnp.stack([yc, y1p, y1m, join(y2p, y2m)]), w], axis=1)
-    g1 = jnp.stack([zc, z1m, z1p, z2m])
-    s1p, s1m, g1p, g1m, z3p = zp(s0), zm(s0), yp(g1), ym(g1), zp(z2p)
-    (s1p, s1m, g1p, g1m, z3p, z2m), _ = gate((s1p, s1m, g1p, g1m, z3p, z2m), ())
-    s2p, s2m, z4p, z3m, g1x = zp(s1p), zm(s1m), zp(z3p), zm(z2m), yp(g1p)
-    (s2p, s2m, z4p, z3m, g1x), _ = gate((s2p, s2m, z4p, z3m, g1x), ())
-    g2 = jnp.stack([z2p, z3m, z3p, z4p])
-    s3p, s3m, g2p, g2m = zp(s2p), zm(s2m), yp(g2), ym(g2)
-    (s3p, s3m, g2p, g2m), _ = gate((s3p, s3m, g2p, g2m), ())
-    s4p, s4m, g2h, g2l = zp(s3p[:2]), zm(s3m[2:]), yp(g2p[:2]), ym(g2m[2:])
-    za = [g1, g1p, g1m, g1x, g2, g2p, g2m, g2h, g2l]
-    ya = [s0, s1m, s2m, s3m, s4p, s3p, s2p, s1p, s4m]
-    return za, ya, early
-
-
-def block_places(route, y, z):
-    by, dz = route // NZ, (route - z) % NZ
-    dy = (by - y) % NY
-    first = (dz == 0) | (dz == 1) | (dz == 7) | (dz == 2)
-    zslot = jnp.where((dz == 1) | (dz == 3), 1, jnp.where((dz == 7) | (dz == 5), 2, jnp.where((dz == 2) | (dz == 4), 3, 0)))
-    yslot = jnp.where(dy == 0, 0, jnp.where(dy == 3, 1, jnp.where(dy == 1, 2, 3)))
-    zarray = jnp.where(first, 0, 4) + yslot
-    tail = (zarray == 7) & (zslot >= 2)
-    late = (dz == 4) & (yslot >= 2)
-    zarray, zslot = jnp.where(tail, 8, zarray), jnp.where(tail, zslot - 2, zslot)
-    yarray, yslot = jnp.where(late, NZ, dz), jnp.where(late, yslot - 2, yslot)
-    ok = (route < y * NZ + z).astype(jnp.int32)
-    return jnp.stack([zarray, zslot, yarray, yslot, ok]).reshape(-1)
+    (z1p, z1m, g0p, g0m, w), early = gate((z1p, z1m, g0p, g0m, w), early)
+    to_p, to_m, w2, z2p, z2m = join(g0p[ZROWS:half], w), join(g0m[half:], w), y2(w), zp(z1p), zm(z1m)
+    both_p, both_m = yp(to_p), ym(to_m)
+    (both_p, both_m, w2, z2p, z2m), _ = gate((both_p, both_m, w2, z2p, z2m), ())
+    n = LAST // 2
+    s0 = kv[ZROWS:], w, g0p[ZROWS:], both_p[n:], g0m[ZROWS:], both_m[n:], both_p[:n], both_m[:n], w2
+    s0p, s0m, ga = join(*s0, z2p[:ZROWS]), join(*s0, z2m[:ZROWS]), join(*(v[:ZROWS] for v in (z1m, z1p, z2m, z2p)))
+    s1p, s1m, gap, gam = zp(s0p), zm(s0m), yp(ga), ym(ga)
+    (s1p, s1m, gap, gam), _ = gate((s1p, s1m, gap, gam), ())
+    z3, chunk = NY * SLOT, lambda v, i: v[i * ZROWS : (i + 1) * ZROWS]
+    z3m, z3p = s1m[z3:], s1p[z3:]
+    s2p, s2m, gbp, gbm = zp(s1p), zm(s1m), yp(join(z3m, z3p, gap[: 2 * ZROWS])), ym(join(z3m, z3p, g0m[:ZROWS]))
+    (s2p, s2m, gbp, gbm), _ = gate((s2p, s2m, gbp, gbm), ())
+    z4 = s2p[z3:]
+    s3p, s3m = zp(s2p[:z3]), zm(s2m[:z3])
+    gcp, gcm = yp(join(z4, chunk(gap, 2), chunk(gbp, 0))), ym(join(z4, chunk(gam, 3), chunk(gbm, 1)))
+    (s3p, s3m, gcp, gcm), _ = gate((s3p, s3m, gcp, gcm), ())
+    s4p, s4m, gdp = zp(s3p[: z3 // 2]), zm(s3m[z3 // 2 :]), yp(chunk(gcp, 0))
+    named = (kv, z1m, z1p, z2m, z2p, s1m, s1p, s2p, g0p, g0m, gap, gam, gbp, gbm, gcp, gcm, gdp)
+    return named, [s0p, s1m, s2m, s3m, s4p, s3p, s2p, s1p, s4m], early
 
 
 TILE = 128
 
 
-def attend_kernel(place_ref, q_ref, k_ref, v_ref, *rest):
-    za, ya, out_ref, kbuf, vbuf, sems = rest[:9], rest[9:18], rest[18], rest[19], rest[20], rest[21]
+def attend_kernel(route_ref, place_ref, table_ref, q_ref, k_ref, v_ref, *rest):
+    count = len(ARRAYS)
+    named, ya, out_ref, (kbuf, vbuf, sems) = rest[:count], rest[count : count + 9], rest[count + 9], rest[count + 10 :]
     n = HEADS * SLOTS
-
-    def copies(u, i, block):
-        half = lambda first, at: pltpu.make_async_copy(
-            block.at[pl.ds(first, HALF)], vbuf.at[u, pl.ds(at, HALF), pl.ds(0, HD)], sems.at[u, i, 1]
-        )
+    y, z = place_ref[0], place_ref[1]
+    me = y * NZ + z
+
+    def copies(u, i, block, first):
+        rows = lambda at, size: block.at[pl.ds(pl.multiple_of(first + at, 16), size)]
+        part = lambda at, size: vbuf.at[u, pl.ds(at, size), pl.ds(0, HD)]
         if i == 1:
-            return [half(0, HALF)]
-        return [pltpu.make_async_copy(block.at[pl.ds(0, BLK)], kbuf.at[u], sems.at[u, i, 0]), half(BLK, 0)]
+            return [pltpu.make_async_copy(rows(0, LAST), part(ZVALUES, LAST), sems.at[u, 2])]
+        return [
+            pltpu.make_async_copy(rows(0, BLK), kbuf.at[u], sems.at[u, 0]),
+            pltpu.make_async_copy(rows(BLK, ZVALUES), part(0, ZVALUES), sems.at[u, 1]),
+        ]
+
+    def start(u, i, arrays, array, first, step):
+        for low in range(0, len(arrays), step):
+
+            @pl.when((array >= low) & (array < low + step))
+            def _():
+                for a in range(low, min(low + step, len(arrays))):
+
+                    @pl.when(array == a)
+                    def _():
+                        for copy in copies(u, i, arrays[a], first):
+                            copy.start()
 
     for u in range(n):
-        for i, arrays in enumerate((za, ya)):
-            array, slot = place_ref[2 * i * n + u], place_ref[(2 * i + 1) * n + u]
-            for low, high in ((0, 4), (4, 9)):
-
-                @pl.when((array >= low) & (array < high))
-                def _():
-                    for a in range(low, high):
-
-                        @pl.when(array == a)
-                        def _():
-                            for copy in copies(u, i, arrays[a].at[slot]):
-                                copy.start()
+        j = route_ref[u]
+        by, dz = j >> 3, (j - z) & (NZ - 1)
+        dy = (by - y) & (NY - 1)
+        code = table_ref[dy * NZ + dz]
+        start(u, 0, named, code & 31, (code >> 5) * 16, 5)
+        slot = jnp.where(dy == 0, 0, jnp.where(dy == 3, 1, jnp.where(dy == 1, 2, 3)))
+        late = (dz == 4) & (slot >= 2)
+        start(u, 1, ya, jnp.where(late, NZ, dz), jnp.where(late, slot - 2, slot) * SLOT, 3)
 
     for u in range(n + 1):
         vbuf[u, :, HD:] = jnp.ones((BLK, HD), jnp.bfloat16)
@@ -113,8 +134,8 @@
         cols = slice(h * HD, (h + 1) * HD)
         for s in range(SLOTS):
             u = h * SLOTS + s
-            for i, arrays in enumerate((za, ya)):
-                for copy in copies(u, i, arrays[0].at[0]):
+            for i, arrays in enumerate((named, ya)):
+                for copy in copies(u, i, arrays[0], 0):
                     copy.wait()
         for t in range(BLK // TILE):
             rows = slice(t * TILE, (t + 1) * TILE)
@@ -129,13 +150,13 @@
                 u = h * SLOTS + s
                 sc = scores_of(q, kbuf[u])
                 top = jnp.max(sc, axis=1, keepdims=True) * SCALE
-                m = jnp.maximum(m, jnp.where(place_ref[4 * n + u] == 1, top, -1e30))
+                m = jnp.maximum(m, jnp.where(route_ref[u] < me, top, -1e30))
                 scores.append(sc)
             e = jnp.exp2(own * SCALE - m).astype(jnp.bfloat16)
             both = jnp.dot(e, vbuf[n, :seen], preferred_element_type=jnp.float32)
             for s in range(SLOTS):
                 u = h * SLOTS + s
-                e = jnp.exp2(scores[s] * SCALE - jnp.where(place_ref[4 * n + u] == 1, m, 1e30)).astype(jnp.bfloat16)
+                e = jnp.exp2(scores[s] * SCALE - jnp.where(route_ref[u] < me, m, 1e30)).astype(jnp.bfloat16)
                 both = both + jnp.dot(e, vbuf[u], preferred_element_type=jnp.float32)
             out_ref[rows, cols] = (both[:, :HD] / both[:, HD:]).astype(out_ref.dtype)
 
@@ -149,7 +170,8 @@
             col = (at_ref[0] + dz) & (NZ - 1)
 
             def copy(array, at):
-                pltpu.make_async_copy(array.at[at, pl.ds(HALF, BLK)], dest.at[col], sems.at[i]).start()
+                rows = pl.ds(pl.multiple_of(at * SLOT + LAST, 16), BLK)
+                pltpu.make_async_copy(array.at[rows], dest.at[col], sems.at[i]).start()
 
             if dz == 4:
                 pl.when(slot < 2)(lambda: copy(arrays[4], slot))
@@ -199,16 +221,20 @@
     )(*scalars, *near, *far)
 
 
-def attention(places, q, k, v, za, ya):
+def attention(route, place, q, k, v, named, ya):
     n = HEADS * SLOTS
+    table = [0] * (NY * NZ)
+    for (dy, dz), (name, first) in places().items():
+        table[dy * NZ + dz] = ARRAYS.index(name) + first // 16 * 32
     scratch = [
         pltpu.VMEM((n, BLK, HD), jnp.bfloat16),
         pltpu.VMEM((n + 1, BLK, 2 * HD), jnp.bfloat16),
-        pltpu.SemaphoreType.DMA((n, 2, 2)),
+        pltpu.SemaphoreType.DMA((n, 3)),
     ]
     out = jax.ShapeDtypeStruct((BLK, HEADS * HD), jnp.bfloat16)
     flops, exps = 6 * (n + HEADS) * BLK * BLK * HD, (n + HEADS) * BLK * BLK
-    return call(attend_kernel, out, (places,), (q, k, v), (*za, *ya), scratch, flops, exps, 56)
+    scalars = (route, place, jnp.asarray(table, jnp.int32))
+    return call(attend_kernel, out, scalars, (q, k, v), (*named, *ya), scratch, flops, exps, 56)
 
 
 def project_own(at, a, w):
@@ -234,13 +260,15 @@
     turn = [
         (at(y, z, x, c), at(x, z, y, c)) for y in range(NY) for z in range(NZ) for x in range(NX) for c in range(NC)
     ]
-    route = lax.dynamic_index_in_dim(routing, y * NZ + z, 0, keepdims=False)
-    places = block_places(route.reshape(-1), y, z)
-    zc, yc = join(keys, values[:HALF]), values[HALF:]
-    rows_of = lambda x: jnp.asarray([0, 2, 3, 1], jnp.int32)[(x - y) % NX]
+    route = lax.dynamic_index_in_dim(routing, y * NZ + z, 0, keepdims=False).reshape(-1)
+
+    def rows_of(x):
+        d = (x - y) % NX
+        return jnp.where(d == 0, 0, jnp.where(d == 3, 1, jnp.where(d == 1, 2, 3)))
+
     at = jnp.stack([z] + [rows_of(x + d) for d in (0, -1, 1, 2)])
-    za, ya, (places, at) = gather(zc, yc, w_out, turn, (places, at))
-    attn = attention(places, queries, keys, values, za, ya)
+    named, ya, (route, at) = gather(join(keys, values), w_out, turn, (route, at))
+    attn = attention(route, jnp.stack([y, z]), queries, keys, values, named, ya)
     x1p, x1m = xp(attn), xm(attn)
     (x1p, x1m), (total, near, far) = gate((x1p, x1m), project_own(at, attn, ya))
     x2p, x2m = xp(x1p[:HALF]), xm(x1m[HALF:])

time: 153 us -> 151 us (0.987)
  starting transfers between devices: 68.2 us -> 61 us
  waiting for transfers between devices: 52.1 us -> 57.7 us
    ppermute x32 -> x29, starting transfers between devices: 66.7 us -> 59.4 us  [shift(): return lax.ppermute(v, axis, [(i, (i + d) % n) for i in range(n)])]
    ppermute x32 -> x29, waiting for transfers between devices: 52 us -> 57.7 us  [shift(): return lax.ppermute(v, axis, [(i, (i + d) % n) for i in range(n)])]
    unnamed x46 -> x65, local copies, waits for them, and re-layouts: 4.71 us -> 7.8 us
    another operation x1, local copies, waits for them, and re-layouts: 3.06 us -> 0.63 us  [body(): at = jnp.stack([z] + [rows_of(x + d) for d in (0, -1, 1, 2)])]
  transfers between devices with their start and end apart: 33 -> 30, of which waited for: 9 -> 14; matrix products, arithmetic and copies ran while one was open for 3% -> 2% of each run, Pallas kernels for 5% -> 5%
where the time goes in v2:
time: 151 us
  starting transfers between devices  61 us (40%)
  waiting for transfers between devices  57.7 us (38%)
  Pallas kernels  19.3 us (13%)
  local copies, waits for them, and re-layouts  10.6 us (7%)
  other arithmetic  1.85 us (1%)
    ppermute x29, starting transfers between devices, shift(): return lax.ppermute(v, axis, [(i, (i + d) % n) for i in range(n)])  59.4 us
    ppermute x29, waiting for transfers between devices, shift(): return lax.ppermute(v, axis, [(i, (i + d) % n) for i in range(n)])  57.7 us
    pallas_call x5, Pallas kernels, call(): pl.pallas_call(kernel, out_shape=out_shape, in_specs=spec(pltpu.SMEM, sca...  19.3 us
    unnamed x65, local copies, waits for them, and re-layouts  7.8 us
  transfers between devices with their start and end apart: 30, of which 14 were waited for; matrix products, arithmetic and copies ran while one was open for 2% of the time, Pallas kernels for 5%

profile of v2, /device:TPU:1, one launch (start us, length us, event | category | flops | bytes accessed | tf_op | source)
XLA Modules:
  0.0 151.1 jit_solution(8132760564153906185)
XLA Ops:
  1.9 2.5 %collective-permute-start = (bf16[1024,128]{1,0:T(8,128)(2,1)S(1)}, bf16[1024,128]{1,0:T(8,128)(2,1)S(1)}, u32[]{:S(2)}, u32[]{:S(2)}) collective-permute-start(bf16[1024,128]{1,0:T(8,128)(2,1)S(1)} %constant_dynamic-update-slice_fusion.rest_0_), channel_id=1, source_target_pairs={{0,8},{8,16},{16,24},{24,32},{32,40},{40,48},{48,56},{56,0},{1,9},... | collective-permute-start | bytes 786440 | tf_op jit(solution)/shard_map/ppermute | solution.py:26
  4.4 4.0 %collective-permute-start.1 = (bf16[1024,128]{1,0:T(8,128)(2,1)S(1)}, bf16[1024,128]{1,0:T(8,128)(2,1)S(1)}, u32[]{:S(2)}, u32[]{:S(2)}) collective-permute-start(bf16[1024,128]{1,0:T(8,128)(2,1)S(1)} %constant_dynamic-update-slice_fusion.rest_0_), channel_id=1, source_target_pairs={{0,56},{8,0},{16,8},{24,16},{32,24},{40,32},{48,40},{56,48},{1,57}... | collective-permute-start | bytes 786440 | tf_op jit(solution)/shard_map/ppermute | solution.py:26
  8.4 1.3 collective-permute-start.2
  9.7 1.4 collective-permute-start.3
  11.2 1.6 %collective-permute-start.4 = (bf16[512,128]{1,0:T(8,128)(2,1)}, bf16[512,128]{1,0:T(8,128)(2,1)S(1)}, u32[]{:S(2)}, u32[]{:S(2)}) collective-permute-start(bf16[512,128]{1,0:T(8,128)(2,1)} %param.10), channel_id=1, source_target_pairs={{0,0},{1,1},{2,64},{3,65},{4,128},{5,129},{6,192},{7,193},{8,8},{9... | collective-permute-start | bytes 393224 | tf_op jit(solution)/shard_map/ppermute | solution.py:64
  15.0 1.6 %collective-permute-done.2.rest_8_ = bf16[1024,128]{1,0:T(8,128)(2,1)S(1)} collective-permute-done((bf16[1024,128]{1,0:T(8,128)(2,1)S(1)}, bf16[1024,128]{1,0:T(8,128)(2,1)S(1)}, u32[]{:S(2)}, u32[]{:S(2)}) %collective-permute-start.2) | collective-permute-done | bytes 262176 | tf_op jit(solution)/shard_map/ppermute | solution.py:26
  16.8 2.7 %collective-permute-start.9 = (bf16[1024,128]{1,0:T(8,128)(2,1)S(1)}, bf16[1024,128]{1,0:T(8,128)(2,1)S(1)}, u32[]{:S(2)}, u32[]{:S(2)}) collective-permute-start(bf16[1024,128]{1,0:T(8,128)(2,1)S(1)} %collective-permute-done.1.rest_1_), channel_id=1, source_target_pairs={{0,56},{8,0},{16,8},{24,16},{32,24},{40,32},{48,40},{56,48},{1,57}... | collective-permute-start | bytes 786440 | tf_op jit(solution)/shard_map/ppermute | solution.py:26
  19.4 6.4 %collective-permute-start.7 = (bf16[512,128]{1,0:T(8,128)(2,1)S(1)}, bf16[512,128]{1,0:T(8,128)(2,1)S(1)}, u32[]{:S(2)}, u32[]{:S(2)}) collective-permute-start(bf16[512,128]{1,0:T(8,128)(2,1)S(1)} %collective-permute-done.4), channel_id=1, source_target_pairs={{0,128},{64,192},{128,0},{192,64},{1,129},{65,193},{129,1},{193,65... | collective-permute-start | bytes 393224 | tf_op jit(solution)/shard_map/ppermute | solution.py:26
  26.0 3.4 %collective-permute-start.5 = (bf16[576,128]{1,0:T(8,128)(2,1)S(1)}, bf16[576,128]{1,0:T(8,128)(2,1)S(1)}, u32[]{:S(2)}, u32[]{:S(2)}) collective-permute-start(bf16[576,128]{1,0:T(8,128)(2,1)S(1)} %get-tuple-element.76), channel_id=1, source_target_pairs={{0,64},{64,128},{128,192},{192,0},{1,65},{65,129},{129,193},{193,1... | collective-permute-start | bytes 442376 | tf_op jit(solution)/shard_map/ppermute | solution.py:26
  29.4 3.6 %collective-permute-done.5 = bf16[576,128]{1,0:T(8,128)(2,1)S(1)} collective-permute-done((bf16[576,128]{1,0:T(8,128)(2,1)S(1)}, bf16[576,128]{1,0:T(8,128)(2,1)S(1)}, u32[]{:S(2)}, u32[]{:S(2)}) %collective-permute-start.5) | collective-permute-done | bytes 147488 | tf_op jit(solution)/shard_map/ppermute | solution.py:26
  33.0 1.9 %collective-permute-done.6 = bf16[576,128]{1,0:T(8,128)(2,1)S(1)} collective-permute-done((bf16[576,128]{1,0:T(8,128)(2,1)S(1)}, bf16[576,128]{1,0:T(8,128)(2,1)S(1)}, u32[]{:S(2)}, u32[]{:S(2)}) %collective-permute-start.6) | collective-permute-done | bytes 147488 | tf_op jit(solution)/shard_map/ppermute | solution.py:26
  36.5 2.1 %collective-permute-start.13 = (bf16[3584,128]{1,0:T(8,128)(2,1)S(1)}, bf16[3584,128]{1,0:T(8,128)(2,1)S(1)}, u32[]{:S(2)}, u32[]{:S(2)}) collective-permute-start(bf16[3584,128]{1,0:T(8,128)(2,1)S(1)} %pad_maximum_fusion), channel_id=1, source_target_pairs={{0,192},{64,0},{128,64},{192,128},{1,193},{65,1},{129,65},{193,129... | collective-permute-start | bytes 2752520 | tf_op jit(solution)/shard_map/ppermute | solution.py:26
  38.6 1.5 collective-permute-start.10
  40.0 17.0 %collective-permute-done.11.rest_5_.rest_18_.rest_1_ = bf16[3456,128]{1,0:T(8,128)(2,1)S(1)} collective-permute-done((bf16[3456,128]{1,0:T(8,128)(2,1)S(1)}, bf16[3456,128]{1,0:T(8,128)(2,1)S(1)}, u32[]{:S(2)}, u32[]{:S(2)}) %collective-permute-start.11) | collective-permute-done | bytes 884768 | tf_op jit(solution)/shard_map/ppermute | solution.py:26
  58.3 2.7 %collective-permute-start.15 = (bf16[3456,128]{1,0:T(8,128)(2,1)S(1)}, bf16[3456,128]{1,0:T(8,128)(2,1)S(1)}, u32[]{:S(2)}, u32[]{:S(2)}) collective-permute-start(bf16[3456,128]{1,0:T(8,128)(2,1)S(1)} %collective-permute-done.11.rest_5_.rest_18_.rest_1_), channel_id=1, source_target_pairs={{0,56},{8,0},{16,8},{24,16},{32,24},{40,32},{48,40},{56,48},{1,57}... | collective-permute-start | bytes 2654216 | tf_op jit(solution)/shard_map/ppermute | solution.py:26
  61.3 2.7 %collective-permute-start.17 = (bf16[2688,128]{1,0:T(8,128)(2,1)S(1)}, bf16[2688,128]{1,0:T(8,128)(2,1)S(1)}, u32[]{:S(2)}, u32[]{:S(2)}) collective-permute-start(bf16[2688,128]{1,0:T(8,128)(2,1)S(1)} %pad_maximum_fusion.4), channel_id=1, source_target_pairs={{0,192},{64,0},{128,64},{192,128},{1,193},{65,1},{129,65},{193,129... | collective-permute-start | bytes 2064392 | tf_op jit(solution)/shard_map/ppermute | solution.py:26
  64.1 10.0 %collective-permute-done.17.rest_13_ = bf16[2688,128]{1,0:T(8,128)(2,1)S(1)} collective-permute-done((bf16[2688,128]{1,0:T(8,128)(2,1)S(1)}, bf16[2688,128]{1,0:T(8,128)(2,1)S(1)}, u32[]{:S(2)}, u32[]{:S(2)}) %collective-permute-start.17) | collective-permute-done | bytes 688160 | tf_op jit(solution)/shard_map/ppermute | solution.py:26
  74.0 2.5 %collective-permute-done.14.rest_7_.rest_23_.rest_6_ = bf16[3456,128]{1,0:T(8,128)(2,1)S(1)} collective-permute-done((bf16[3456,128]{1,0:T(8,128)(2,1)S(1)}, bf16[3456,128]{1,0:T(8,128)(2,1)S(1)}, u32[]{:S(2)}, u32[]{:S(2)}) %collective-permute-start.14) | collective-permute-done | bytes 884768 | tf_op jit(solution)/shard_map/ppermute | solution.py:26
  76.5 3.3 %collective-permute-done.16.rest_12_ = bf16[3584,128]{1,0:T(8,128)(2,1)S(1)} collective-permute-done((bf16[3584,128]{1,0:T(8,128)(2,1)S(1)}, bf16[3584,128]{1,0:T(8,128)(2,1)S(1)}, u32[]{:S(2)}, u32[]{:S(2)}) %collective-permute-start.16) | collective-permute-done | bytes 917536 | tf_op jit(solution)/shard_map/ppermute | solution.py:26
  80.8 2.7 %collective-permute-start.21 = (bf16[2688,128]{1,0:T(8,128)(2,1)S(1)}, bf16[2688,128]{1,0:T(8,128)(2,1)S(1)}, u32[]{:S(2)}, u32[]{:S(2)}) collective-permute-start(bf16[2688,128]{1,0:T(8,128)(2,1)S(1)} %get-tuple-element.73), channel_id=1, source_target_pairs={{0,192},{64,0},{128,64},{192,128},{1,193},{65,1},{129,65},{193,129... | collective-permute-start | bytes 2064392 | tf_op jit(solution)/shard_map/ppermute | solution.py:26
  83.7 2.7 %collective-permute-start.19 = (bf16[2560,128]{1,0:T(8,128)(2,1)S(1)}, bf16[2560,128]{1,0:T(8,128)(2,1)S(1)}, u32[]{:S(2)}, u32[]{:S(2)}) collective-permute-start(bf16[2560,128]{1,0:T(8,128)(2,1)S(1)} %slice.107), channel_id=1, source_target_pairs={{0,56},{8,0},{16,8},{24,16},{32,24},{40,32},{48,40},{56,48},{1,57}... | collective-permute-start | bytes 1966088 | tf_op jit(solution)/shard_map/ppermute | solution.py:26
  86.4 8.7 %collective-permute-done.18.rest_22_.rest_5_ = bf16[2560,128]{1,0:T(8,128)(2,1)S(1)} collective-permute-done((bf16[2560,128]{1,0:T(8,128)(2,1)S(1)}, bf16[2560,128]{1,0:T(8,128)(2,1)S(1)}, u32[]{:S(2)}, u32[]{:S(2)}) %collective-permute-start.18) | collective-permute-done | bytes 655392 | tf_op jit(solution)/shard_map/ppermute | solution.py:26
  95.3 2.7 %collective-permute-start.24 = (bf16[1280,128]{1,0:T(8,128)(2,1)S(1)}, bf16[1280,128]{1,0:T(8,128)(2,1)S(1)}, u32[]{:S(2)}, u32[]{:S(2)}) collective-permute-start(bf16[1280,128]{1,0:T(8,128)(2,1)S(1)} %slice.115), channel_id=1, source_target_pairs={{0,56},{8,0},{16,8},{24,16},{32,24},{40,32},{48,40},{56,48},{1,57}... | collective-permute-start | bytes 983048 | tf_op jit(solution)/shard_map/ppermute | solution.py:26
  98.9 5.5 %collective-permute-done.22.rest_16_ = bf16[896,128]{1,0:T(8,128)(2,1)S(1)} collective-permute-done((bf16[896,128]{1,0:T(8,128)(2,1)S(1)}, bf16[896,128]{1,0:T(8,128)(2,1)S(1)}, u32[]{:S(2)}, u32[]{:S(2)}) %collective-permute-start.22) | collective-permute-done | bytes 229408 | tf_op jit(solution)/shard_map/ppermute | solution.py:26
  106.2 11.5 %shard_map.64.a_ref = bf16[512,512]{1,0:T(8,128)(2,1)} custom-call(s32[12]{0:T(128)} %reshape.4.route_ref, s32[2]{0:T(128)} %pad_add_fusion.place_ref, s32[32]{0:T(128)} %constant.58.clone.table_ref, bf16[512,512]{1,0:T(8,128)(2,1)} %q_ref.1, bf16[512,128]{1,0:T(8,128)(2,1)} %k_ref.1, bf16[512,128]{1,0:T(8,128)(2,1)} %v_ref.1, bf16[1024,128]{1,0:T(8,128)(2,1)} %copy-done.24, ...), custom_call_target="tpu_custom_call" | custom-call | flops 3221225472 | bytes 8388608 | tf_op jit(solution)/shard_map/pallas_call | solution.py:213
  117.9 2.7 %collective-permute-start.26 = (bf16[512,512]{1,0:T(8,128)(2,1)}, bf16[512,512]{1,0:T(8,128)(2,1)S(1)}, u32[]{:S(2)}, u32[]{:S(2)}) collective-permute-start(bf16[512,512]{1,0:T(8,128)(2,1)} %shard_map.64.a_ref), channel_id=1, source_target_pairs={{0,6},{2,0},{4,2},{6,4},{1,7},{3,1},{5,3},{7,5},{8,14},{10,8},{12,... | collective-permute-start | bytes 1572872 | tf_op jit(solution)/shard_map/ppermute | solution.py:26
  120.5 5.7 %shard_map.65 = (f32[512,1024]{1,0:T(8,128)}, bf16[2,8,512,128]{3,2,1,0:T(8,128)(2,1)}, bf16[8,512,128]{2,1,0:T(8,128)(2,1)}) custom-call(s32[5]{0:T(128)} %stack.30.at_ref, bf16[512,512]{1,0:T(8,128)(2,1)} %shard_map.64.a_ref, bf16[3456,128]{1,0:T(8,128)(2,1)} %copy-done.7, bf16[3456,128]{1,0:T(8,128)(2,1)} %copy-done.5, bf16[3456,128]{1,0:T(8,128)(2,1)} %copy-done.8, ...), custom_call_target="tpu_custom_call" | custom-call | flops 536870912 | bytes 8388608 | tf_op jit(solution)/shard_map/pallas_call | solution.py:213
  127.8 2.4 %collective-permute-start.28 = (bf16[256,512]{1,0:T(8,128)(2,1)S(1)}, bf16[256,512]{1,0:T(8,128)(2,1)S(1)}, u32[]{:S(2)}, u32[]{:S(2)}) collective-permute-start(bf16[256,512]{1,0:T(8,128)(2,1)S(1)} %slice.117), channel_id=1, source_target_pairs={{0,6},{2,0},{4,2},{6,4},{1,7},{3,1},{5,3},{7,5},{8,14},{10,8},{12,... | collective-permute-start | bytes 786440 | tf_op jit(solution)/shard_map/ppermute | solution.py:26
  130.2 1.6 %copy-done.2 = f32[512,1024]{1,0:T(8,128)S(1)} copy-done((f32[512,1024]{1,0:T(8,128)S(1)}, f32[512,1024]{1,0:T(8,128)}, u32[]{:S(2)}) %copy-start.2) | copy-done | bytes 2097176
  131.8 1.6 %copy-done.3 = bf16[2,8,512,128]{3,2,1,0:T(8,128)(2,1)S(1)} copy-done((bf16[2,8,512,128]{3,2,1,0:T(8,128)(2,1)S(1)}, bf16[2,8,512,128]{3,2,1,0:T(8,128)(2,1)}, u32[]{:S(2)}) %copy-start.3) | copy-done | bytes 2097176
  133.4 1.2 shard_map.66.total_ref
  135.3 13.3 %collective-permute-start.29 = (bf16[512,512]{1,0:T(8,128)(2,1)S(1)}, bf16[512,512]{1,0:T(8,128)(2,1)S(1)}, u32[]{:S(2)}, u32[]{:S(2)}) collective-permute-start(bf16[512,512]{1,0:T(8,128)(2,1)S(1)} %shard_map.68), channel_id=1, source_target_pairs={{0,1},{1,0},{2,3},{3,2},{4,5},{5,4},{6,7},{7,6},{8,9},{9,8},{10,11... | collective-permute-start | bytes 1572872 | tf_op jit(solution)/shard_map/ppermute | solution.py:26
  (134 shorter events, 16.1 us)
Async XLA Ops:
  1.9 33.2 %copy-start.24 = (bf16[1024,128]{1,0:T(8,128)(2,1)}, bf16[1024,128]{1,0:T(8,128)(2,1)S(1)}, u32[]{:S(2)}) copy-start(bf16[1024,128]{1,0:T(8,128)(2,1)S(1)} %constant_dynamic-update-slice_fusion.rest_0_) | copy-start | bytes 786436
  1.9 13.1 %collective-permute-start = (bf16[1024,128]{1,0:T(8,128)(2,1)S(1)}, bf16[1024,128]{1,0:T(8,128)(2,1)S(1)}, u32[]{:S(2)}, u32[]{:S(2)}) collective-permute-start(bf16[1024,128]{1,0:T(8,128)(2,1)S(1)} %constant_dynamic-update-slice_fusion.rest_0_), channel_id=1, source_target_pairs={{0,8},{8,16},{16,24},{24,32},{32,40},{40,48},{48,56},{56,0},{1,9},... | collective-permute-start | bytes 786440 | tf_op jit(solution)/shard_map/ppermute | solution.py:26
  4.4 10.6 %collective-permute-start.1 = (bf16[1024,128]{1,0:T(8,128)(2,1)S(1)}, bf16[1024,128]{1,0:T(8,128)(2,1)S(1)}, u32[]{:S(2)}, u32[]{:S(2)}) collective-permute-start(bf16[1024,128]{1,0:T(8,128)(2,1)S(1)} %constant_dynamic-update-slice_fusion.rest_0_), channel_id=1, source_target_pairs={{0,56},{8,0},{16,8},{24,16},{32,24},{40,32},{48,40},{56,48},{1,57}... | collective-permute-start | bytes 786440 | tf_op jit(solution)/shard_map/ppermute | solution.py:26
  8.4 8.2 %collective-permute-start.2 = (bf16[1024,128]{1,0:T(8,128)(2,1)S(1)}, bf16[1024,128]{1,0:T(8,128)(2,1)S(1)}, u32[]{:S(2)}, u32[]{:S(2)}) collective-permute-start(bf16[1024,128]{1,0:T(8,128)(2,1)S(1)} %constant_dynamic-update-slice_fusion.rest_0_), channel_id=1, source_target_pairs={{0,64},{64,128},{128,192},{192,0},{1,65},{65,129},{129,193},{193,1... | collective-permute-start | bytes 786440 | tf_op jit(solution)/shard_map/ppermute | solution.py:26
  9.7 6.9 %collective-permute-start.3 = (bf16[1024,128]{1,0:T(8,128)(2,1)S(1)}, bf16[1024,128]{1,0:T(8,128)(2,1)S(1)}, u32[]{:S(2)}, u32[]{:S(2)}) collective-permute-start(bf16[1024,128]{1,0:T(8,128)(2,1)S(1)} %constant_dynamic-update-slice_fusion.rest_0_), channel_id=1, source_target_pairs={{0,192},{64,0},{128,64},{192,128},{1,193},{65,1},{129,65},{193,129... | collective-permute-start | bytes 786440 | tf_op jit(solution)/shard_map/ppermute | solution.py:26
  11.2 3.8 %collective-permute-start.4 = (bf16[512,128]{1,0:T(8,128)(2,1)}, bf16[512,128]{1,0:T(8,128)(2,1)S(1)}, u32[]{:S(2)}, u32[]{:S(2)}) collective-permute-start(bf16[512,128]{1,0:T(8,128)(2,1)} %param.10), channel_id=1, source_target_pairs={{0,0},{1,1},{2,64},{3,65},{4,128},{5,129},{6,192},{7,193},{8,8},{9... | collective-permute-start | bytes 393224 | tf_op jit(solution)/shard_map/ppermute | solution.py:64
  16.7 18.2 %collective-permute-start.8 = (bf16[1024,128]{1,0:T(8,128)(2,1)S(1)}, bf16[1024,128]{1,0:T(8,128)(2,1)S(1)}, u32[]{:S(2)}, u32[]{:S(2)}) collective-permute-start(bf16[1024,128]{1,0:T(8,128)(2,1)S(1)} %collective-permute-done.rest_2_), channel_id=1, source_target_pairs={{0,8},{8,16},{16,24},{24,32},{32,40},{40,48},{48,56},{56,0},{1,9},... | collective-permute-start | bytes 786440 | tf_op jit(solution)/shard_map/ppermute | solution.py:26
  16.8 18.1 %collective-permute-start.9 = (bf16[1024,128]{1,0:T(8,128)(2,1)S(1)}, bf16[1024,128]{1,0:T(8,128)(2,1)S(1)}, u32[]{:S(2)}, u32[]{:S(2)}) collective-permute-start(bf16[1024,128]{1,0:T(8,128)(2,1)S(1)} %collective-permute-done.1.rest_1_), channel_id=1, source_target_pairs={{0,56},{8,0},{16,8},{24,16},{32,24},{40,32},{48,40},{56,48},{1,57}... | collective-permute-start | bytes 786440 | tf_op jit(solution)/shard_map/ppermute | solution.py:26
  19.4 9.9 %collective-permute-start.7 = (bf16[512,128]{1,0:T(8,128)(2,1)S(1)}, bf16[512,128]{1,0:T(8,128)(2,1)S(1)}, u32[]{:S(2)}, u32[]{:S(2)}) collective-permute-start(bf16[512,128]{1,0:T(8,128)(2,1)S(1)} %collective-permute-done.4), channel_id=1, source_target_pairs={{0,128},{64,192},{128,0},{192,64},{1,129},{65,193},{129,1},{193,65... | collective-permute-start | bytes 393224 | tf_op jit(solution)/shard_map/ppermute | solution.py:26
  26.0 7.1 %collective-permute-start.5 = (bf16[576,128]{1,0:T(8,128)(2,1)S(1)}, bf16[576,128]{1,0:T(8,128)(2,1)S(1)}, u32[]{:S(2)}, u32[]{:S(2)}) collective-permute-start(bf16[576,128]{1,0:T(8,128)(2,1)S(1)} %get-tuple-element.76), channel_id=1, source_target_pairs={{0,64},{64,128},{128,192},{192,0},{1,65},{65,129},{129,193},{193,1... | collective-permute-start | bytes 442376 | tf_op jit(solution)/shard_map/ppermute | solution.py:26
  29.3 5.5 %collective-permute-start.6 = (bf16[576,128]{1,0:T(8,128)(2,1)S(1)}, bf16[576,128]{1,0:T(8,128)(2,1)S(1)}, u32[]{:S(2)}, u32[]{:S(2)}) collective-permute-start(bf16[576,128]{1,0:T(8,128)(2,1)S(1)} %get-tuple-element.75), channel_id=1, source_target_pairs={{0,192},{64,0},{128,64},{192,128},{1,193},{65,1},{129,65},{193,129... | collective-permute-start | bytes 442376 | tf_op jit(solution)/shard_map/ppermute | solution.py:26
  35.7 25.3 %copy-start.7 = (bf16[3456,128]{1,0:T(8,128)(2,1)}, bf16[3456,128]{1,0:T(8,128)(2,1)S(1)}, u32[]{:S(2)}) copy-start(bf16[3456,128]{1,0:T(8,128)(2,1)S(1)} %get-tuple-element.72.rest_17_.rest_0_) | copy-start | bytes 2654212
  35.8 22.1 %collective-permute-start.12 = (bf16[3584,128]{1,0:T(8,128)(2,1)S(1)}, bf16[3584,128]{1,0:T(8,128)(2,1)S(1)}, u32[]{:S(2)}, u32[]{:S(2)}) collective-permute-start(bf16[3584,128]{1,0:T(8,128)(2,1)S(1)} %pad_maximum_fusion), channel_id=1, source_target_pairs={{0,64},{64,128},{128,192},{192,0},{1,65},{65,129},{129,193},{193,1... | collective-permute-start | bytes 2752520 | tf_op jit(solution)/shard_map/ppermute | solution.py:26
  36.5 21.5 %collective-permute-start.13 = (bf16[3584,128]{1,0:T(8,128)(2,1)S(1)}, bf16[3584,128]{1,0:T(8,128)(2,1)S(1)}, u32[]{:S(2)}, u32[]{:S(2)}) collective-permute-start(bf16[3584,128]{1,0:T(8,128)(2,1)S(1)} %pad_maximum_fusion), channel_id=1, source_target_pairs={{0,192},{64,0},{128,64},{192,128},{1,193},{65,1},{129,65},{193,129... | collective-permute-start | bytes 2752520 | tf_op jit(solution)/shard_map/ppermute | solution.py:26
  38.6 18.4 %collective-permute-start.11 = (bf16[3456,128]{1,0:T(8,128)(2,1)S(1)}, bf16[3456,128]{1,0:T(8,128)(2,1)S(1)}, u32[]{:S(2)}, u32[]{:S(2)}) collective-permute-start(bf16[3456,128]{1,0:T(8,128)(2,1)S(1)} %get-tuple-element.70), channel_id=1, source_target_pairs={{0,56},{8,0},{16,8},{24,16},{32,24},{40,32},{48,40},{56,48},{1,57}... | collective-permute-start | bytes 2654216 | tf_op jit(solution)/shard_map/ppermute | solution.py:26
  38.6 19.4 %collective-permute-start.10 = (bf16[3456,128]{1,0:T(8,128)(2,1)S(1)}, bf16[3456,128]{1,0:T(8,128)(2,1)S(1)}, u32[]{:S(2)}, u32[]{:S(2)}) collective-permute-start(bf16[3456,128]{1,0:T(8,128)(2,1)S(1)} %get-tuple-element.72.rest_17_.rest_0_), channel_id=1, source_target_pairs={{0,8},{8,16},{16,24},{24,32},{32,40},{40,48},{48,56},{56,0},{1,9},... | collective-permute-start | bytes 2654216 | tf_op jit(solution)/shard_map/ppermute | solution.py:26
  58.0 18.5 %collective-permute-start.14 = (bf16[3456,128]{1,0:T(8,128)(2,1)S(1)}, bf16[3456,128]{1,0:T(8,128)(2,1)S(1)}, u32[]{:S(2)}, u32[]{:S(2)}) collective-permute-start(bf16[3456,128]{1,0:T(8,128)(2,1)S(1)} %collective-permute-done.10.rest_6_.rest_24_.rest_7_), channel_id=1, source_target_pairs={{0,8},{8,16},{16,24},{24,32},{32,40},{40,48},{48,56},{56,0},{1,9},... | collective-permute-start | bytes 2654216 | tf_op jit(solution)/shard_map/ppermute | solution.py:26
  58.3 18.2 %collective-permute-start.15 = (bf16[3456,128]{1,0:T(8,128)(2,1)S(1)}, bf16[3456,128]{1,0:T(8,128)(2,1)S(1)}, u32[]{:S(2)}, u32[]{:S(2)}) collective-permute-start(bf16[3456,128]{1,0:T(8,128)(2,1)S(1)} %collective-permute-done.11.rest_5_.rest_18_.rest_1_), channel_id=1, source_target_pairs={{0,56},{8,0},{16,8},{24,16},{32,24},{40,32},{48,40},{56,48},{1,57}... | collective-permute-start | bytes 2654216 | tf_op jit(solution)/shard_map/ppermute | solution.py:26
  61.2 18.7 %collective-permute-start.16 = (bf16[3584,128]{1,0:T(8,128)(2,1)S(1)}, bf16[3584,128]{1,0:T(8,128)(2,1)S(1)}, u32[]{:S(2)}, u32[]{:S(2)}) collective-permute-start(bf16[3584,128]{1,0:T(8,128)(2,1)S(1)} %pad_maximum_fusion.1), channel_id=1, source_target_pairs={{0,64},{64,128},{128,192},{192,0},{1,65},{65,129},{129,193},{193,1... | collective-permute-start | bytes 2752520 | tf_op jit(solution)/shard_map/ppermute | solution.py:26
  61.3 12.7 %collective-permute-start.17 = (bf16[2688,128]{1,0:T(8,128)(2,1)S(1)}, bf16[2688,128]{1,0:T(8,128)(2,1)S(1)}, u32[]{:S(2)}, u32[]{:S(2)}) collective-permute-start(bf16[2688,128]{1,0:T(8,128)(2,1)S(1)} %pad_maximum_fusion.4), channel_id=1, source_target_pairs={{0,192},{64,0},{128,64},{192,128},{1,193},{65,1},{129,65},{193,129... | collective-permute-start | bytes 2064392 | tf_op jit(solution)/shard_map/ppermute | solution.py:26
  80.8 14.3 %collective-permute-start.20 = (bf16[2688,128]{1,0:T(8,128)(2,1)S(1)}, bf16[2688,128]{1,0:T(8,128)(2,1)S(1)}, u32[]{:S(2)}, u32[]{:S(2)}) collective-permute-start(bf16[2688,128]{1,0:T(8,128)(2,1)S(1)} %get-tuple-element.74), channel_id=1, source_target_pairs={{0,64},{64,128},{128,192},{192,0},{1,65},{65,129},{129,193},{193,1... | collective-permute-start | bytes 2064392 | tf_op jit(solution)/shard_map/ppermute | solution.py:26
  80.8 14.3 %collective-permute-start.21 = (bf16[2688,128]{1,0:T(8,128)(2,1)S(1)}, bf16[2688,128]{1,0:T(8,128)(2,1)S(1)}, u32[]{:S(2)}, u32[]{:S(2)}) collective-permute-start(bf16[2688,128]{1,0:T(8,128)(2,1)S(1)} %get-tuple-element.73), channel_id=1, source_target_pairs={{0,192},{64,0},{128,64},{192,128},{1,193},{65,1},{129,65},{193,129... | collective-permute-start | bytes 2064392 | tf_op jit(solution)/shard_map/ppermute | solution.py:26
  83.5 11.5 %collective-permute-start.18 = (bf16[2560,128]{1,0:T(8,128)(2,1)S(1)}, bf16[2560,128]{1,0:T(8,128)(2,1)S(1)}, u32[]{:S(2)}, u32[]{:S(2)}) collective-permute-start(bf16[2560,128]{1,0:T(8,128)(2,1)S(1)} %slice.106), channel_id=1, source_target_pairs={{0,8},{8,16},{16,24},{24,32},{32,40},{40,48},{48,56},{56,0},{1,9},... | collective-permute-start | bytes 1966088 | tf_op jit(solution)/shard_map/ppermute | solution.py:26
  83.7 11.4 %collective-permute-start.19 = (bf16[2560,128]{1,0:T(8,128)(2,1)S(1)}, bf16[2560,128]{1,0:T(8,128)(2,1)S(1)}, u32[]{:S(2)}, u32[]{:S(2)}) collective-permute-start(bf16[2560,128]{1,0:T(8,128)(2,1)S(1)} %slice.107), channel_id=1, source_target_pairs={{0,56},{8,0},{16,8},{24,16},{32,24},{40,32},{48,40},{56,48},{1,57}... | collective-permute-start | bytes 1966088 | tf_op jit(solution)/shard_map/ppermute | solution.py:26
  95.1 9.6 %collective-permute-start.23 = (bf16[1280,128]{1,0:T(8,128)(2,1)S(1)}, bf16[1280,128]{1,0:T(8,128)(2,1)S(1)}, u32[]{:S(2)}, u32[]{:S(2)}) collective-permute-start(bf16[1280,128]{1,0:T(8,128)(2,1)S(1)} %slice.114), channel_id=1, source_target_pairs={{0,8},{8,16},{16,24},{24,32},{32,40},{40,48},{48,56},{56,0},{1,9},... | collective-permute-start | bytes 983048 | tf_op jit(solution)/shard_map/ppermute | solution.py:26
  95.3 9.5 %collective-permute-start.24 = (bf16[1280,128]{1,0:T(8,128)(2,1)S(1)}, bf16[1280,128]{1,0:T(8,128)(2,1)S(1)}, u32[]{:S(2)}, u32[]{:S(2)}) collective-permute-start(bf16[1280,128]{1,0:T(8,128)(2,1)S(1)} %slice.115), channel_id=1, source_target_pairs={{0,56},{8,0},{16,8},{24,16},{32,24},{40,32},{48,40},{56,48},{1,57}... | collective-permute-start | bytes 983048 | tf_op jit(solution)/shard_map/ppermute | solution.py:26
  98.0 6.4 %collective-permute-start.22 = (bf16[896,128]{1,0:T(8,128)(2,1)S(1)}, bf16[896,128]{1,0:T(8,128)(2,1)S(1)}, u32[]{:S(2)}, u32[]{:S(2)}) collective-permute-start(bf16[896,128]{1,0:T(8,128)(2,1)S(1)} %slice.113), channel_id=1, source_target_pairs={{0,64},{64,128},{128,192},{192,0},{1,65},{65,129},{129,193},{193,1... | collective-permute-start | bytes 688136 | tf_op jit(solution)/shard_map/ppermute | solution.py:26
  117.8 9.5 %collective-permute-start.25 = (bf16[512,512]{1,0:T(8,128)(2,1)}, bf16[512,512]{1,0:T(8,128)(2,1)S(1)}, u32[]{:S(2)}, u32[]{:S(2)}) collective-permute-start(bf16[512,512]{1,0:T(8,128)(2,1)} %shard_map.64.a_ref), channel_id=1, source_target_pairs={{0,2},{2,4},{4,6},{6,0},{1,3},{3,5},{5,7},{7,1},{8,10},{10,12},{12... | collective-permute-start | bytes 1572872 | tf_op jit(solution)/shard_map/ppermute | solution.py:26
  117.9 9.4 %collective-permute-start.26 = (bf16[512,512]{1,0:T(8,128)(2,1)}, bf16[512,512]{1,0:T(8,128)(2,1)S(1)}, u32[]{:S(2)}, u32[]{:S(2)}) collective-permute-start(bf16[512,512]{1,0:T(8,128)(2,1)} %shard_map.64.a_ref), channel_id=1, source_target_pairs={{0,6},{2,0},{4,2},{6,4},{1,7},{3,1},{5,3},{7,5},{8,14},{10,8},{12,... | collective-permute-start | bytes 1572872 | tf_op jit(solution)/shard_map/ppermute | solution.py:26
  127.3 7.5 %collective-permute-start.27 = (bf16[256,512]{1,0:T(8,128)(2,1)S(1)}, bf16[256,512]{1,0:T(8,128)(2,1)S(1)}, u32[]{:S(2)}, u32[]{:S(2)}) collective-permute-start(bf16[256,512]{1,0:T(8,128)(2,1)S(1)} %slice.116), channel_id=1, source_target_pairs={{0,2},{2,4},{4,6},{6,0},{1,3},{3,5},{5,7},{7,1},{8,10},{10,12},{12... | collective-permute-start | bytes 786440 | tf_op jit(solution)/shard_map/ppermute | solution.py:26
  127.8 7.0 %collective-permute-start.28 = (bf16[256,512]{1,0:T(8,128)(2,1)S(1)}, bf16[256,512]{1,0:T(8,128)(2,1)S(1)}, u32[]{:S(2)}, u32[]{:S(2)}) collective-permute-start(bf16[256,512]{1,0:T(8,128)(2,1)S(1)} %slice.117), channel_id=1, source_target_pairs={{0,6},{2,0},{4,2},{6,4},{1,7},{3,1},{5,3},{7,5},{8,14},{10,8},{12,... | collective-permute-start | bytes 786440 | tf_op jit(solution)/shard_map/ppermute | solution.py:26
  135.3 14.9 %collective-permute-start.29 = (bf16[512,512]{1,0:T(8,128)(2,1)S(1)}, bf16[512,512]{1,0:T(8,128)(2,1)S(1)}, u32[]{:S(2)}, u32[]{:S(2)}) collective-permute-start(bf16[512,512]{1,0:T(8,128)(2,1)S(1)} %shard_map.68), channel_id=1, source_target_pairs={{0,1},{1,0},{2,3},{3,2},{4,5},{5,4},{6,7},{7,6},{8,9},{9,8},{10,11... | collective-permute-start | bytes 1572872 | tf_op jit(solution)/shard_map/ppermute | solution.py:26
  (27 other events, 219.7 us)

commit v3 on v2

--- a/solution.py
+++ b/solution.py
@@ -267,7 +267,7 @@
         return jnp.where(d == 0, 0, jnp.where(d == 3, 1, jnp.where(d == 1, 2, 3)))
 
     at = jnp.stack([z] + [rows_of(x + d) for d in (0, -1, 1, 2)])
-    named, ya, (route, at) = gather(join(keys, values), w_out, turn, (route, at))
+    named, ya, (route, at) = gather(jnp.stack([keys, values]).reshape(2 * BLK, HD), w_out, turn, (route, at))
     attn = attention(route, jnp.stack([y, z]), queries, keys, values, named, ya)
     x1p, x1m = xp(attn), xm(attn)
     (x1p, x1m), (total, near, far) = gate((x1p, x1m), project_own(at, attn, ya))

time: 151 us -> 151 us (level)
  local copies, waits for them, and re-layouts: 10.6 us -> 7.99 us
    unnamed x65 -> x64, local copies, waits for them, and re-layouts: 7.8 us -> 6.12 us
  transfers between devices with their start and end apart: 30 -> 30, of which waited for: 14 -> 15; matrix products, arithmetic and copies ran while one was open for 2% -> 2% of each run, Pallas kernels for 5% -> 5%
where the time goes in v3:
time: 151 us; the launch traced here: 150 us
  starting transfers between devices  61 us (40%)
  waiting for transfers between devices  58.5 us (39%)
  Pallas kernels  19.3 us (13%)
  local copies, waits for them, and re-layouts  7.99 us (5%)
  other arithmetic  2.86 us (2%)
    ppermute x29, starting transfers between devices, shift(): return lax.ppermute(v, axis, [(i, (i + d) % n) for i in range(n)])  59.4 us
    ppermute x29, waiting for transfers between devices, shift(): return lax.ppermute(v, axis, [(i, (i + d) % n) for i in range(n)])  58.5 us
    pallas_call x5, Pallas kernels, call(): pl.pallas_call(kernel, out_shape=out_shape, in_specs=spec(pltpu.SMEM, sca...  19.3 us
    unnamed x64, local copies, waits for them, and re-layouts  6.12 us
  transfers between devices with their start and end apart: 30, of which 15 were waited for; matrix products, arithmetic and copies ran while one was open for 2% of the time, Pallas kernels for 5%

profile of v3, /device:TPU:1, one launch (start us, length us, event | category | flops | bytes accessed | tf_op | source)
XLA Modules:
  0.0 150.3 jit_solution(58312633236523271)
XLA Ops:
  1.0 2.5 %collective-permute-start = (bf16[1024,128]{1,0:T(8,128)(2,1)S(1)}, bf16[1024,128]{1,0:T(8,128)(2,1)S(1)}, u32[]{:S(2)}, u32[]{:S(2)}) collective-permute-start(bf16[1024,128]{1,0:T(8,128)(2,1)S(1)} %bitcast.11), channel_id=1, source_target_pairs={{0,8},{8,16},{16,24},{24,32},{32,40},{40,48},{48,56},{56,0},{1,9},... | collective-permute-start | bytes 786440 | tf_op jit(solution)/shard_map/ppermute | solution.py:26
  3.6 4.0 %collective-permute-start.1 = (bf16[1024,128]{1,0:T(8,128)(2,1)S(1)}, bf16[1024,128]{1,0:T(8,128)(2,1)S(1)}, u32[]{:S(2)}, u32[]{:S(2)}) collective-permute-start(bf16[1024,128]{1,0:T(8,128)(2,1)S(1)} %bitcast.12), channel_id=1, source_target_pairs={{0,56},{8,0},{16,8},{24,16},{32,24},{40,32},{48,40},{56,48},{1,57}... | collective-permute-start | bytes 786440 | tf_op jit(solution)/shard_map/ppermute | solution.py:26
  7.6 1.3 collective-permute-start.2
  8.9 1.4 collective-permute-start.3
  10.3 1.6 %collective-permute-start.4 = (bf16[512,128]{1,0:T(8,128)(2,1)}, bf16[512,128]{1,0:T(8,128)(2,1)S(1)}, u32[]{:S(2)}, u32[]{:S(2)}) collective-permute-start(bf16[512,128]{1,0:T(8,128)(2,1)} %param.10), channel_id=1, source_target_pairs={{0,0},{1,1},{2,64},{3,65},{4,128},{5,129},{6,192},{7,193},{8,8},{9... | collective-permute-start | bytes 393224 | tf_op jit(solution)/shard_map/ppermute | solution.py:64
  13.5 2.2 %collective-permute-done.2.rest_8_ = bf16[1024,128]{1,0:T(8,128)(2,1)S(1)} collective-permute-done((bf16[1024,128]{1,0:T(8,128)(2,1)S(1)}, bf16[1024,128]{1,0:T(8,128)(2,1)S(1)}, u32[]{:S(2)}, u32[]{:S(2)}) %collective-permute-start.2) | collective-permute-done | bytes 262176 | tf_op jit(solution)/shard_map/ppermute | solution.py:26
  15.9 2.7 %collective-permute-start.9 = (bf16[1024,128]{1,0:T(8,128)(2,1)S(1)}, bf16[1024,128]{1,0:T(8,128)(2,1)S(1)}, u32[]{:S(2)}, u32[]{:S(2)}) collective-permute-start(bf16[1024,128]{1,0:T(8,128)(2,1)S(1)} %collective-permute-done.1.rest_1_), channel_id=1, source_target_pairs={{0,56},{8,0},{16,8},{24,16},{32,24},{40,32},{48,40},{56,48},{1,57}... | collective-permute-start | bytes 786440 | tf_op jit(solution)/shard_map/ppermute | solution.py:26
  18.6 6.4 %collective-permute-start.7 = (bf16[512,128]{1,0:T(8,128)(2,1)S(1)}, bf16[512,128]{1,0:T(8,128)(2,1)S(1)}, u32[]{:S(2)}, u32[]{:S(2)}) collective-permute-start(bf16[512,128]{1,0:T(8,128)(2,1)S(1)} %collective-permute-done.4), channel_id=1, source_target_pairs={{0,128},{64,192},{128,0},{192,64},{1,129},{65,193},{129,1},{193,65... | collective-permute-start | bytes 393224 | tf_op jit(solution)/shard_map/ppermute | solution.py:26
  25.1 3.4 %collective-permute-start.5 = (bf16[576,128]{1,0:T(8,128)(2,1)S(1)}, bf16[576,128]{1,0:T(8,128)(2,1)S(1)}, u32[]{:S(2)}, u32[]{:S(2)}) collective-permute-start(bf16[576,128]{1,0:T(8,128)(2,1)S(1)} %get-tuple-element.76), channel_id=1, source_target_pairs={{0,64},{64,128},{128,192},{192,0},{1,65},{65,129},{129,193},{193,1... | collective-permute-start | bytes 442376 | tf_op jit(solution)/shard_map/ppermute | solution.py:26
  28.5 3.6 %collective-permute-done.5 = bf16[576,128]{1,0:T(8,128)(2,1)S(1)} collective-permute-done((bf16[576,128]{1,0:T(8,128)(2,1)S(1)}, bf16[576,128]{1,0:T(8,128)(2,1)S(1)}, u32[]{:S(2)}, u32[]{:S(2)}) %collective-permute-start.5) | collective-permute-done | bytes 147488 | tf_op jit(solution)/shard_map/ppermute | solution.py:26
  32.2 1.9 %collective-permute-done.6 = bf16[576,128]{1,0:T(8,128)(2,1)S(1)} collective-permute-done((bf16[576,128]{1,0:T(8,128)(2,1)S(1)}, bf16[576,128]{1,0:T(8,128)(2,1)S(1)}, u32[]{:S(2)}, u32[]{:S(2)}) %collective-permute-start.6) | collective-permute-done | bytes 147488 | tf_op jit(solution)/shard_map/ppermute | solution.py:26
  35.6 2.1 %collective-permute-start.13 = (bf16[3584,128]{1,0:T(8,128)(2,1)S(1)}, bf16[3584,128]{1,0:T(8,128)(2,1)S(1)}, u32[]{:S(2)}, u32[]{:S(2)}) collective-permute-start(bf16[3584,128]{1,0:T(8,128)(2,1)S(1)} %pad_maximum_fusion), channel_id=1, source_target_pairs={{0,192},{64,0},{128,64},{192,128},{1,193},{65,1},{129,65},{193,129... | collective-permute-start | bytes 2752520 | tf_op jit(solution)/shard_map/ppermute | solution.py:26
  37.7 1.5 collective-permute-start.10
  39.2 17.0 %collective-permute-done.11.rest_5_.rest_18_.rest_1_ = bf16[3456,128]{1,0:T(8,128)(2,1)S(1)} collective-permute-done((bf16[3456,128]{1,0:T(8,128)(2,1)S(1)}, bf16[3456,128]{1,0:T(8,128)(2,1)S(1)}, u32[]{:S(2)}, u32[]{:S(2)}) %collective-permute-start.11) | collective-permute-done | bytes 884768 | tf_op jit(solution)/shard_map/ppermute | solution.py:26
  57.5 2.7 %collective-permute-start.15 = (bf16[3456,128]{1,0:T(8,128)(2,1)S(1)}, bf16[3456,128]{1,0:T(8,128)(2,1)S(1)}, u32[]{:S(2)}, u32[]{:S(2)}) collective-permute-start(bf16[3456,128]{1,0:T(8,128)(2,1)S(1)} %collective-permute-done.11.rest_5_.rest_18_.rest_1_), channel_id=1, source_target_pairs={{0,56},{8,0},{16,8},{24,16},{32,24},{40,32},{48,40},{56,48},{1,57}... | collective-permute-start | bytes 2654216 | tf_op jit(solution)/shard_map/ppermute | solution.py:26
  60.5 2.7 %collective-permute-start.17 = (bf16[2688,128]{1,0:T(8,128)(2,1)S(1)}, bf16[2688,128]{1,0:T(8,128)(2,1)S(1)}, u32[]{:S(2)}, u32[]{:S(2)}) collective-permute-start(bf16[2688,128]{1,0:T(8,128)(2,1)S(1)} %pad_maximum_fusion.4), channel_id=1, source_target_pairs={{0,192},{64,0},{128,64},{192,128},{1,193},{65,1},{129,65},{193,129... | collective-permute-start | bytes 2064392 | tf_op jit(solution)/shard_map/ppermute | solution.py:26
  63.2 10.0 %collective-permute-done.17.rest_13_ = bf16[2688,128]{1,0:T(8,128)(2,1)S(1)} collective-permute-done((bf16[2688,128]{1,0:T(8,128)(2,1)S(1)}, bf16[2688,128]{1,0:T(8,128)(2,1)S(1)}, u32[]{:S(2)}, u32[]{:S(2)}) %collective-permute-start.17) | collective-permute-done | bytes 688160 | tf_op jit(solution)/shard_map/ppermute | solution.py:26
  73.2 2.5 %collective-permute-done.14.rest_7_.rest_23_.rest_6_ = bf16[3456,128]{1,0:T(8,128)(2,1)S(1)} collective-permute-done((bf16[3456,128]{1,0:T(8,128)(2,1)S(1)}, bf16[3456,128]{1,0:T(8,128)(2,1)S(1)}, u32[]{:S(2)}, u32[]{:S(2)}) %collective-permute-start.14) | collective-permute-done | bytes 884768 | tf_op jit(solution)/shard_map/ppermute | solution.py:26
  75.7 3.3 %collective-permute-done.16.rest_12_ = bf16[3584,128]{1,0:T(8,128)(2,1)S(1)} collective-permute-done((bf16[3584,128]{1,0:T(8,128)(2,1)S(1)}, bf16[3584,128]{1,0:T(8,128)(2,1)S(1)}, u32[]{:S(2)}, u32[]{:S(2)}) %collective-permute-start.16) | collective-permute-done | bytes 917536 | tf_op jit(solution)/shard_map/ppermute | solution.py:26
  79.9 2.7 %collective-permute-start.21 = (bf16[2688,128]{1,0:T(8,128)(2,1)S(1)}, bf16[2688,128]{1,0:T(8,128)(2,1)S(1)}, u32[]{:S(2)}, u32[]{:S(2)}) collective-permute-start(bf16[2688,128]{1,0:T(8,128)(2,1)S(1)} %get-tuple-element.73), channel_id=1, source_target_pairs={{0,192},{64,0},{128,64},{192,128},{1,193},{65,1},{129,65},{193,129... | collective-permute-start | bytes 2064392 | tf_op jit(solution)/shard_map/ppermute | solution.py:26
  82.8 2.7 %collective-permute-start.19 = (bf16[2560,128]{1,0:T(8,128)(2,1)S(1)}, bf16[2560,128]{1,0:T(8,128)(2,1)S(1)}, u32[]{:S(2)}, u32[]{:S(2)}) collective-permute-start(bf16[2560,128]{1,0:T(8,128)(2,1)S(1)} %slice.107), channel_id=1, source_target_pairs={{0,56},{8,0},{16,8},{24,16},{32,24},{40,32},{48,40},{56,48},{1,57}... | collective-permute-start | bytes 1966088 | tf_op jit(solution)/shard_map/ppermute | solution.py:26
  85.5 8.7 %collective-permute-done.18.rest_22_.rest_5_ = bf16[2560,128]{1,0:T(8,128)(2,1)S(1)} collective-permute-done((bf16[2560,128]{1,0:T(8,128)(2,1)S(1)}, bf16[2560,128]{1,0:T(8,128)(2,1)S(1)}, u32[]{:S(2)}, u32[]{:S(2)}) %collective-permute-start.18) | collective-permute-done | bytes 655392 | tf_op jit(solution)/shard_map/ppermute | solution.py:26
  94.4 2.7 %collective-permute-start.24 = (bf16[1280,128]{1,0:T(8,128)(2,1)S(1)}, bf16[1280,128]{1,0:T(8,128)(2,1)S(1)}, u32[]{:S(2)}, u32[]{:S(2)}) collective-permute-start(bf16[1280,128]{1,0:T(8,128)(2,1)S(1)} %slice.115), channel_id=1, source_target_pairs={{0,56},{8,0},{16,8},{24,16},{32,24},{40,32},{48,40},{56,48},{1,57}... | collective-permute-start | bytes 983048 | tf_op jit(solution)/shard_map/ppermute | solution.py:26
  98.1 5.5 %collective-permute-done.22.rest_16_ = bf16[896,128]{1,0:T(8,128)(2,1)S(1)} collective-permute-done((bf16[896,128]{1,0:T(8,128)(2,1)S(1)}, bf16[896,128]{1,0:T(8,128)(2,1)S(1)}, u32[]{:S(2)}, u32[]{:S(2)}) %collective-permute-start.22) | collective-permute-done | bytes 229408 | tf_op jit(solution)/shard_map/ppermute | solution.py:26
  105.4 11.5 %shard_map.64.a_ref = bf16[512,512]{1,0:T(8,128)(2,1)} custom-call(s32[12]{0:T(128)} %reshape.8.route_ref, s32[2]{0:T(128)} %pad_add_fusion.place_ref, s32[32]{0:T(128)} %constant.58.clone.table_ref, bf16[512,512]{1,0:T(8,128)(2,1)} %q_ref.1, bf16[512,128]{1,0:T(8,128)(2,1)} %k_ref.1, bf16[512,128]{1,0:T(8,128)(2,1)} %v_ref.1, bf16[1024,128]{1,0:T(8,128)(2,1)} %bitcast.16, ...), custom_call_target="tpu_custom_call" | custom-call | flops 3221225472 | bytes 8388608 | tf_op jit(solution)/shard_map/pallas_call | solution.py:213
  117.0 2.7 %collective-permute-start.26 = (bf16[512,512]{1,0:T(8,128)(2,1)}, bf16[512,512]{1,0:T(8,128)(2,1)S(1)}, u32[]{:S(2)}, u32[]{:S(2)}) collective-permute-start(bf16[512,512]{1,0:T(8,128)(2,1)} %shard_map.64.a_ref), channel_id=1, source_target_pairs={{0,6},{2,0},{4,2},{6,4},{1,7},{3,1},{5,3},{7,5},{8,14},{10,8},{12,... | collective-permute-start | bytes 1572872 | tf_op jit(solution)/shard_map/ppermute | solution.py:26
  119.7 5.7 %shard_map.65 = (f32[512,1024]{1,0:T(8,128)}, bf16[2,8,512,128]{3,2,1,0:T(8,128)(2,1)}, bf16[8,512,128]{2,1,0:T(8,128)(2,1)}) custom-call(s32[5]{0:T(128)} %stack.42.at_ref, bf16[512,512]{1,0:T(8,128)(2,1)} %shard_map.64.a_ref, bf16[3456,128]{1,0:T(8,128)(2,1)} %copy-done.7, bf16[3456,128]{1,0:T(8,128)(2,1)} %copy-done.5, bf16[3456,128]{1,0:T(8,128)(2,1)} %copy-done.8, ...), custom_call_target="tpu_custom_call" | custom-call | flops 536870912 | bytes 8388608 | tf_op jit(solution)/shard_map/pallas_call | solution.py:213
  127.0 2.4 %collective-permute-start.28 = (bf16[256,512]{1,0:T(8,128)(2,1)S(1)}, bf16[256,512]{1,0:T(8,128)(2,1)S(1)}, u32[]{:S(2)}, u32[]{:S(2)}) collective-permute-start(bf16[256,512]{1,0:T(8,128)(2,1)S(1)} %slice.117), channel_id=1, source_target_pairs={{0,6},{2,0},{4,2},{6,4},{1,7},{3,1},{5,3},{7,5},{8,14},{10,8},{12,... | collective-permute-start | bytes 786440 | tf_op jit(solution)/shard_map/ppermute | solution.py:26
  129.4 1.6 %copy-done.2 = f32[512,1024]{1,0:T(8,128)S(1)} copy-done((f32[512,1024]{1,0:T(8,128)S(1)}, f32[512,1024]{1,0:T(8,128)}, u32[]{:S(2)}) %copy-start.2) | copy-done | bytes 2097176
  131.0 1.6 %copy-done.3 = bf16[2,8,512,128]{3,2,1,0:T(8,128)(2,1)S(1)} copy-done((bf16[2,8,512,128]{3,2,1,0:T(8,128)(2,1)S(1)}, bf16[2,8,512,128]{3,2,1,0:T(8,128)(2,1)}, u32[]{:S(2)}) %copy-start.3) | copy-done | bytes 2097176
  132.5 1.2 shard_map.66.total_ref
  134.4 13.3 %collective-permute-start.29 = (bf16[512,512]{1,0:T(8,128)(2,1)S(1)}, bf16[512,512]{1,0:T(8,128)(2,1)S(1)}, u32[]{:S(2)}, u32[]{:S(2)}) collective-permute-start(bf16[512,512]{1,0:T(8,128)(2,1)S(1)} %shard_map.68), channel_id=1, source_target_pairs={{0,1},{1,0},{2,3},{3,2},{4,5},{5,4},{6,7},{7,6},{8,9},{9,8},{10,11... | collective-permute-start | bytes 1572872 | tf_op jit(solution)/shard_map/ppermute | solution.py:26
  (133 shorter events, 14.6 us)
Async XLA Ops:
  1.0 33.2 %copy-start.18 = (bf16[2,512,128]{2,1,0:T(8,128)(2,1)}, bf16[2,512,128]{2,1,0:T(8,128)(2,1)S(1)}, u32[]{:S(2)}) copy-start(bf16[2,512,128]{2,1,0:T(8,128)(2,1)S(1)} %pad_maximum_fusion.5) | copy-start | bytes 786436
  1.0 12.5 %collective-permute-start = (bf16[1024,128]{1,0:T(8,128)(2,1)S(1)}, bf16[1024,128]{1,0:T(8,128)(2,1)S(1)}, u32[]{:S(2)}, u32[]{:S(2)}) collective-permute-start(bf16[1024,128]{1,0:T(8,128)(2,1)S(1)} %bitcast.11), channel_id=1, source_target_pairs={{0,8},{8,16},{16,24},{24,32},{32,40},{40,48},{48,56},{56,0},{1,9},... | collective-permute-start | bytes 786440 | tf_op jit(solution)/shard_map/ppermute | solution.py:26
  3.6 10.0 %collective-permute-start.1 = (bf16[1024,128]{1,0:T(8,128)(2,1)S(1)}, bf16[1024,128]{1,0:T(8,128)(2,1)S(1)}, u32[]{:S(2)}, u32[]{:S(2)}) collective-permute-start(bf16[1024,128]{1,0:T(8,128)(2,1)S(1)} %bitcast.12), channel_id=1, source_target_pairs={{0,56},{8,0},{16,8},{24,16},{32,24},{40,32},{48,40},{56,48},{1,57}... | collective-permute-start | bytes 786440 | tf_op jit(solution)/shard_map/ppermute | solution.py:26
  7.6 8.2 %collective-permute-start.2 = (bf16[1024,128]{1,0:T(8,128)(2,1)S(1)}, bf16[1024,128]{1,0:T(8,128)(2,1)S(1)}, u32[]{:S(2)}, u32[]{:S(2)}) collective-permute-start(bf16[1024,128]{1,0:T(8,128)(2,1)S(1)} %bitcast.13), channel_id=1, source_target_pairs={{0,64},{64,128},{128,192},{192,0},{1,65},{65,129},{129,193},{193,1... | collective-permute-start | bytes 786440 | tf_op jit(solution)/shard_map/ppermute | solution.py:26
  8.9 6.9 %collective-permute-start.3 = (bf16[1024,128]{1,0:T(8,128)(2,1)S(1)}, bf16[1024,128]{1,0:T(8,128)(2,1)S(1)}, u32[]{:S(2)}, u32[]{:S(2)}) collective-permute-start(bf16[1024,128]{1,0:T(8,128)(2,1)S(1)} %bitcast.14), channel_id=1, source_target_pairs={{0,192},{64,0},{128,64},{192,128},{1,193},{65,1},{129,65},{193,129... | collective-permute-start | bytes 786440 | tf_op jit(solution)/shard_map/ppermute | solution.py:26
  10.3 3.0 %collective-permute-start.4 = (bf16[512,128]{1,0:T(8,128)(2,1)}, bf16[512,128]{1,0:T(8,128)(2,1)S(1)}, u32[]{:S(2)}, u32[]{:S(2)}) collective-permute-start(bf16[512,128]{1,0:T(8,128)(2,1)} %param.10), channel_id=1, source_target_pairs={{0,0},{1,1},{2,64},{3,65},{4,128},{5,129},{6,192},{7,193},{8,8},{9... | collective-permute-start | bytes 393224 | tf_op jit(solution)/shard_map/ppermute | solution.py:64
  15.8 18.2 %collective-permute-start.8 = (bf16[1024,128]{1,0:T(8,128)(2,1)S(1)}, bf16[1024,128]{1,0:T(8,128)(2,1)S(1)}, u32[]{:S(2)}, u32[]{:S(2)}) collective-permute-start(bf16[1024,128]{1,0:T(8,128)(2,1)S(1)} %collective-permute-done.rest_2_), channel_id=1, source_target_pairs={{0,8},{8,16},{16,24},{24,32},{32,40},{40,48},{48,56},{56,0},{1,9},... | collective-permute-start | bytes 786440 | tf_op jit(solution)/shard_map/ppermute | solution.py:26
  15.9 18.1 %collective-permute-start.9 = (bf16[1024,128]{1,0:T(8,128)(2,1)S(1)}, bf16[1024,128]{1,0:T(8,128)(2,1)S(1)}, u32[]{:S(2)}, u32[]{:S(2)}) collective-permute-start(bf16[1024,128]{1,0:T(8,128)(2,1)S(1)} %collective-permute-done.1.rest_1_), channel_id=1, source_target_pairs={{0,56},{8,0},{16,8},{24,16},{32,24},{40,32},{48,40},{56,48},{1,57}... | collective-permute-start | bytes 786440 | tf_op jit(solution)/shard_map/ppermute | solution.py:26
  18.6 9.9 %collective-permute-start.7 = (bf16[512,128]{1,0:T(8,128)(2,1)S(1)}, bf16[512,128]{1,0:T(8,128)(2,1)S(1)}, u32[]{:S(2)}, u32[]{:S(2)}) collective-permute-start(bf16[512,128]{1,0:T(8,128)(2,1)S(1)} %collective-permute-done.4), channel_id=1, source_target_pairs={{0,128},{64,192},{128,0},{192,64},{1,129},{65,193},{129,1},{193,65... | collective-permute-start | bytes 393224 | tf_op jit(solution)/shard_map/ppermute | solution.py:26
  25.1 7.1 %collective-permute-start.5 = (bf16[576,128]{1,0:T(8,128)(2,1)S(1)}, bf16[576,128]{1,0:T(8,128)(2,1)S(1)}, u32[]{:S(2)}, u32[]{:S(2)}) collective-permute-start(bf16[576,128]{1,0:T(8,128)(2,1)S(1)} %get-tuple-element.76), channel_id=1, source_target_pairs={{0,64},{64,128},{128,192},{192,0},{1,65},{65,129},{129,193},{193,1... | collective-permute-start | bytes 442376 | tf_op jit(solution)/shard_map/ppermute | solution.py:26
  28.5 5.5 %collective-permute-start.6 = (bf16[576,128]{1,0:T(8,128)(2,1)S(1)}, bf16[576,128]{1,0:T(8,128)(2,1)S(1)}, u32[]{:S(2)}, u32[]{:S(2)}) collective-permute-start(bf16[576,128]{1,0:T(8,128)(2,1)S(1)} %get-tuple-element.75), channel_id=1, source_target_pairs={{0,192},{64,0},{128,64},{192,128},{1,193},{65,1},{129,65},{193,129... | collective-permute-start | bytes 442376 | tf_op jit(solution)/shard_map/ppermute | solution.py:26
  34.9 25.3 %copy-start.7 = (bf16[3456,128]{1,0:T(8,128)(2,1)}, bf16[3456,128]{1,0:T(8,128)(2,1)S(1)}, u32[]{:S(2)}) copy-start(bf16[3456,128]{1,0:T(8,128)(2,1)S(1)} %get-tuple-element.72.rest_17_.rest_0_) | copy-start | bytes 2654212
  35.0 22.1 %collective-permute-start.12 = (bf16[3584,128]{1,0:T(8,128)(2,1)S(1)}, bf16[3584,128]{1,0:T(8,128)(2,1)S(1)}, u32[]{:S(2)}, u32[]{:S(2)}) collective-permute-start(bf16[3584,128]{1,0:T(8,128)(2,1)S(1)} %pad_maximum_fusion), channel_id=1, source_target_pairs={{0,64},{64,128},{128,192},{192,0},{1,65},{65,129},{129,193},{193,1... | collective-permute-start | bytes 2752520 | tf_op jit(solution)/shard_map/ppermute | solution.py:26
  35.6 21.5 %collective-permute-start.13 = (bf16[3584,128]{1,0:T(8,128)(2,1)S(1)}, bf16[3584,128]{1,0:T(8,128)(2,1)S(1)}, u32[]{:S(2)}, u32[]{:S(2)}) collective-permute-start(bf16[3584,128]{1,0:T(8,128)(2,1)S(1)} %pad_maximum_fusion), channel_id=1, source_target_pairs={{0,192},{64,0},{128,64},{192,128},{1,193},{65,1},{129,65},{193,129... | collective-permute-start | bytes 2752520 | tf_op jit(solution)/shard_map/ppermute | solution.py:26
  37.7 18.4 %collective-permute-start.11 = (bf16[3456,128]{1,0:T(8,128)(2,1)S(1)}, bf16[3456,128]{1,0:T(8,128)(2,1)S(1)}, u32[]{:S(2)}, u32[]{:S(2)}) collective-permute-start(bf16[3456,128]{1,0:T(8,128)(2,1)S(1)} %get-tuple-element.70), channel_id=1, source_target_pairs={{0,56},{8,0},{16,8},{24,16},{32,24},{40,32},{48,40},{56,48},{1,57}... | collective-permute-start | bytes 2654216 | tf_op jit(solution)/shard_map/ppermute | solution.py:26
  37.7 19.4 %collective-permute-start.10 = (bf16[3456,128]{1,0:T(8,128)(2,1)S(1)}, bf16[3456,128]{1,0:T(8,128)(2,1)S(1)}, u32[]{:S(2)}, u32[]{:S(2)}) collective-permute-start(bf16[3456,128]{1,0:T(8,128)(2,1)S(1)} %get-tuple-element.72.rest_17_.rest_0_), channel_id=1, source_target_pairs={{0,8},{8,16},{16,24},{24,32},{32,40},{40,48},{48,56},{56,0},{1,9},... | collective-permute-start | bytes 2654216 | tf_op jit(solution)/shard_map/ppermute | solution.py:26
  57.1 18.5 %collective-permute-start.14 = (bf16[3456,128]{1,0:T(8,128)(2,1)S(1)}, bf16[3456,128]{1,0:T(8,128)(2,1)S(1)}, u32[]{:S(2)}, u32[]{:S(2)}) collective-permute-start(bf16[3456,128]{1,0:T(8,128)(2,1)S(1)} %collective-permute-done.10.rest_6_.rest_24_.rest_7_), channel_id=1, source_target_pairs={{0,8},{8,16},{16,24},{24,32},{32,40},{40,48},{48,56},{56,0},{1,9},... | collective-permute-start | bytes 2654216 | tf_op jit(solution)/shard_map/ppermute | solution.py:26
  57.5 18.2 %collective-permute-start.15 = (bf16[3456,128]{1,0:T(8,128)(2,1)S(1)}, bf16[3456,128]{1,0:T(8,128)(2,1)S(1)}, u32[]{:S(2)}, u32[]{:S(2)}) collective-permute-start(bf16[3456,128]{1,0:T(8,128)(2,1)S(1)} %collective-permute-done.11.rest_5_.rest_18_.rest_1_), channel_id=1, source_target_pairs={{0,56},{8,0},{16,8},{24,16},{32,24},{40,32},{48,40},{56,48},{1,57}... | collective-permute-start | bytes 2654216 | tf_op jit(solution)/shard_map/ppermute | solution.py:26
  60.3 18.7 %collective-permute-start.16 = (bf16[3584,128]{1,0:T(8,128)(2,1)S(1)}, bf16[3584,128]{1,0:T(8,128)(2,1)S(1)}, u32[]{:S(2)}, u32[]{:S(2)}) collective-permute-start(bf16[3584,128]{1,0:T(8,128)(2,1)S(1)} %pad_maximum_fusion.1), channel_id=1, source_target_pairs={{0,64},{64,128},{128,192},{192,0},{1,65},{65,129},{129,193},{193,1... | collective-permute-start | bytes 2752520 | tf_op jit(solution)/shard_map/ppermute | solution.py:26
  60.5 12.7 %collective-permute-start.17 = (bf16[2688,128]{1,0:T(8,128)(2,1)S(1)}, bf16[2688,128]{1,0:T(8,128)(2,1)S(1)}, u32[]{:S(2)}, u32[]{:S(2)}) collective-permute-start(bf16[2688,128]{1,0:T(8,128)(2,1)S(1)} %pad_maximum_fusion.4), channel_id=1, source_target_pairs={{0,192},{64,0},{128,64},{192,128},{1,193},{65,1},{129,65},{193,129... | collective-permute-start | bytes 2064392 | tf_op jit(solution)/shard_map/ppermute | solution.py:26
  79.9 14.3 %collective-permute-start.20 = (bf16[2688,128]{1,0:T(8,128)(2,1)S(1)}, bf16[2688,128]{1,0:T(8,128)(2,1)S(1)}, u32[]{:S(2)}, u32[]{:S(2)}) collective-permute-start(bf16[2688,128]{1,0:T(8,128)(2,1)S(1)} %get-tuple-element.74), channel_id=1, source_target_pairs={{0,64},{64,128},{128,192},{192,0},{1,65},{65,129},{129,193},{193,1... | collective-permute-start | bytes 2064392 | tf_op jit(solution)/shard_map/ppermute | solution.py:26
  79.9 14.3 %collective-permute-start.21 = (bf16[2688,128]{1,0:T(8,128)(2,1)S(1)}, bf16[2688,128]{1,0:T(8,128)(2,1)S(1)}, u32[]{:S(2)}, u32[]{:S(2)}) collective-permute-start(bf16[2688,128]{1,0:T(8,128)(2,1)S(1)} %get-tuple-element.73), channel_id=1, source_target_pairs={{0,192},{64,0},{128,64},{192,128},{1,193},{65,1},{129,65},{193,129... | collective-permute-start | bytes 2064392 | tf_op jit(solution)/shard_map/ppermute | solution.py:26
  82.7 11.5 %collective-permute-start.18 = (bf16[2560,128]{1,0:T(8,128)(2,1)S(1)}, bf16[2560,128]{1,0:T(8,128)(2,1)S(1)}, u32[]{:S(2)}, u32[]{:S(2)}) collective-permute-start(bf16[2560,128]{1,0:T(8,128)(2,1)S(1)} %slice.106), channel_id=1, source_target_pairs={{0,8},{8,16},{16,24},{24,32},{32,40},{40,48},{48,56},{56,0},{1,9},... | collective-permute-start | bytes 1966088 | tf_op jit(solution)/shard_map/ppermute | solution.py:26
  82.8 11.4 %collective-permute-start.19 = (bf16[2560,128]{1,0:T(8,128)(2,1)S(1)}, bf16[2560,128]{1,0:T(8,128)(2,1)S(1)}, u32[]{:S(2)}, u32[]{:S(2)}) collective-permute-start(bf16[2560,128]{1,0:T(8,128)(2,1)S(1)} %slice.107), channel_id=1, source_target_pairs={{0,56},{8,0},{16,8},{24,16},{32,24},{40,32},{48,40},{56,48},{1,57}... | collective-permute-start | bytes 1966088 | tf_op jit(solution)/shard_map/ppermute | solution.py:26
  94.3 9.6 %collective-permute-start.23 = (bf16[1280,128]{1,0:T(8,128)(2,1)S(1)}, bf16[1280,128]{1,0:T(8,128)(2,1)S(1)}, u32[]{:S(2)}, u32[]{:S(2)}) collective-permute-start(bf16[1280,128]{1,0:T(8,128)(2,1)S(1)} %slice.114), channel_id=1, source_target_pairs={{0,8},{8,16},{16,24},{24,32},{32,40},{40,48},{48,56},{56,0},{1,9},... | collective-permute-start | bytes 983048 | tf_op jit(solution)/shard_map/ppermute | solution.py:26
  94.4 9.5 %collective-permute-start.24 = (bf16[1280,128]{1,0:T(8,128)(2,1)S(1)}, bf16[1280,128]{1,0:T(8,128)(2,1)S(1)}, u32[]{:S(2)}, u32[]{:S(2)}) collective-permute-start(bf16[1280,128]{1,0:T(8,128)(2,1)S(1)} %slice.115), channel_id=1, source_target_pairs={{0,56},{8,0},{16,8},{24,16},{32,24},{40,32},{48,40},{56,48},{1,57}... | collective-permute-start | bytes 983048 | tf_op jit(solution)/shard_map/ppermute | solution.py:26
  97.2 6.4 %collective-permute-start.22 = (bf16[896,128]{1,0:T(8,128)(2,1)S(1)}, bf16[896,128]{1,0:T(8,128)(2,1)S(1)}, u32[]{:S(2)}, u32[]{:S(2)}) collective-permute-start(bf16[896,128]{1,0:T(8,128)(2,1)S(1)} %slice.113), channel_id=1, source_target_pairs={{0,64},{64,128},{128,192},{192,0},{1,65},{65,129},{129,193},{193,1... | collective-permute-start | bytes 688136 | tf_op jit(solution)/shard_map/ppermute | solution.py:26
  116.9 9.5 %collective-permute-start.25 = (bf16[512,512]{1,0:T(8,128)(2,1)}, bf16[512,512]{1,0:T(8,128)(2,1)S(1)}, u32[]{:S(2)}, u32[]{:S(2)}) collective-permute-start(bf16[512,512]{1,0:T(8,128)(2,1)} %shard_map.64.a_ref), channel_id=1, source_target_pairs={{0,2},{2,4},{4,6},{6,0},{1,3},{3,5},{5,7},{7,1},{8,10},{10,12},{12... | collective-permute-start | bytes 1572872 | tf_op jit(solution)/shard_map/ppermute | solution.py:26
  117.0 9.4 %collective-permute-start.26 = (bf16[512,512]{1,0:T(8,128)(2,1)}, bf16[512,512]{1,0:T(8,128)(2,1)S(1)}, u32[]{:S(2)}, u32[]{:S(2)}) collective-permute-start(bf16[512,512]{1,0:T(8,128)(2,1)} %shard_map.64.a_ref), channel_id=1, source_target_pairs={{0,6},{2,0},{4,2},{6,4},{1,7},{3,1},{5,3},{7,5},{8,14},{10,8},{12,... | collective-permute-start | bytes 1572872 | tf_op jit(solution)/shard_map/ppermute | solution.py:26
  126.5 7.5 %collective-permute-start.27 = (bf16[256,512]{1,0:T(8,128)(2,1)S(1)}, bf16[256,512]{1,0:T(8,128)(2,1)S(1)}, u32[]{:S(2)}, u32[]{:S(2)}) collective-permute-start(bf16[256,512]{1,0:T(8,128)(2,1)S(1)} %slice.116), channel_id=1, source_target_pairs={{0,2},{2,4},{4,6},{6,0},{1,3},{3,5},{5,7},{7,1},{8,10},{10,12},{12... | collective-permute-start | bytes 786440 | tf_op jit(solution)/shard_map/ppermute | solution.py:26
  127.0 7.0 %collective-permute-start.28 = (bf16[256,512]{1,0:T(8,128)(2,1)S(1)}, bf16[256,512]{1,0:T(8,128)(2,1)S(1)}, u32[]{:S(2)}, u32[]{:S(2)}) collective-permute-start(bf16[256,512]{1,0:T(8,128)(2,1)S(1)} %slice.117), channel_id=1, source_target_pairs={{0,6},{2,0},{4,2},{6,4},{1,7},{3,1},{5,3},{7,5},{8,14},{10,8},{12,... | collective-permute-start | bytes 786440 | tf_op jit(solution)/shard_map/ppermute | solution.py:26
  134.4 14.9 %collective-permute-start.29 = (bf16[512,512]{1,0:T(8,128)(2,1)S(1)}, bf16[512,512]{1,0:T(8,128)(2,1)S(1)}, u32[]{:S(2)}, u32[]{:S(2)}) collective-permute-start(bf16[512,512]{1,0:T(8,128)(2,1)S(1)} %shard_map.68), channel_id=1, source_target_pairs={{0,1},{1,0},{2,3},{3,2},{4,5},{5,4},{6,7},{7,6},{8,9},{9,8},{10,11... | collective-permute-start | bytes 1572872 | tf_op jit(solution)/shard_map/ppermute | solution.py:26
  (27 other events, 220.0 us)

commit v4 on v3

--- a/solution.py
+++ b/solution.py
@@ -79,9 +79,12 @@
     s3p, s3m = zp(s2p[:z3]), zm(s2m[:z3])
     gcp, gcm = yp(join(z4, chunk(gap, 2), chunk(gbp, 0))), ym(join(z4, chunk(gam, 3), chunk(gbm, 1)))
     (s3p, s3m, gcp, gcm), _ = gate((s3p, s3m, gcp, gcm), ())
-    s4p, s4m, gdp = zp(s3p[: z3 // 2]), zm(s3m[z3 // 2 :]), yp(chunk(gcp, 0))
+    slots = lambda v, two, first, size: join(*(v[i * SLOT + first : i * SLOT + first + size] for i in two))
+    v4p, v4m, gdp = zp(slots(s3p, (0, 1), 0, LAST)), zm(slots(s3m, (2, 3), 0, LAST)), yp(chunk(gcp, 0))
+    w4p, w4m = zp(slots(s3p, (0, 1), LAST, BLK)), zm(slots(s3m, (2, 3), LAST, BLK))
     named = (kv, z1m, z1p, z2m, z2p, s1m, s1p, s2p, g0p, g0m, gap, gam, gbp, gbm, gcp, gcm, gdp)
-    return named, [s0p, s1m, s2m, s3m, s4p, s3p, s2p, s1p, s4m], early
+    ring = lambda p, m: [s0p, s1m, s2m, s3m, p, s3p, s2p, s1p, m]
+    return named, ring(v4p, v4m), ring(w4p, w4m), early
 
 
 TILE = 128
@@ -124,7 +127,7 @@
         start(u, 0, named, code & 31, (code >> 5) * 16, 5)
         slot = jnp.where(dy == 0, 0, jnp.where(dy == 3, 1, jnp.where(dy == 1, 2, 3)))
         late = (dz == 4) & (slot >= 2)
-        start(u, 1, ya, jnp.where(late, NZ, dz), jnp.where(late, slot - 2, slot) * SLOT, 3)
+        start(u, 1, ya, jnp.where(late, NZ, dz), jnp.where(late, slot - 2, slot) * jnp.where(dz == 4, LAST, SLOT), 3)
 
     for u in range(n + 1):
         vbuf[u, :, HD:] = jnp.ones((BLK, HD), jnp.bfloat16)
@@ -170,7 +173,7 @@
             col = (at_ref[0] + dz) & (NZ - 1)
 
             def copy(array, at):
-                rows = pl.ds(pl.multiple_of(at * SLOT + LAST, 16), BLK)
+                rows = pl.ds(pl.multiple_of(at * BLK if dz == 4 else at * SLOT + LAST, 16), BLK)
                 pltpu.make_async_copy(array.at[rows], dest.at[col], sems.at[i]).start()
 
             if dz == 4:
@@ -267,10 +270,11 @@
         return jnp.where(d == 0, 0, jnp.where(d == 3, 1, jnp.where(d == 1, 2, 3)))
 
     at = jnp.stack([z] + [rows_of(x + d) for d in (0, -1, 1, 2)])
-    named, ya, (route, at) = gather(jnp.stack([keys, values]).reshape(2 * BLK, HD), w_out, turn, (route, at))
+    named, ya, w, (route, at) = gather(jnp.stack([keys, values]).reshape(2 * BLK, HD), w_out, turn, (route, at))
     attn = attention(route, jnp.stack([y, z]), queries, keys, values, named, ya)
+    attn, w = gate(attn, w)
     x1p, x1m = xp(attn), xm(attn)
-    (x1p, x1m), (total, near, far) = gate((x1p, x1m), project_own(at, attn, ya))
+    (x1p, x1m), (total, near, far) = gate((x1p, x1m), project_own(at, attn, w))
     x2p, x2m = xp(x1p[:HALF]), xm(x1m[HALF:])
     total = project_near(total, x1p, x1m, near)
     theirs = swap(project_far(1 - c, total, x2p, x2m, far, jnp.bfloat16))

time: 151 us -> 152 us (level)
  waiting for transfers between devices: 58.5 us -> 64.5 us
  starting transfers between devices: 61 us -> 57.2 us
    ppermute x29 -> x31, waiting for transfers between devices: 58.5 us -> 64.5 us  [shift(): return lax.ppermute(v, axis, [(i, (i + d) % n) for i in range(n)])]
    ppermute x29 -> x31, starting transfers between devices: 59.4 us -> 55.7 us  [shift(): return lax.ppermute(v, axis, [(i, (i + d) % n) for i in range(n)])]
    unnamed x64 -> x68, local copies, waits for them, and re-layouts: 6.12 us -> 5.27 us
  transfers between devices with their start and end apart: 30 -> 32, of which waited for: 15 -> 15; matrix products, arithmetic and copies ran while one was open for 2% -> 2% of each run, Pallas kernels for 5% -> 12%
where the time goes in v4:
time: 152 us
  waiting for transfers between devices  64.5 us (42%)
  starting transfers between devices  57.2 us (38%)
  Pallas kernels  19.4 us (13%)
  local copies, waits for them, and re-layouts  7.24 us (5%)
  other arithmetic  2.94 us (2%)
    ppermute x31, waiting for transfers between devices, shift(): return lax.ppermute(v, axis, [(i, (i + d) % n) for i in range(n)])  64.5 us
    ppermute x31, starting transfers between devices, shift(): return lax.ppermute(v, axis, [(i, (i + d) % n) for i in range(n)])  55.7 us
    pallas_call x5, Pallas kernels, call(): pl.pallas_call(kernel, out_shape=out_shape, in_specs=spec(pltpu.SMEM, sca...  19.4 us
    unnamed x68, local copies, waits for them, and re-layouts  5.27 us
  transfers between devices with their start and end apart: 32, of which 15 were waited for; matrix products, arithmetic and copies ran while one was open for 2% of the time, Pallas kernels for 12%

profile of v4, /device:TPU:1, one launch (start us, length us, event | category | flops | bytes accessed | tf_op | source)
XLA Modules:
  0.0 151.9 jit_solution(2883439580809129486)
XLA Ops:
  1.0 3.6 %collective-permute-start.3 = (bf16[1024,128]{1,0:T(8,128)(2,1)S(1)}, bf16[1024,128]{1,0:T(8,128)(2,1)S(1)}, u32[]{:S(2)}, u32[]{:S(2)}) collective-permute-start(bf16[1024,128]{1,0:T(8,128)(2,1)S(1)} %bitcast.11), channel_id=1, source_target_pairs={{0,192},{64,0},{128,64},{192,128},{1,193},{65,1},{129,65},{193,129... | collective-permute-start | bytes 786440 | tf_op jit(solution)/shard_map/ppermute | solution.py:26
  4.7 5.6 %collective-permute-start.1 = (bf16[1024,128]{1,0:T(8,128)(2,1)S(1)}, bf16[1024,128]{1,0:T(8,128)(2,1)S(1)}, u32[]{:S(2)}, u32[]{:S(2)}) collective-permute-start(bf16[1024,128]{1,0:T(8,128)(2,1)S(1)} %bitcast.13), channel_id=1, source_target_pairs={{0,56},{8,0},{16,8},{24,16},{32,24},{40,32},{48,40},{56,48},{1,57}... | collective-permute-start | bytes 786440 | tf_op jit(solution)/shard_map/ppermute | solution.py:26
  10.2 1.6 %collective-permute-start.4 = (bf16[512,128]{1,0:T(8,128)(2,1)}, bf16[512,128]{1,0:T(8,128)(2,1)S(1)}, u32[]{:S(2)}, u32[]{:S(2)}) collective-permute-start(bf16[512,128]{1,0:T(8,128)(2,1)} %param.10), channel_id=1, source_target_pairs={{0,0},{1,1},{2,64},{3,65},{4,128},{5,129},{6,192},{7,193},{8,8},{9... | collective-permute-start | bytes 393224 | tf_op jit(solution)/shard_map/ppermute | solution.py:64
  13.4 1.5 collective-permute-done.1.rest_1_
  14.9 3.1 %collective-permute-done.rest_2_ = bf16[1024,128]{1,0:T(8,128)(2,1)S(1)} collective-permute-done((bf16[1024,128]{1,0:T(8,128)(2,1)S(1)}, bf16[1024,128]{1,0:T(8,128)(2,1)S(1)}, u32[]{:S(2)}, u32[]{:S(2)}) %collective-permute-start) | collective-permute-done | bytes 262176 | tf_op jit(solution)/shard_map/ppermute | solution.py:26
  18.5 1.2 collective-permute-start.8
  19.7 5.6 %collective-permute-start.7 = (bf16[512,128]{1,0:T(8,128)(2,1)S(1)}, bf16[512,128]{1,0:T(8,128)(2,1)S(1)}, u32[]{:S(2)}, u32[]{:S(2)}) collective-permute-start(bf16[512,128]{1,0:T(8,128)(2,1)S(1)} %collective-permute-done.4), channel_id=1, source_target_pairs={{0,128},{64,192},{128,0},{192,64},{1,129},{65,193},{129,1},{193,65... | collective-permute-start | bytes 393224 | tf_op jit(solution)/shard_map/ppermute | solution.py:26
  25.3 2.9 %collective-permute-start.6 = (bf16[576,128]{1,0:T(8,128)(2,1)S(1)}, bf16[576,128]{1,0:T(8,128)(2,1)S(1)}, u32[]{:S(2)}, u32[]{:S(2)}) collective-permute-start(bf16[576,128]{1,0:T(8,128)(2,1)S(1)} %get-tuple-element.103), channel_id=1, source_target_pairs={{0,192},{64,0},{128,64},{192,128},{1,193},{65,1},{129,65},{193,129... | collective-permute-start | bytes 442376 | tf_op jit(solution)/shard_map/ppermute | solution.py:26
  28.9 4.9 %collective-permute-done.6 = bf16[576,128]{1,0:T(8,128)(2,1)S(1)} collective-permute-done((bf16[576,128]{1,0:T(8,128)(2,1)S(1)}, bf16[576,128]{1,0:T(8,128)(2,1)S(1)}, u32[]{:S(2)}, u32[]{:S(2)}) %collective-permute-start.6) | collective-permute-done | bytes 147488 | tf_op jit(solution)/shard_map/ppermute | solution.py:26
  34.7 3.6 %collective-permute-start.13 = (bf16[3584,128]{1,0:T(8,128)(2,1)S(1)}, bf16[3584,128]{1,0:T(8,128)(2,1)S(1)}, u32[]{:S(2)}, u32[]{:S(2)}) collective-permute-start(bf16[3584,128]{1,0:T(8,128)(2,1)S(1)} %pad_maximum_fusion), channel_id=1, source_target_pairs={{0,192},{64,0},{128,64},{192,128},{1,193},{65,1},{129,65},{193,129... | collective-permute-start | bytes 2752520 | tf_op jit(solution)/shard_map/ppermute | solution.py:26
  38.3 2.3 %collective-permute-start.11 = (bf16[3456,128]{1,0:T(8,128)(2,1)S(1)}, bf16[3456,128]{1,0:T(8,128)(2,1)S(1)}, u32[]{:S(2)}, u32[]{:S(2)}) collective-permute-start(bf16[3456,128]{1,0:T(8,128)(2,1)S(1)} %get-tuple-element.98), channel_id=1, source_target_pairs={{0,56},{8,0},{16,8},{24,16},{32,24},{40,32},{48,40},{56,48},{1,57}... | collective-permute-start | bytes 2654216 | tf_op jit(solution)/shard_map/ppermute | solution.py:26
  40.6 17.5 %collective-permute-done.11.rest_5_.rest_18_.rest_1_ = bf16[3456,128]{1,0:T(8,128)(2,1)S(1)} collective-permute-done((bf16[3456,128]{1,0:T(8,128)(2,1)S(1)}, bf16[3456,128]{1,0:T(8,128)(2,1)S(1)}, u32[]{:S(2)}, u32[]{:S(2)}) %collective-permute-start.11) | collective-permute-done | bytes 884768 | tf_op jit(solution)/shard_map/ppermute | solution.py:26
  58.0 2.9 %collective-permute-done.10.rest_6_.rest_24_.rest_7_ = bf16[3456,128]{1,0:T(8,128)(2,1)S(1)} collective-permute-done((bf16[3456,128]{1,0:T(8,128)(2,1)S(1)}, bf16[3456,128]{1,0:T(8,128)(2,1)S(1)}, u32[]{:S(2)}, u32[]{:S(2)}) %collective-permute-start.10) | collective-permute-done | bytes 884768 | tf_op jit(solution)/shard_map/ppermute | solution.py:26
  63.1 2.7 %collective-permute-start.17 = (bf16[2688,128]{1,0:T(8,128)(2,1)S(1)}, bf16[2688,128]{1,0:T(8,128)(2,1)S(1)}, u32[]{:S(2)}, u32[]{:S(2)}) collective-permute-start(bf16[2688,128]{1,0:T(8,128)(2,1)S(1)} %pad_maximum_fusion.4), channel_id=1, source_target_pairs={{0,192},{64,0},{128,64},{192,128},{1,193},{65,1},{129,65},{193,129... | collective-permute-start | bytes 2064392 | tf_op jit(solution)/shard_map/ppermute | solution.py:26
  65.9 11.0 %collective-permute-done.17.rest_13_ = bf16[2688,128]{1,0:T(8,128)(2,1)S(1)} collective-permute-done((bf16[2688,128]{1,0:T(8,128)(2,1)S(1)}, bf16[2688,128]{1,0:T(8,128)(2,1)S(1)}, u32[]{:S(2)}, u32[]{:S(2)}) %collective-permute-start.17) | collective-permute-done | bytes 688160 | tf_op jit(solution)/shard_map/ppermute | solution.py:26
  76.9 2.5 %collective-permute-done.15.rest_19_.rest_2_ = bf16[3456,128]{1,0:T(8,128)(2,1)S(1)} collective-permute-done((bf16[3456,128]{1,0:T(8,128)(2,1)S(1)}, bf16[3456,128]{1,0:T(8,128)(2,1)S(1)}, u32[]{:S(2)}, u32[]{:S(2)}) %collective-permute-start.15) | collective-permute-done | bytes 884768 | tf_op jit(solution)/shard_map/ppermute | solution.py:26
  79.4 2.4 %collective-permute-done.14.rest_7_.rest_23_.rest_6_ = bf16[3456,128]{1,0:T(8,128)(2,1)S(1)} collective-permute-done((bf16[3456,128]{1,0:T(8,128)(2,1)S(1)}, bf16[3456,128]{1,0:T(8,128)(2,1)S(1)}, u32[]{:S(2)}, u32[]{:S(2)}) %collective-permute-start.14) | collective-permute-done | bytes 884768 | tf_op jit(solution)/shard_map/ppermute | solution.py:26
  85.5 2.4 %collective-permute-start.19 = (bf16[2560,128]{1,0:T(8,128)(2,1)S(1)}, bf16[2560,128]{1,0:T(8,128)(2,1)S(1)}, u32[]{:S(2)}, u32[]{:S(2)}) collective-permute-start(bf16[2560,128]{1,0:T(8,128)(2,1)S(1)} %slice.125), channel_id=1, source_target_pairs={{0,56},{8,0},{16,8},{24,16},{32,24},{40,32},{48,40},{56,48},{1,57}... | collective-permute-start | bytes 1966088 | tf_op jit(solution)/shard_map/ppermute | solution.py:26
  88.6 9.2 %collective-permute-done.18.rest_22_.rest_5_ = bf16[2560,128]{1,0:T(8,128)(2,1)S(1)} collective-permute-done((bf16[2560,128]{1,0:T(8,128)(2,1)S(1)}, bf16[2560,128]{1,0:T(8,128)(2,1)S(1)}, u32[]{:S(2)}, u32[]{:S(2)}) %collective-permute-start.18) | collective-permute-done | bytes 655392 | tf_op jit(solution)/shard_map/ppermute | solution.py:26
  98.4 2.3 %collective-permute-start.24 = (bf16[256,128]{1,0:T(8,128)(2,1)S(1)}, bf16[256,128]{1,0:T(8,128)(2,1)S(1)}, u32[]{:S(2)}, u32[]{:S(2)}) collective-permute-start(bf16[256,128]{1,0:T(8,128)(2,1)S(1)} %pad_maximum_fusion.11), channel_id=1, source_target_pairs={{0,56},{8,0},{16,8},{24,16},{32,24},{40,32},{48,40},{56,48},{1,57}... | collective-permute-start | bytes 196616 | tf_op jit(solution)/shard_map/ppermute | solution.py:26
  101.2 3.0 %collective-permute-start.26 = (bf16[1024,128]{1,0:T(8,128)(2,1)S(1)}, bf16[1024,128]{1,0:T(8,128)(2,1)S(1)}, u32[]{:S(2)}, u32[]{:S(2)}) collective-permute-start(bf16[1024,128]{1,0:T(8,128)(2,1)S(1)} %pad_maximum_fusion.7), channel_id=1, source_target_pairs={{0,56},{8,0},{16,8},{24,16},{32,24},{40,32},{48,40},{56,48},{1,57}... | collective-permute-start | bytes 786440 | tf_op jit(solution)/shard_map/ppermute | solution.py:26
  104.1 2.7 %collective-permute-done.22.rest_16_ = bf16[896,128]{1,0:T(8,128)(2,1)S(1)} collective-permute-done((bf16[896,128]{1,0:T(8,128)(2,1)S(1)}, bf16[896,128]{1,0:T(8,128)(2,1)S(1)}, u32[]{:S(2)}, u32[]{:S(2)}) %collective-permute-start.22) | collective-permute-done | bytes 229408 | tf_op jit(solution)/shard_map/ppermute | solution.py:26
  107.5 11.6 %shard_map.64.a_ref = bf16[512,512]{1,0:T(8,128)(2,1)} custom-call(s32[12]{0:T(128)} %reshape.8.route_ref, s32[2]{0:T(128)} %pad_add_fusion.place_ref, s32[32]{0:T(128)} %constant.58.clone.table_ref, bf16[512,512]{1,0:T(8,128)(2,1)} %q_ref.1, bf16[512,128]{1,0:T(8,128)(2,1)} %k_ref.1, bf16[512,128]{1,0:T(8,128)(2,1)} %v_ref.1, bf16[1024,128]{1,0:T(8,128)(2,1)} %bitcast.16, ...), custom_call_target="tpu_custom_call" | custom-call | flops 3221225472 | bytes 8388608 | tf_op jit(solution)/shard_map/pallas_call | solution.py:216
  119.3 1.5 collective-permute-start.27
  120.7 5.6 %shard_map.65 = (f32[512,1024]{1,0:T(8,128)}, bf16[2,8,512,128]{3,2,1,0:T(8,128)(2,1)}, bf16[8,512,128]{2,1,0:T(8,128)(2,1)}) custom-call(s32[5]{0:T(128)} %stack.42.at_ref, bf16[512,512]{1,0:T(8,128)(2,1)} %shard_map.64.a_ref, bf16[3456,128]{1,0:T(8,128)(2,1)} %copy-done.7, bf16[3456,128]{1,0:T(8,128)(2,1)} %copy-done.5, bf16[3456,128]{1,0:T(8,128)(2,1)} %copy-done.8, ...), custom_call_target="tpu_custom_call" | custom-call | flops 536870912 | bytes 8388608 | tf_op jit(solution)/shard_map/pallas_call | solution.py:216
  127.5 1.3 collective-permute-done.27.a0_ref
  129.4 2.2 %collective-permute-start.30 = (bf16[256,512]{1,0:T(8,128)(2,1)S(1)}, bf16[256,512]{1,0:T(8,128)(2,1)S(1)}, u32[]{:S(2)}, u32[]{:S(2)}) collective-permute-start(bf16[256,512]{1,0:T(8,128)(2,1)S(1)} %slice.141), channel_id=1, source_target_pairs={{0,6},{2,0},{4,2},{6,4},{1,7},{3,1},{5,3},{7,5},{8,14},{10,8},{12,... | collective-permute-start | bytes 786440 | tf_op jit(solution)/shard_map/ppermute | solution.py:26
  131.6 1.6 %copy-done.2 = f32[512,1024]{1,0:T(8,128)S(1)} copy-done((f32[512,1024]{1,0:T(8,128)S(1)}, f32[512,1024]{1,0:T(8,128)}, u32[]{:S(2)}) %copy-start.2) | copy-done | bytes 2097176
  133.2 1.6 %copy-done.3 = bf16[2,8,512,128]{3,2,1,0:T(8,128)(2,1)S(1)} copy-done((bf16[2,8,512,128]{3,2,1,0:T(8,128)(2,1)S(1)}, bf16[2,8,512,128]{3,2,1,0:T(8,128)(2,1)}, u32[]{:S(2)}) %copy-start.3) | copy-done | bytes 2097176
  134.8 1.2 shard_map.66.total_ref
  136.0 2.4 %collective-permute-done.29.a0_ref = bf16[256,512]{1,0:T(8,128)(2,1)S(1)} collective-permute-done((bf16[256,512]{1,0:T(8,128)(2,1)S(1)}, bf16[256,512]{1,0:T(8,128)(2,1)S(1)}, u32[]{:S(2)}, u32[]{:S(2)}) %collective-permute-start.29) | collective-permute-done | bytes 262176 | tf_op jit(solution)/shard_map/ppermute | solution.py:26
  138.9 10.5 %collective-permute-start.31 = (bf16[512,512]{1,0:T(8,128)(2,1)S(1)}, bf16[512,512]{1,0:T(8,128)(2,1)S(1)}, u32[]{:S(2)}, u32[]{:S(2)}) collective-permute-start(bf16[512,512]{1,0:T(8,128)(2,1)S(1)} %shard_map.68), channel_id=1, source_target_pairs={{0,1},{1,0},{2,3},{3,2},{4,5},{5,4},{6,7},{7,6},{8,9},{9,8},{10,11... | collective-permute-start | bytes 1572872 | tf_op jit(solution)/shard_map/ppermute | solution.py:26
  (145 shorter events, 17.3 us)
Async XLA Ops:
  1.0 12.3 %collective-permute-start.3 = (bf16[1024,128]{1,0:T(8,128)(2,1)S(1)}, bf16[1024,128]{1,0:T(8,128)(2,1)S(1)}, u32[]{:S(2)}, u32[]{:S(2)}) collective-permute-start(bf16[1024,128]{1,0:T(8,128)(2,1)S(1)} %bitcast.11), channel_id=1, source_target_pairs={{0,192},{64,0},{128,64},{192,128},{1,193},{65,1},{129,65},{193,129... | collective-permute-start | bytes 786440 | tf_op jit(solution)/shard_map/ppermute | solution.py:26
  4.7 8.7 %collective-permute-start.2 = (bf16[1024,128]{1,0:T(8,128)(2,1)S(1)}, bf16[1024,128]{1,0:T(8,128)(2,1)S(1)}, u32[]{:S(2)}, u32[]{:S(2)}) collective-permute-start(bf16[1024,128]{1,0:T(8,128)(2,1)S(1)} %bitcast.12), channel_id=1, source_target_pairs={{0,64},{64,128},{128,192},{192,0},{1,65},{65,129},{129,193},{193,1... | collective-permute-start | bytes 786440 | tf_op jit(solution)/shard_map/ppermute | solution.py:26
  4.7 10.2 %collective-permute-start.1 = (bf16[1024,128]{1,0:T(8,128)(2,1)S(1)}, bf16[1024,128]{1,0:T(8,128)(2,1)S(1)}, u32[]{:S(2)}, u32[]{:S(2)}) collective-permute-start(bf16[1024,128]{1,0:T(8,128)(2,1)S(1)} %bitcast.13), channel_id=1, source_target_pairs={{0,56},{8,0},{16,8},{24,16},{32,24},{40,32},{48,40},{56,48},{1,57}... | collective-permute-start | bytes 786440 | tf_op jit(solution)/shard_map/ppermute | solution.py:26
  10.2 7.8 %collective-permute-start = (bf16[1024,128]{1,0:T(8,128)(2,1)S(1)}, bf16[1024,128]{1,0:T(8,128)(2,1)S(1)}, u32[]{:S(2)}, u32[]{:S(2)}) collective-permute-start(bf16[1024,128]{1,0:T(8,128)(2,1)S(1)} %bitcast.14), channel_id=1, source_target_pairs={{0,8},{8,16},{16,24},{24,32},{32,40},{40,48},{48,56},{56,0},{1,9},... | collective-permute-start | bytes 786440 | tf_op jit(solution)/shard_map/ppermute | solution.py:26
  10.2 3.1 %collective-permute-start.4 = (bf16[512,128]{1,0:T(8,128)(2,1)}, bf16[512,128]{1,0:T(8,128)(2,1)S(1)}, u32[]{:S(2)}, u32[]{:S(2)}) collective-permute-start(bf16[512,128]{1,0:T(8,128)(2,1)} %param.10), channel_id=1, source_target_pairs={{0,0},{1,1},{2,64},{3,65},{4,128},{5,129},{6,192},{7,193},{8,8},{9... | collective-permute-start | bytes 393224 | tf_op jit(solution)/shard_map/ppermute | solution.py:64
  18.0 15.8 %collective-permute-start.9 = (bf16[1024,128]{1,0:T(8,128)(2,1)S(1)}, bf16[1024,128]{1,0:T(8,128)(2,1)S(1)}, u32[]{:S(2)}, u32[]{:S(2)}) collective-permute-start(bf16[1024,128]{1,0:T(8,128)(2,1)S(1)} %collective-permute-done.1.rest_1_), channel_id=1, source_target_pairs={{0,56},{8,0},{16,8},{24,16},{32,24},{40,32},{48,40},{56,48},{1,57}... | collective-permute-start | bytes 786440 | tf_op jit(solution)/shard_map/ppermute | solution.py:26
  18.5 15.4 %collective-permute-start.8 = (bf16[1024,128]{1,0:T(8,128)(2,1)S(1)}, bf16[1024,128]{1,0:T(8,128)(2,1)S(1)}, u32[]{:S(2)}, u32[]{:S(2)}) collective-permute-start(bf16[1024,128]{1,0:T(8,128)(2,1)S(1)} %collective-permute-done.rest_2_), channel_id=1, source_target_pairs={{0,8},{8,16},{16,24},{24,32},{32,40},{40,48},{48,56},{56,0},{1,9},... | collective-permute-start | bytes 786440 | tf_op jit(solution)/shard_map/ppermute | solution.py:26
  19.7 9.2 %collective-permute-start.7 = (bf16[512,128]{1,0:T(8,128)(2,1)S(1)}, bf16[512,128]{1,0:T(8,128)(2,1)S(1)}, u32[]{:S(2)}, u32[]{:S(2)}) collective-permute-start(bf16[512,128]{1,0:T(8,128)(2,1)S(1)} %collective-permute-done.4), channel_id=1, source_target_pairs={{0,128},{64,192},{128,0},{192,64},{1,129},{65,193},{129,1},{193,65... | collective-permute-start | bytes 393224 | tf_op jit(solution)/shard_map/ppermute | solution.py:26
  25.3 8.5 %collective-permute-start.6 = (bf16[576,128]{1,0:T(8,128)(2,1)S(1)}, bf16[576,128]{1,0:T(8,128)(2,1)S(1)}, u32[]{:S(2)}, u32[]{:S(2)}) collective-permute-start(bf16[576,128]{1,0:T(8,128)(2,1)S(1)} %get-tuple-element.103), channel_id=1, source_target_pairs={{0,192},{64,0},{128,64},{192,128},{1,193},{65,1},{129,65},{193,129... | collective-permute-start | bytes 442376 | tf_op jit(solution)/shard_map/ppermute | solution.py:26
  28.2 5.6 %collective-permute-start.5 = (bf16[576,128]{1,0:T(8,128)(2,1)S(1)}, bf16[576,128]{1,0:T(8,128)(2,1)S(1)}, u32[]{:S(2)}, u32[]{:S(2)}) collective-permute-start(bf16[576,128]{1,0:T(8,128)(2,1)S(1)} %get-tuple-element.104), channel_id=1, source_target_pairs={{0,64},{64,128},{128,192},{192,0},{1,65},{65,129},{129,193},{193,1... | collective-permute-start | bytes 442376 | tf_op jit(solution)/shard_map/ppermute | solution.py:26
  34.7 26.3 %collective-permute-start.13 = (bf16[3584,128]{1,0:T(8,128)(2,1)S(1)}, bf16[3584,128]{1,0:T(8,128)(2,1)S(1)}, u32[]{:S(2)}, u32[]{:S(2)}) collective-permute-start(bf16[3584,128]{1,0:T(8,128)(2,1)S(1)} %pad_maximum_fusion), channel_id=1, source_target_pairs={{0,192},{64,0},{128,64},{192,128},{1,193},{65,1},{129,65},{193,129... | collective-permute-start | bytes 2752520 | tf_op jit(solution)/shard_map/ppermute | solution.py:26
  38.3 22.7 %collective-permute-start.12 = (bf16[3584,128]{1,0:T(8,128)(2,1)S(1)}, bf16[3584,128]{1,0:T(8,128)(2,1)S(1)}, u32[]{:S(2)}, u32[]{:S(2)}) collective-permute-start(bf16[3584,128]{1,0:T(8,128)(2,1)S(1)} %pad_maximum_fusion), channel_id=1, source_target_pairs={{0,64},{64,128},{128,192},{192,0},{1,65},{65,129},{129,193},{193,1... | collective-permute-start | bytes 2752520 | tf_op jit(solution)/shard_map/ppermute | solution.py:26
  38.3 19.7 %collective-permute-start.11 = (bf16[3456,128]{1,0:T(8,128)(2,1)S(1)}, bf16[3456,128]{1,0:T(8,128)(2,1)S(1)}, u32[]{:S(2)}, u32[]{:S(2)}) collective-permute-start(bf16[3456,128]{1,0:T(8,128)(2,1)S(1)} %get-tuple-element.98), channel_id=1, source_target_pairs={{0,56},{8,0},{16,8},{24,16},{32,24},{40,32},{48,40},{56,48},{1,57}... | collective-permute-start | bytes 2654216 | tf_op jit(solution)/shard_map/ppermute | solution.py:26
  40.6 20.4 %collective-permute-start.10 = (bf16[3456,128]{1,0:T(8,128)(2,1)S(1)}, bf16[3456,128]{1,0:T(8,128)(2,1)S(1)}, u32[]{:S(2)}, u32[]{:S(2)}) collective-permute-start(bf16[3456,128]{1,0:T(8,128)(2,1)S(1)} %get-tuple-element.72.rest_17_.rest_0_), channel_id=1, source_target_pairs={{0,8},{8,16},{16,24},{24,32},{32,40},{40,48},{48,56},{56,0},{1,9},... | collective-permute-start | bytes 2654216 | tf_op jit(solution)/shard_map/ppermute | solution.py:26
  61.0 18.3 %collective-permute-start.15 = (bf16[3456,128]{1,0:T(8,128)(2,1)S(1)}, bf16[3456,128]{1,0:T(8,128)(2,1)S(1)}, u32[]{:S(2)}, u32[]{:S(2)}) collective-permute-start(bf16[3456,128]{1,0:T(8,128)(2,1)S(1)} %collective-permute-done.11.rest_5_.rest_18_.rest_1_), channel_id=1, source_target_pairs={{0,56},{8,0},{16,8},{24,16},{32,24},{40,32},{48,40},{56,48},{1,57}... | collective-permute-start | bytes 2654216 | tf_op jit(solution)/shard_map/ppermute | solution.py:26
  62.1 19.7 %collective-permute-start.14 = (bf16[3456,128]{1,0:T(8,128)(2,1)S(1)}, bf16[3456,128]{1,0:T(8,128)(2,1)S(1)}, u32[]{:S(2)}, u32[]{:S(2)}) collective-permute-start(bf16[3456,128]{1,0:T(8,128)(2,1)S(1)} %collective-permute-done.10.rest_6_.rest_24_.rest_7_), channel_id=1, source_target_pairs={{0,8},{8,16},{16,24},{24,32},{32,40},{40,48},{48,56},{56,0},{1,9},... | collective-permute-start | bytes 2654216 | tf_op jit(solution)/shard_map/ppermute | solution.py:26
  63.0 19.7 %collective-permute-start.16 = (bf16[3584,128]{1,0:T(8,128)(2,1)S(1)}, bf16[3584,128]{1,0:T(8,128)(2,1)S(1)}, u32[]{:S(2)}, u32[]{:S(2)}) collective-permute-start(bf16[3584,128]{1,0:T(8,128)(2,1)S(1)} %pad_maximum_fusion.1), channel_id=1, source_target_pairs={{0,64},{64,128},{128,192},{192,0},{1,65},{65,129},{129,193},{193,1... | collective-permute-start | bytes 2752520 | tf_op jit(solution)/shard_map/ppermute | solution.py:26
  63.1 13.7 %collective-permute-start.17 = (bf16[2688,128]{1,0:T(8,128)(2,1)S(1)}, bf16[2688,128]{1,0:T(8,128)(2,1)S(1)}, u32[]{:S(2)}, u32[]{:S(2)}) collective-permute-start(bf16[2688,128]{1,0:T(8,128)(2,1)S(1)} %pad_maximum_fusion.4), channel_id=1, source_target_pairs={{0,192},{64,0},{128,64},{192,128},{1,193},{65,1},{129,65},{193,129... | collective-permute-start | bytes 2064392 | tf_op jit(solution)/shard_map/ppermute | solution.py:26
  83.6 14.2 %collective-permute-start.21 = (bf16[2688,128]{1,0:T(8,128)(2,1)S(1)}, bf16[2688,128]{1,0:T(8,128)(2,1)S(1)}, u32[]{:S(2)}, u32[]{:S(2)}) collective-permute-start(bf16[2688,128]{1,0:T(8,128)(2,1)S(1)} %get-tuple-element.101), channel_id=1, source_target_pairs={{0,192},{64,0},{128,64},{192,128},{1,193},{65,1},{129,65},{193,129... | collective-permute-start | bytes 2064392 | tf_op jit(solution)/shard_map/ppermute | solution.py:26
  84.5 13.3 %collective-permute-start.20 = (bf16[2688,128]{1,0:T(8,128)(2,1)S(1)}, bf16[2688,128]{1,0:T(8,128)(2,1)S(1)}, u32[]{:S(2)}, u32[]{:S(2)}) collective-permute-start(bf16[2688,128]{1,0:T(8,128)(2,1)S(1)} %get-tuple-element.102), channel_id=1, source_target_pairs={{0,64},{64,128},{128,192},{192,0},{1,65},{65,129},{129,193},{193,1... | collective-permute-start | bytes 2064392 | tf_op jit(solution)/shard_map/ppermute | solution.py:26
  85.2 12.6 %collective-permute-start.18 = (bf16[2560,128]{1,0:T(8,128)(2,1)S(1)}, bf16[2560,128]{1,0:T(8,128)(2,1)S(1)}, u32[]{:S(2)}, u32[]{:S(2)}) collective-permute-start(bf16[2560,128]{1,0:T(8,128)(2,1)S(1)} %slice.124), channel_id=1, source_target_pairs={{0,8},{8,16},{16,24},{24,32},{32,40},{40,48},{48,56},{56,0},{1,9},... | collective-permute-start | bytes 1966088 | tf_op jit(solution)/shard_map/ppermute | solution.py:26
  85.5 12.2 %collective-permute-start.19 = (bf16[2560,128]{1,0:T(8,128)(2,1)S(1)}, bf16[2560,128]{1,0:T(8,128)(2,1)S(1)}, u32[]{:S(2)}, u32[]{:S(2)}) collective-permute-start(bf16[2560,128]{1,0:T(8,128)(2,1)S(1)} %slice.125), channel_id=1, source_target_pairs={{0,56},{8,0},{16,8},{24,16},{32,24},{40,32},{48,40},{56,48},{1,57}... | collective-permute-start | bytes 1966088 | tf_op jit(solution)/shard_map/ppermute | solution.py:26
  97.9 6.2 %collective-permute-start.23 = (bf16[256,128]{1,0:T(8,128)(2,1)S(1)}, bf16[256,128]{1,0:T(8,128)(2,1)S(1)}, u32[]{:S(2)}, u32[]{:S(2)}) collective-permute-start(bf16[256,128]{1,0:T(8,128)(2,1)S(1)} %pad_maximum_fusion.10), channel_id=1, source_target_pairs={{0,8},{8,16},{16,24},{24,32},{32,40},{40,48},{48,56},{56,0},{1,9},... | collective-permute-start | bytes 196616 | tf_op jit(solution)/shard_map/ppermute | solution.py:26
  98.4 5.7 %collective-permute-start.24 = (bf16[256,128]{1,0:T(8,128)(2,1)S(1)}, bf16[256,128]{1,0:T(8,128)(2,1)S(1)}, u32[]{:S(2)}, u32[]{:S(2)}) collective-permute-start(bf16[256,128]{1,0:T(8,128)(2,1)S(1)} %pad_maximum_fusion.11), channel_id=1, source_target_pairs={{0,56},{8,0},{16,8},{24,16},{32,24},{40,32},{48,40},{56,48},{1,57}... | collective-permute-start | bytes 196616 | tf_op jit(solution)/shard_map/ppermute | solution.py:26
  100.7 6.2 %collective-permute-start.22 = (bf16[896,128]{1,0:T(8,128)(2,1)S(1)}, bf16[896,128]{1,0:T(8,128)(2,1)S(1)}, u32[]{:S(2)}, u32[]{:S(2)}) collective-permute-start(bf16[896,128]{1,0:T(8,128)(2,1)S(1)} %slice.131), channel_id=1, source_target_pairs={{0,64},{64,128},{128,192},{192,0},{1,65},{65,129},{129,193},{193,1... | collective-permute-start | bytes 688136 | tf_op jit(solution)/shard_map/ppermute | solution.py:26
  101.0 18.1 %collective-permute-start.25 = (bf16[1024,128]{1,0:T(8,128)(2,1)S(1)}, bf16[1024,128]{1,0:T(8,128)(2,1)S(1)}, u32[]{:S(2)}, u32[]{:S(2)}) collective-permute-start(bf16[1024,128]{1,0:T(8,128)(2,1)S(1)} %pad_maximum_fusion.6), channel_id=1, source_target_pairs={{0,8},{8,16},{16,24},{24,32},{32,40},{40,48},{48,56},{56,0},{1,9},... | collective-permute-start | bytes 786440 | tf_op jit(solution)/shard_map/ppermute | solution.py:26
  101.2 18.0 %collective-permute-start.26 = (bf16[1024,128]{1,0:T(8,128)(2,1)S(1)}, bf16[1024,128]{1,0:T(8,128)(2,1)S(1)}, u32[]{:S(2)}, u32[]{:S(2)}) collective-permute-start(bf16[1024,128]{1,0:T(8,128)(2,1)S(1)} %pad_maximum_fusion.7), channel_id=1, source_target_pairs={{0,56},{8,0},{16,8},{24,16},{32,24},{40,32},{48,40},{56,48},{1,57}... | collective-permute-start | bytes 786440 | tf_op jit(solution)/shard_map/ppermute | solution.py:26
  119.2 8.3 %collective-permute-start.28 = (bf16[512,512]{1,0:T(8,128)(2,1)}, bf16[512,512]{1,0:T(8,128)(2,1)S(1)}, u32[]{:S(2)}, u32[]{:S(2)}) collective-permute-start(bf16[512,512]{1,0:T(8,128)(2,1)} %shard_map.64.a_ref), channel_id=1, source_target_pairs={{0,6},{2,0},{4,2},{6,4},{1,7},{3,1},{5,3},{7,5},{8,14},{10,8},{12,... | collective-permute-start | bytes 1572872 | tf_op jit(solution)/shard_map/ppermute | solution.py:26
  119.3 9.5 %collective-permute-start.27 = (bf16[512,512]{1,0:T(8,128)(2,1)}, bf16[512,512]{1,0:T(8,128)(2,1)S(1)}, u32[]{:S(2)}, u32[]{:S(2)}) collective-permute-start(bf16[512,512]{1,0:T(8,128)(2,1)} %shard_map.64.a_ref), channel_id=1, source_target_pairs={{0,2},{2,4},{4,6},{6,0},{1,3},{3,5},{5,7},{7,1},{8,10},{10,12},{12... | collective-permute-start | bytes 1572872 | tf_op jit(solution)/shard_map/ppermute | solution.py:26
  128.8 9.6 %collective-permute-start.29 = (bf16[256,512]{1,0:T(8,128)(2,1)S(1)}, bf16[256,512]{1,0:T(8,128)(2,1)S(1)}, u32[]{:S(2)}, u32[]{:S(2)}) collective-permute-start(bf16[256,512]{1,0:T(8,128)(2,1)S(1)} %slice.140), channel_id=1, source_target_pairs={{0,2},{2,4},{4,6},{6,0},{1,3},{3,5},{5,7},{7,1},{8,10},{10,12},{12... | collective-permute-start | bytes 786440 | tf_op jit(solution)/shard_map/ppermute | solution.py:26
  129.4 9.0 %collective-permute-start.30 = (bf16[256,512]{1,0:T(8,128)(2,1)S(1)}, bf16[256,512]{1,0:T(8,128)(2,1)S(1)}, u32[]{:S(2)}, u32[]{:S(2)}) collective-permute-start(bf16[256,512]{1,0:T(8,128)(2,1)S(1)} %slice.141), channel_id=1, source_target_pairs={{0,6},{2,0},{4,2},{6,4},{1,7},{3,1},{5,3},{7,5},{8,14},{10,8},{12,... | collective-permute-start | bytes 786440 | tf_op jit(solution)/shard_map/ppermute | solution.py:26
  138.9 12.0 %collective-permute-start.31 = (bf16[512,512]{1,0:T(8,128)(2,1)S(1)}, bf16[512,512]{1,0:T(8,128)(2,1)S(1)}, u32[]{:S(2)}, u32[]{:S(2)}) collective-permute-start(bf16[512,512]{1,0:T(8,128)(2,1)S(1)} %shard_map.68), channel_id=1, source_target_pairs={{0,1},{1,0},{2,3},{3,2},{4,5},{5,4},{6,7},{7,6},{8,9},{9,8},{10,11... | collective-permute-start | bytes 1572872 | tf_op jit(solution)/shard_map/ppermute | solution.py:26
  (31 other events, 281.5 us)

commit v5 on v3

--- a/solution.py
+++ b/solution.py
@@ -17,7 +17,7 @@
 ARRAYS = ("kv", "z1m", "z1p", "z2m", "z2p", "s1m", "s1p", "s2p", "g0p", "g0m")
 ARRAYS += ("gap", "gam", "gbp", "gbm", "gcp", "gcm", "gdp")
 HALF = BLK // 2
-ZROWS = 896
+ZROWS = 880
 ZVALUES = ZROWS - BLK
 LAST = BLK - ZVALUES
 SLOT = LAST + BLK

time: 151 us -> 151 us (level)
  no operation moved by 1% of the time
where the time goes in v5:
time: 151 us
  starting transfers between devices  60.6 us (40%)
  waiting for transfers between devices  59.2 us (39%)
  Pallas kernels  19.4 us (13%)
  local copies, waits for them, and re-layouts  7.99 us (5%)
  other arithmetic  2.94 us (2%)
    ppermute x29, waiting for transfers between devices, shift(): return lax.ppermute(v, axis, [(i, (i + d) % n) for i in range(n)])  59.2 us
    ppermute x29, starting transfers between devices, shift(): return lax.ppermute(v, axis, [(i, (i + d) % n) for i in range(n)])  59.1 us
    pallas_call x5, Pallas kernels, call(): pl.pallas_call(kernel, out_shape=out_shape, in_specs=spec(pltpu.SMEM, sca...  19.4 us
    unnamed x64, local copies, waits for them, and re-layouts  6.04 us
  transfers between devices with their start and end apart: 30, of which 15 were waited for; matrix products, arithmetic and copies ran while one was open for 2% of the time, Pallas kernels for 5%

profile of v5, /device:TPU:1, one launch (start us, length us, event | category | flops | bytes accessed | tf_op | source)
XLA Modules:
  0.0 150.7 jit_solution(1292545353710260762)
XLA Ops:
  1.0 2.5 %collective-permute-start = (bf16[1024,128]{1,0:T(8,128)(2,1)S(1)}, bf16[1024,128]{1,0:T(8,128)(2,1)S(1)}, u32[]{:S(2)}, u32[]{:S(2)}) collective-permute-start(bf16[1024,128]{1,0:T(8,128)(2,1)S(1)} %bitcast.11), channel_id=1, source_target_pairs={{0,8},{8,16},{16,24},{24,32},{32,40},{40,48},{48,56},{56,0},{1,9},... | collective-permute-start | bytes 786440 | tf_op jit(solution)/shard_map/ppermute | solution.py:26
  3.6 4.0 %collective-permute-start.1 = (bf16[1024,128]{1,0:T(8,128)(2,1)S(1)}, bf16[1024,128]{1,0:T(8,128)(2,1)S(1)}, u32[]{:S(2)}, u32[]{:S(2)}) collective-permute-start(bf16[1024,128]{1,0:T(8,128)(2,1)S(1)} %bitcast.12), channel_id=1, source_target_pairs={{0,56},{8,0},{16,8},{24,16},{32,24},{40,32},{48,40},{56,48},{1,57}... | collective-permute-start | bytes 786440 | tf_op jit(solution)/shard_map/ppermute | solution.py:26
  7.6 1.3 collective-permute-start.2
  8.9 1.4 collective-permute-start.3
  10.3 1.6 %collective-permute-start.4 = (bf16[512,128]{1,0:T(8,128)(2,1)}, bf16[512,128]{1,0:T(8,128)(2,1)S(1)}, u32[]{:S(2)}, u32[]{:S(2)}) collective-permute-start(bf16[512,128]{1,0:T(8,128)(2,1)} %param.10), channel_id=1, source_target_pairs={{0,0},{1,1},{2,64},{3,65},{4,128},{5,129},{6,192},{7,193},{8,8},{9... | collective-permute-start | bytes 393224 | tf_op jit(solution)/shard_map/ppermute | solution.py:64
  13.5 2.2 %collective-permute-done.2.rest_8_ = bf16[1024,128]{1,0:T(8,128)(2,1)S(1)} collective-permute-done((bf16[1024,128]{1,0:T(8,128)(2,1)S(1)}, bf16[1024,128]{1,0:T(8,128)(2,1)S(1)}, u32[]{:S(2)}, u32[]{:S(2)}) %collective-permute-start.2) | collective-permute-done | bytes 262176 | tf_op jit(solution)/shard_map/ppermute | solution.py:26
  15.9 2.7 %collective-permute-start.9 = (bf16[1024,128]{1,0:T(8,128)(2,1)S(1)}, bf16[1024,128]{1,0:T(8,128)(2,1)S(1)}, u32[]{:S(2)}, u32[]{:S(2)}) collective-permute-start(bf16[1024,128]{1,0:T(8,128)(2,1)S(1)} %collective-permute-done.1.rest_1_), channel_id=1, source_target_pairs={{0,56},{8,0},{16,8},{24,16},{32,24},{40,32},{48,40},{56,48},{1,57}... | collective-permute-start | bytes 786440 | tf_op jit(solution)/shard_map/ppermute | solution.py:26
  18.6 6.4 %collective-permute-start.7 = (bf16[512,128]{1,0:T(8,128)(2,1)S(1)}, bf16[512,128]{1,0:T(8,128)(2,1)S(1)}, u32[]{:S(2)}, u32[]{:S(2)}) collective-permute-start(bf16[512,128]{1,0:T(8,128)(2,1)S(1)} %collective-permute-done.4), channel_id=1, source_target_pairs={{0,128},{64,192},{128,0},{192,64},{1,129},{65,193},{129,1},{193,65... | collective-permute-start | bytes 393224 | tf_op jit(solution)/shard_map/ppermute | solution.py:26
  25.1 3.4 %collective-permute-start.5 = (bf16[584,128]{1,0:T(8,128)(2,1)S(1)}, bf16[584,128]{1,0:T(8,128)(2,1)S(1)}, u32[]{:S(2)}, u32[]{:S(2)}) collective-permute-start(bf16[584,128]{1,0:T(8,128)(2,1)S(1)} %get-tuple-element.76), channel_id=1, source_target_pairs={{0,64},{64,128},{128,192},{192,0},{1,65},{65,129},{129,193},{193,1... | collective-permute-start | bytes 448520 | tf_op jit(solution)/shard_map/ppermute | solution.py:26
  28.5 3.7 %collective-permute-done.5 = bf16[584,128]{1,0:T(8,128)(2,1)S(1)} collective-permute-done((bf16[584,128]{1,0:T(8,128)(2,1)S(1)}, bf16[584,128]{1,0:T(8,128)(2,1)S(1)}, u32[]{:S(2)}, u32[]{:S(2)}) %collective-permute-start.5) | collective-permute-done | bytes 149536 | tf_op jit(solution)/shard_map/ppermute | solution.py:26
  32.2 1.9 %collective-permute-done.6 = bf16[584,128]{1,0:T(8,128)(2,1)S(1)} collective-permute-done((bf16[584,128]{1,0:T(8,128)(2,1)S(1)}, bf16[584,128]{1,0:T(8,128)(2,1)S(1)}, u32[]{:S(2)}, u32[]{:S(2)}) %collective-permute-start.6) | collective-permute-done | bytes 149536 | tf_op jit(solution)/shard_map/ppermute | solution.py:26
  35.6 2.1 %collective-permute-start.13 = (bf16[3520,128]{1,0:T(8,128)(2,1)S(1)}, bf16[3520,128]{1,0:T(8,128)(2,1)S(1)}, u32[]{:S(2)}, u32[]{:S(2)}) collective-permute-start(bf16[3520,128]{1,0:T(8,128)(2,1)S(1)} %pad_maximum_fusion), channel_id=1, source_target_pairs={{0,192},{64,0},{128,64},{192,128},{1,193},{65,1},{129,65},{193,129... | collective-permute-start | bytes 2703368 | tf_op jit(solution)/shard_map/ppermute | solution.py:26
  37.8 1.5 collective-permute-start.10
  39.2 17.2 %collective-permute-done.11.rest_5_.rest_18_.rest_1_ = bf16[3504,128]{1,0:T(8,128)(2,1)S(1)} collective-permute-done((bf16[3504,128]{1,0:T(8,128)(2,1)S(1)}, bf16[3504,128]{1,0:T(8,128)(2,1)S(1)}, u32[]{:S(2)}, u32[]{:S(2)}) %collective-permute-start.11) | collective-permute-done | bytes 897056 | tf_op jit(solution)/shard_map/ppermute | solution.py:26
  57.8 2.7 %collective-permute-start.15 = (bf16[3504,128]{1,0:T(8,128)(2,1)S(1)}, bf16[3504,128]{1,0:T(8,128)(2,1)S(1)}, u32[]{:S(2)}, u32[]{:S(2)}) collective-permute-start(bf16[3504,128]{1,0:T(8,128)(2,1)S(1)} %collective-permute-done.11.rest_5_.rest_18_.rest_1_), channel_id=1, source_target_pairs={{0,56},{8,0},{16,8},{24,16},{32,24},{40,32},{48,40},{56,48},{1,57}... | collective-permute-start | bytes 2691080 | tf_op jit(solution)/shard_map/ppermute | solution.py:26
  60.8 2.7 %collective-permute-start.17 = (bf16[2640,128]{1,0:T(8,128)(2,1)S(1)}, bf16[2640,128]{1,0:T(8,128)(2,1)S(1)}, u32[]{:S(2)}, u32[]{:S(2)}) collective-permute-start(bf16[2640,128]{1,0:T(8,128)(2,1)S(1)} %pad_maximum_fusion.4), channel_id=1, source_target_pairs={{0,192},{64,0},{128,64},{192,128},{1,193},{65,1},{129,65},{193,129... | collective-permute-start | bytes 2027528 | tf_op jit(solution)/shard_map/ppermute | solution.py:26
  63.5 9.7 %collective-permute-done.17.rest_13_ = bf16[2640,128]{1,0:T(8,128)(2,1)S(1)} collective-permute-done((bf16[2640,128]{1,0:T(8,128)(2,1)S(1)}, bf16[2640,128]{1,0:T(8,128)(2,1)S(1)}, u32[]{:S(2)}, u32[]{:S(2)}) %collective-permute-start.17) | collective-permute-done | bytes 675872 | tf_op jit(solution)/shard_map/ppermute | solution.py:26
  73.2 3.0 %collective-permute-done.14.rest_7_.rest_23_.rest_6_ = bf16[3504,128]{1,0:T(8,128)(2,1)S(1)} collective-permute-done((bf16[3504,128]{1,0:T(8,128)(2,1)S(1)}, bf16[3504,128]{1,0:T(8,128)(2,1)S(1)}, u32[]{:S(2)}, u32[]{:S(2)}) %collective-permute-start.14) | collective-permute-done | bytes 897056 | tf_op jit(solution)/shard_map/ppermute | solution.py:26
  76.3 2.7 %collective-permute-done.16.rest_12_ = bf16[3520,128]{1,0:T(8,128)(2,1)S(1)} collective-permute-done((bf16[3520,128]{1,0:T(8,128)(2,1)S(1)}, bf16[3520,128]{1,0:T(8,128)(2,1)S(1)}, u32[]{:S(2)}, u32[]{:S(2)}) %collective-permute-start.16) | collective-permute-done | bytes 901152 | tf_op jit(solution)/shard_map/ppermute | solution.py:26
  79.9 2.7 %collective-permute-start.21 = (bf16[2640,128]{1,0:T(8,128)(2,1)S(1)}, bf16[2640,128]{1,0:T(8,128)(2,1)S(1)}, u32[]{:S(2)}, u32[]{:S(2)}) collective-permute-start(bf16[2640,128]{1,0:T(8,128)(2,1)S(1)} %get-tuple-element.73), channel_id=1, source_target_pairs={{0,192},{64,0},{128,64},{192,128},{1,193},{65,1},{129,65},{193,129... | collective-permute-start | bytes 2027528 | tf_op jit(solution)/shard_map/ppermute | solution.py:26
  82.8 2.7 %collective-permute-start.19 = (bf16[2624,128]{1,0:T(8,128)(2,1)S(1)}, bf16[2624,128]{1,0:T(8,128)(2,1)S(1)}, u32[]{:S(2)}, u32[]{:S(2)}) collective-permute-start(bf16[2624,128]{1,0:T(8,128)(2,1)S(1)} %slice.107), channel_id=1, source_target_pairs={{0,56},{8,0},{16,8},{24,16},{32,24},{40,32},{48,40},{56,48},{1,57}... | collective-permute-start | bytes 2015240 | tf_op jit(solution)/shard_map/ppermute | solution.py:26
  85.5 9.0 %collective-permute-done.18.rest_22_.rest_5_ = bf16[2624,128]{1,0:T(8,128)(2,1)S(1)} collective-permute-done((bf16[2624,128]{1,0:T(8,128)(2,1)S(1)}, bf16[2624,128]{1,0:T(8,128)(2,1)S(1)}, u32[]{:S(2)}, u32[]{:S(2)}) %collective-permute-start.18) | collective-permute-done | bytes 671776 | tf_op jit(solution)/shard_map/ppermute | solution.py:26
  94.7 2.7 %collective-permute-start.24 = (bf16[1312,128]{1,0:T(8,128)(2,1)S(1)}, bf16[1312,128]{1,0:T(8,128)(2,1)S(1)}, u32[]{:S(2)}, u32[]{:S(2)}) collective-permute-start(bf16[1312,128]{1,0:T(8,128)(2,1)S(1)} %slice.115), channel_id=1, source_target_pairs={{0,56},{8,0},{16,8},{24,16},{32,24},{40,32},{48,40},{56,48},{1,57}... | collective-permute-start | bytes 1007624 | tf_op jit(solution)/shard_map/ppermute | solution.py:26
  98.4 5.4 %collective-permute-done.22.rest_16_ = bf16[880,128]{1,0:T(8,128)(2,1)S(1)} collective-permute-done((bf16[880,128]{1,0:T(8,128)(2,1)S(1)}, bf16[880,128]{1,0:T(8,128)(2,1)S(1)}, u32[]{:S(2)}, u32[]{:S(2)}) %collective-permute-start.22) | collective-permute-done | bytes 225312 | tf_op jit(solution)/shard_map/ppermute | solution.py:26
  105.8 11.6 %shard_map.64.a_ref = bf16[512,512]{1,0:T(8,128)(2,1)} custom-call(s32[12]{0:T(128)} %reshape.8.route_ref, s32[2]{0:T(128)} %pad_add_fusion.place_ref, s32[32]{0:T(128)} %constant.58.clone.table_ref, bf16[512,512]{1,0:T(8,128)(2,1)} %q_ref.1, bf16[512,128]{1,0:T(8,128)(2,1)} %k_ref.1, bf16[512,128]{1,0:T(8,128)(2,1)} %v_ref.1, bf16[1024,128]{1,0:T(8,128)(2,1)} %bitcast.16, ...), custom_call_target="tpu_custom_call" | custom-call | flops 3221225472 | bytes 8388608 | tf_op jit(solution)/shard_map/pallas_call | solution.py:213
  117.5 2.7 %collective-permute-start.26 = (bf16[512,512]{1,0:T(8,128)(2,1)}, bf16[512,512]{1,0:T(8,128)(2,1)S(1)}, u32[]{:S(2)}, u32[]{:S(2)}) collective-permute-start(bf16[512,512]{1,0:T(8,128)(2,1)} %shard_map.64.a_ref), channel_id=1, source_target_pairs={{0,6},{2,0},{4,2},{6,4},{1,7},{3,1},{5,3},{7,5},{8,14},{10,8},{12,... | collective-permute-start | bytes 1572872 | tf_op jit(solution)/shard_map/ppermute | solution.py:26
  120.2 5.7 %shard_map.65 = (f32[512,1024]{1,0:T(8,128)}, bf16[2,8,512,128]{3,2,1,0:T(8,128)(2,1)}, bf16[8,512,128]{2,1,0:T(8,128)(2,1)}) custom-call(s32[5]{0:T(128)} %stack.42.at_ref, bf16[512,512]{1,0:T(8,128)(2,1)} %shard_map.64.a_ref, bf16[3504,128]{1,0:T(8,128)(2,1)} %copy-done.7, bf16[3504,128]{1,0:T(8,128)(2,1)} %copy-done.5, bf16[3504,128]{1,0:T(8,128)(2,1)} %copy-done.8, ...), custom_call_target="tpu_custom_call" | custom-call | flops 536870912 | bytes 8388608 | tf_op jit(solution)/shard_map/pallas_call | solution.py:213
  127.3 2.5 %collective-permute-start.28 = (bf16[256,512]{1,0:T(8,128)(2,1)S(1)}, bf16[256,512]{1,0:T(8,128)(2,1)S(1)}, u32[]{:S(2)}, u32[]{:S(2)}) collective-permute-start(bf16[256,512]{1,0:T(8,128)(2,1)S(1)} %slice.117), channel_id=1, source_target_pairs={{0,6},{2,0},{4,2},{6,4},{1,7},{3,1},{5,3},{7,5},{8,14},{10,8},{12,... | collective-permute-start | bytes 786440 | tf_op jit(solution)/shard_map/ppermute | solution.py:26
  129.8 1.6 %copy-done.2 = f32[512,1024]{1,0:T(8,128)S(1)} copy-done((f32[512,1024]{1,0:T(8,128)S(1)}, f32[512,1024]{1,0:T(8,128)}, u32[]{:S(2)}) %copy-start.2) | copy-done | bytes 2097176
  131.4 1.6 %copy-done.3 = bf16[2,8,512,128]{3,2,1,0:T(8,128)(2,1)S(1)} copy-done((bf16[2,8,512,128]{3,2,1,0:T(8,128)(2,1)S(1)}, bf16[2,8,512,128]{3,2,1,0:T(8,128)(2,1)}, u32[]{:S(2)}) %copy-start.3) | copy-done | bytes 2097176
  133.0 1.2 shard_map.66.total_ref
  135.3 13.0 %collective-permute-start.29 = (bf16[512,512]{1,0:T(8,128)(2,1)S(1)}, bf16[512,512]{1,0:T(8,128)(2,1)S(1)}, u32[]{:S(2)}, u32[]{:S(2)}) collective-permute-start(bf16[512,512]{1,0:T(8,128)(2,1)S(1)} %shard_map.68), channel_id=1, source_target_pairs={{0,1},{1,0},{2,3},{3,2},{4,5},{5,4},{6,7},{7,6},{8,9},{9,8},{10,11... | collective-permute-start | bytes 1572872 | tf_op jit(solution)/shard_map/ppermute | solution.py:26
  (133 shorter events, 15.1 us)
Async XLA Ops:
  1.0 33.3 %copy-start.18 = (bf16[2,512,128]{2,1,0:T(8,128)(2,1)}, bf16[2,512,128]{2,1,0:T(8,128)(2,1)S(1)}, u32[]{:S(2)}) copy-start(bf16[2,512,128]{2,1,0:T(8,128)(2,1)S(1)} %pad_maximum_fusion.5) | copy-start | bytes 786436
  1.0 12.5 %collective-permute-start = (bf16[1024,128]{1,0:T(8,128)(2,1)S(1)}, bf16[1024,128]{1,0:T(8,128)(2,1)S(1)}, u32[]{:S(2)}, u32[]{:S(2)}) collective-permute-start(bf16[1024,128]{1,0:T(8,128)(2,1)S(1)} %bitcast.11), channel_id=1, source_target_pairs={{0,8},{8,16},{16,24},{24,32},{32,40},{40,48},{48,56},{56,0},{1,9},... | collective-permute-start | bytes 786440 | tf_op jit(solution)/shard_map/ppermute | solution.py:26
  3.6 10.0 %collective-permute-start.1 = (bf16[1024,128]{1,0:T(8,128)(2,1)S(1)}, bf16[1024,128]{1,0:T(8,128)(2,1)S(1)}, u32[]{:S(2)}, u32[]{:S(2)}) collective-permute-start(bf16[1024,128]{1,0:T(8,128)(2,1)S(1)} %bitcast.12), channel_id=1, source_target_pairs={{0,56},{8,0},{16,8},{24,16},{32,24},{40,32},{48,40},{56,48},{1,57}... | collective-permute-start | bytes 786440 | tf_op jit(solution)/shard_map/ppermute | solution.py:26
  7.6 8.2 %collective-permute-start.2 = (bf16[1024,128]{1,0:T(8,128)(2,1)S(1)}, bf16[1024,128]{1,0:T(8,128)(2,1)S(1)}, u32[]{:S(2)}, u32[]{:S(2)}) collective-permute-start(bf16[1024,128]{1,0:T(8,128)(2,1)S(1)} %bitcast.13), channel_id=1, source_target_pairs={{0,64},{64,128},{128,192},{192,0},{1,65},{65,129},{129,193},{193,1... | collective-permute-start | bytes 786440 | tf_op jit(solution)/shard_map/ppermute | solution.py:26
  8.9 6.9 %collective-permute-start.3 = (bf16[1024,128]{1,0:T(8,128)(2,1)S(1)}, bf16[1024,128]{1,0:T(8,128)(2,1)S(1)}, u32[]{:S(2)}, u32[]{:S(2)}) collective-permute-start(bf16[1024,128]{1,0:T(8,128)(2,1)S(1)} %bitcast.14), channel_id=1, source_target_pairs={{0,192},{64,0},{128,64},{192,128},{1,193},{65,1},{129,65},{193,129... | collective-permute-start | bytes 786440 | tf_op jit(solution)/shard_map/ppermute | solution.py:26
  10.3 3.1 %collective-permute-start.4 = (bf16[512,128]{1,0:T(8,128)(2,1)}, bf16[512,128]{1,0:T(8,128)(2,1)S(1)}, u32[]{:S(2)}, u32[]{:S(2)}) collective-permute-start(bf16[512,128]{1,0:T(8,128)(2,1)} %param.10), channel_id=1, source_target_pairs={{0,0},{1,1},{2,64},{3,65},{4,128},{5,129},{6,192},{7,193},{8,8},{9... | collective-permute-start | bytes 393224 | tf_op jit(solution)/shard_map/ppermute | solution.py:64
  15.8 18.3 %collective-permute-start.8 = (bf16[1024,128]{1,0:T(8,128)(2,1)S(1)}, bf16[1024,128]{1,0:T(8,128)(2,1)S(1)}, u32[]{:S(2)}, u32[]{:S(2)}) collective-permute-start(bf16[1024,128]{1,0:T(8,128)(2,1)S(1)} %collective-permute-done.rest_2_), channel_id=1, source_target_pairs={{0,8},{8,16},{16,24},{24,32},{32,40},{40,48},{48,56},{56,0},{1,9},... | collective-permute-start | bytes 786440 | tf_op jit(solution)/shard_map/ppermute | solution.py:26
  15.9 18.2 %collective-permute-start.9 = (bf16[1024,128]{1,0:T(8,128)(2,1)S(1)}, bf16[1024,128]{1,0:T(8,128)(2,1)S(1)}, u32[]{:S(2)}, u32[]{:S(2)}) collective-permute-start(bf16[1024,128]{1,0:T(8,128)(2,1)S(1)} %collective-permute-done.1.rest_1_), channel_id=1, source_target_pairs={{0,56},{8,0},{16,8},{24,16},{32,24},{40,32},{48,40},{56,48},{1,57}... | collective-permute-start | bytes 786440 | tf_op jit(solution)/shard_map/ppermute | solution.py:26
  18.6 9.9 %collective-permute-start.7 = (bf16[512,128]{1,0:T(8,128)(2,1)S(1)}, bf16[512,128]{1,0:T(8,128)(2,1)S(1)}, u32[]{:S(2)}, u32[]{:S(2)}) collective-permute-start(bf16[512,128]{1,0:T(8,128)(2,1)S(1)} %collective-permute-done.4), channel_id=1, source_target_pairs={{0,128},{64,192},{128,0},{192,64},{1,129},{65,193},{129,1},{193,65... | collective-permute-start | bytes 393224 | tf_op jit(solution)/shard_map/ppermute | solution.py:26
  25.1 7.1 %collective-permute-start.5 = (bf16[584,128]{1,0:T(8,128)(2,1)S(1)}, bf16[584,128]{1,0:T(8,128)(2,1)S(1)}, u32[]{:S(2)}, u32[]{:S(2)}) collective-permute-start(bf16[584,128]{1,0:T(8,128)(2,1)S(1)} %get-tuple-element.76), channel_id=1, source_target_pairs={{0,64},{64,128},{128,192},{192,0},{1,65},{65,129},{129,193},{193,1... | collective-permute-start | bytes 448520 | tf_op jit(solution)/shard_map/ppermute | solution.py:26
  28.5 5.6 %collective-permute-start.6 = (bf16[584,128]{1,0:T(8,128)(2,1)S(1)}, bf16[584,128]{1,0:T(8,128)(2,1)S(1)}, u32[]{:S(2)}, u32[]{:S(2)}) collective-permute-start(bf16[584,128]{1,0:T(8,128)(2,1)S(1)} %get-tuple-element.75), channel_id=1, source_target_pairs={{0,192},{64,0},{128,64},{192,128},{1,193},{65,1},{129,65},{193,129... | collective-permute-start | bytes 448520 | tf_op jit(solution)/shard_map/ppermute | solution.py:26
  34.9 25.6 %copy-start.7 = (bf16[3504,128]{1,0:T(8,128)(2,1)}, bf16[3504,128]{1,0:T(8,128)(2,1)S(1)}, u32[]{:S(2)}) copy-start(bf16[3504,128]{1,0:T(8,128)(2,1)S(1)} %get-tuple-element.72.rest_17_.rest_0_) | copy-start | bytes 2691076
  35.0 22.4 %collective-permute-start.12 = (bf16[3520,128]{1,0:T(8,128)(2,1)S(1)}, bf16[3520,128]{1,0:T(8,128)(2,1)S(1)}, u32[]{:S(2)}, u32[]{:S(2)}) collective-permute-start(bf16[3520,128]{1,0:T(8,128)(2,1)S(1)} %pad_maximum_fusion), channel_id=1, source_target_pairs={{0,64},{64,128},{128,192},{192,0},{1,65},{65,129},{129,193},{193,1... | collective-permute-start | bytes 2703368 | tf_op jit(solution)/shard_map/ppermute | solution.py:26
  35.6 21.8 %collective-permute-start.13 = (bf16[3520,128]{1,0:T(8,128)(2,1)S(1)}, bf16[3520,128]{1,0:T(8,128)(2,1)S(1)}, u32[]{:S(2)}, u32[]{:S(2)}) collective-permute-start(bf16[3520,128]{1,0:T(8,128)(2,1)S(1)} %pad_maximum_fusion), channel_id=1, source_target_pairs={{0,192},{64,0},{128,64},{192,128},{1,193},{65,1},{129,65},{193,129... | collective-permute-start | bytes 2703368 | tf_op jit(solution)/shard_map/ppermute | solution.py:26
  37.8 18.7 %collective-permute-start.11 = (bf16[3504,128]{1,0:T(8,128)(2,1)S(1)}, bf16[3504,128]{1,0:T(8,128)(2,1)S(1)}, u32[]{:S(2)}, u32[]{:S(2)}) collective-permute-start(bf16[3504,128]{1,0:T(8,128)(2,1)S(1)} %get-tuple-element.70), channel_id=1, source_target_pairs={{0,56},{8,0},{16,8},{24,16},{32,24},{40,32},{48,40},{56,48},{1,57}... | collective-permute-start | bytes 2691080 | tf_op jit(solution)/shard_map/ppermute | solution.py:26
  37.8 19.6 %collective-permute-start.10 = (bf16[3504,128]{1,0:T(8,128)(2,1)S(1)}, bf16[3504,128]{1,0:T(8,128)(2,1)S(1)}, u32[]{:S(2)}, u32[]{:S(2)}) collective-permute-start(bf16[3504,128]{1,0:T(8,128)(2,1)S(1)} %get-tuple-element.72.rest_17_.rest_0_), channel_id=1, source_target_pairs={{0,8},{8,16},{16,24},{24,32},{32,40},{40,48},{48,56},{56,0},{1,9},... | collective-permute-start | bytes 2691080 | tf_op jit(solution)/shard_map/ppermute | solution.py:26
  57.5 18.8 %collective-permute-start.14 = (bf16[3504,128]{1,0:T(8,128)(2,1)S(1)}, bf16[3504,128]{1,0:T(8,128)(2,1)S(1)}, u32[]{:S(2)}, u32[]{:S(2)}) collective-permute-start(bf16[3504,128]{1,0:T(8,128)(2,1)S(1)} %collective-permute-done.10.rest_6_.rest_24_.rest_7_), channel_id=1, source_target_pairs={{0,8},{8,16},{16,24},{24,32},{32,40},{40,48},{48,56},{56,0},{1,9},... | collective-permute-start | bytes 2691080 | tf_op jit(solution)/shard_map/ppermute | solution.py:26
  57.8 18.5 %collective-permute-start.15 = (bf16[3504,128]{1,0:T(8,128)(2,1)S(1)}, bf16[3504,128]{1,0:T(8,128)(2,1)S(1)}, u32[]{:S(2)}, u32[]{:S(2)}) collective-permute-start(bf16[3504,128]{1,0:T(8,128)(2,1)S(1)} %collective-permute-done.11.rest_5_.rest_18_.rest_1_), channel_id=1, source_target_pairs={{0,56},{8,0},{16,8},{24,16},{32,24},{40,32},{48,40},{56,48},{1,57}... | collective-permute-start | bytes 2691080 | tf_op jit(solution)/shard_map/ppermute | solution.py:26
  60.6 18.3 %collective-permute-start.16 = (bf16[3520,128]{1,0:T(8,128)(2,1)S(1)}, bf16[3520,128]{1,0:T(8,128)(2,1)S(1)}, u32[]{:S(2)}, u32[]{:S(2)}) collective-permute-start(bf16[3520,128]{1,0:T(8,128)(2,1)S(1)} %pad_maximum_fusion.1), channel_id=1, source_target_pairs={{0,64},{64,128},{128,192},{192,0},{1,65},{65,129},{129,193},{193,1... | collective-permute-start | bytes 2703368 | tf_op jit(solution)/shard_map/ppermute | solution.py:26
  60.8 12.5 %collective-permute-start.17 = (bf16[2640,128]{1,0:T(8,128)(2,1)S(1)}, bf16[2640,128]{1,0:T(8,128)(2,1)S(1)}, u32[]{:S(2)}, u32[]{:S(2)}) collective-permute-start(bf16[2640,128]{1,0:T(8,128)(2,1)S(1)} %pad_maximum_fusion.4), channel_id=1, source_target_pairs={{0,192},{64,0},{128,64},{192,128},{1,193},{65,1},{129,65},{193,129... | collective-permute-start | bytes 2027528 | tf_op jit(solution)/shard_map/ppermute | solution.py:26
  79.9 14.6 %collective-permute-start.20 = (bf16[2640,128]{1,0:T(8,128)(2,1)S(1)}, bf16[2640,128]{1,0:T(8,128)(2,1)S(1)}, u32[]{:S(2)}, u32[]{:S(2)}) collective-permute-start(bf16[2640,128]{1,0:T(8,128)(2,1)S(1)} %get-tuple-element.74), channel_id=1, source_target_pairs={{0,64},{64,128},{128,192},{192,0},{1,65},{65,129},{129,193},{193,1... | collective-permute-start | bytes 2027528 | tf_op jit(solution)/shard_map/ppermute | solution.py:26
  79.9 14.6 %collective-permute-start.21 = (bf16[2640,128]{1,0:T(8,128)(2,1)S(1)}, bf16[2640,128]{1,0:T(8,128)(2,1)S(1)}, u32[]{:S(2)}, u32[]{:S(2)}) collective-permute-start(bf16[2640,128]{1,0:T(8,128)(2,1)S(1)} %get-tuple-element.73), channel_id=1, source_target_pairs={{0,192},{64,0},{128,64},{192,128},{1,193},{65,1},{129,65},{193,129... | collective-permute-start | bytes 2027528 | tf_op jit(solution)/shard_map/ppermute | solution.py:26
  82.6 11.9 %collective-permute-start.18 = (bf16[2624,128]{1,0:T(8,128)(2,1)S(1)}, bf16[2624,128]{1,0:T(8,128)(2,1)S(1)}, u32[]{:S(2)}, u32[]{:S(2)}) collective-permute-start(bf16[2624,128]{1,0:T(8,128)(2,1)S(1)} %slice.106), channel_id=1, source_target_pairs={{0,8},{8,16},{16,24},{24,32},{32,40},{40,48},{48,56},{56,0},{1,9},... | collective-permute-start | bytes 2015240 | tf_op jit(solution)/shard_map/ppermute | solution.py:26
  82.8 11.7 %collective-permute-start.19 = (bf16[2624,128]{1,0:T(8,128)(2,1)S(1)}, bf16[2624,128]{1,0:T(8,128)(2,1)S(1)}, u32[]{:S(2)}, u32[]{:S(2)}) collective-permute-start(bf16[2624,128]{1,0:T(8,128)(2,1)S(1)} %slice.107), channel_id=1, source_target_pairs={{0,56},{8,0},{16,8},{24,16},{32,24},{40,32},{48,40},{56,48},{1,57}... | collective-permute-start | bytes 2015240 | tf_op jit(solution)/shard_map/ppermute | solution.py:26
  94.6 9.7 %collective-permute-start.23 = (bf16[1312,128]{1,0:T(8,128)(2,1)S(1)}, bf16[1312,128]{1,0:T(8,128)(2,1)S(1)}, u32[]{:S(2)}, u32[]{:S(2)}) collective-permute-start(bf16[1312,128]{1,0:T(8,128)(2,1)S(1)} %slice.114), channel_id=1, source_target_pairs={{0,8},{8,16},{16,24},{24,32},{32,40},{40,48},{48,56},{56,0},{1,9},... | collective-permute-start | bytes 1007624 | tf_op jit(solution)/shard_map/ppermute | solution.py:26
  94.7 9.6 %collective-permute-start.24 = (bf16[1312,128]{1,0:T(8,128)(2,1)S(1)}, bf16[1312,128]{1,0:T(8,128)(2,1)S(1)}, u32[]{:S(2)}, u32[]{:S(2)}) collective-permute-start(bf16[1312,128]{1,0:T(8,128)(2,1)S(1)} %slice.115), channel_id=1, source_target_pairs={{0,56},{8,0},{16,8},{24,16},{32,24},{40,32},{48,40},{56,48},{1,57}... | collective-permute-start | bytes 1007624 | tf_op jit(solution)/shard_map/ppermute | solution.py:26
  97.5 6.3 %collective-permute-start.22 = (bf16[880,128]{1,0:T(8,128)(2,1)S(1)}, bf16[880,128]{1,0:T(8,128)(2,1)S(1)}, u32[]{:S(2)}, u32[]{:S(2)}) collective-permute-start(bf16[880,128]{1,0:T(8,128)(2,1)S(1)} %slice.113), channel_id=1, source_target_pairs={{0,64},{64,128},{128,192},{192,0},{1,65},{65,129},{129,193},{193,1... | collective-permute-start | bytes 675848 | tf_op jit(solution)/shard_map/ppermute | solution.py:26
  117.4 9.5 %collective-permute-start.25 = (bf16[512,512]{1,0:T(8,128)(2,1)}, bf16[512,512]{1,0:T(8,128)(2,1)S(1)}, u32[]{:S(2)}, u32[]{:S(2)}) collective-permute-start(bf16[512,512]{1,0:T(8,128)(2,1)} %shard_map.64.a_ref), channel_id=1, source_target_pairs={{0,2},{2,4},{4,6},{6,0},{1,3},{3,5},{5,7},{7,1},{8,10},{10,12},{12... | collective-permute-start | bytes 1572872 | tf_op jit(solution)/shard_map/ppermute | solution.py:26
  117.5 9.4 %collective-permute-start.26 = (bf16[512,512]{1,0:T(8,128)(2,1)}, bf16[512,512]{1,0:T(8,128)(2,1)S(1)}, u32[]{:S(2)}, u32[]{:S(2)}) collective-permute-start(bf16[512,512]{1,0:T(8,128)(2,1)} %shard_map.64.a_ref), channel_id=1, source_target_pairs={{0,6},{2,0},{4,2},{6,4},{1,7},{3,1},{5,3},{7,5},{8,14},{10,8},{12,... | collective-permute-start | bytes 1572872 | tf_op jit(solution)/shard_map/ppermute | solution.py:26
  127.0 7.9 %collective-permute-start.27 = (bf16[256,512]{1,0:T(8,128)(2,1)S(1)}, bf16[256,512]{1,0:T(8,128)(2,1)S(1)}, u32[]{:S(2)}, u32[]{:S(2)}) collective-permute-start(bf16[256,512]{1,0:T(8,128)(2,1)S(1)} %slice.116), channel_id=1, source_target_pairs={{0,2},{2,4},{4,6},{6,0},{1,3},{3,5},{5,7},{7,1},{8,10},{10,12},{12... | collective-permute-start | bytes 786440 | tf_op jit(solution)/shard_map/ppermute | solution.py:26
  127.3 7.5 %collective-permute-start.28 = (bf16[256,512]{1,0:T(8,128)(2,1)S(1)}, bf16[256,512]{1,0:T(8,128)(2,1)S(1)}, u32[]{:S(2)}, u32[]{:S(2)}) collective-permute-start(bf16[256,512]{1,0:T(8,128)(2,1)S(1)} %slice.117), channel_id=1, source_target_pairs={{0,6},{2,0},{4,2},{6,4},{1,7},{3,1},{5,3},{7,5},{8,14},{10,8},{12,... | collective-permute-start | bytes 786440 | tf_op jit(solution)/shard_map/ppermute | solution.py:26
  135.3 14.5 %collective-permute-start.29 = (bf16[512,512]{1,0:T(8,128)(2,1)S(1)}, bf16[512,512]{1,0:T(8,128)(2,1)S(1)}, u32[]{:S(2)}, u32[]{:S(2)}) collective-permute-start(bf16[512,512]{1,0:T(8,128)(2,1)S(1)} %shard_map.68), channel_id=1, source_target_pairs={{0,1},{1,0},{2,3},{3,2},{4,5},{5,4},{6,7},{7,6},{8,9},{9,8},{10,11... | collective-permute-start | bytes 1572872 | tf_op jit(solution)/shard_map/ppermute | solution.py:26
  (27 other events, 219.4 us)
